TPU v7x, 512 devices: a whole 4x8x8 slice. The times are simulated.
512 devices in a mesh: frame: 64 (over y, z_hi, core), row: 8 (over x, z_lo).
Axes of the slice: x: 4, y: 8, z: 8 (z_hi: 4, z_lo: 2; z = z_hi * 2 + z_lo), core: 2. Of those that a mesh axis runs over, the one named last changes fastest.
Arguments:
- latents: bfloat16 [64, 1024, 640], P('frame', 'row'), may hold values from -6 to 6
- norm_gain: float32 [640], replicated, may hold values from 0.1 to 1.9
- w_query: bfloat16 [640, 640], replicated
- w_key: bfloat16 [640, 640], replicated, as said below
- w_value: bfloat16 [640, 640], replicated, may hold values from -0.25 to 0.25
- w_out: bfloat16 [640, 640], replicated, may hold values from -2 to 2
Outputs:
- mixed: bfloat16 [64, 1024, 640], P('frame', 'row')
Inputs may be any that keep to these rules, and one draw needn't show every extreme that they name: `w_key`: a weight matrix scaled for 640 inputs.
All inputs are finite; a program needn't handle non-finite values.
Results may differ from a plain program's by a relative error of at most 0.015.
Values may be sent and summed in bfloat16 or wider, within the bound.
No kernel may reach another device: no remote copies, remote signals or barrier semaphores. Data moves between devices by JAX's collectives and lax.ppermute only.
A program may use at most 128 MiB of HBM per device.

v0:
```python
import jax
import jax.numpy as jnp
from jax import lax
from jax.sharding import PartitionSpec as P

HEADS = 8


def passed_along(array, axis, by):
    count = lax.axis_size(axis)
    pairs = [(i, i + by) for i in range(count) if 0 <= i + by < count]
    return lax.ppermute(array, axis, pairs)


def from_root(array, axis, root):
    mine = lax.axis_index(axis) == root
    return lax.psum(jnp.where(mine, array, jnp.zeros_like(array)), axis)


def layer_norm(latents, norm_gain):
    values = latents.astype(jnp.float32)
    center = values - jnp.mean(values, axis=-1, keepdims=True)
    spread = jnp.mean(center * center, axis=-1, keepdims=True)
    return (center * lax.rsqrt(spread + 1e-05) * norm_gain).astype(jnp.bfloat16)


def project(normed, weight):
    flat = normed.reshape(-1, normed.shape[-1])
    return (
        jnp.dot(flat, weight, preferred_element_type=jnp.float32)
        .astype(jnp.bfloat16)
        .reshape(normed.shape[:-1] + (weight.shape[1],))
    )


def body(latents, norm_gain, w_query, w_key, w_value, w_out):
    frames_here, positions, channels = latents.shape
    head_dim = channels // HEADS
    normed = layer_norm(latents, norm_gain)
    query = project(normed, w_query)
    key = project(normed, w_key)
    value = project(normed, w_value)
    prior_key, prior_value = passed_along((key[-1], value[-1]), "frame", 1)
    first_key, first_value = (from_root(key[0], "frame", 0), from_root(value[0], "frame", 0))
    stack_key = jnp.concatenate([prior_key[None], key, first_key[None]], axis=0)
    stack_value = jnp.concatenate([prior_value[None], value, first_value[None]], axis=0)
    full_key, full_value = (
        lax.all_gather(stack_key, "row", axis=1, tiled=True),
        lax.all_gather(stack_value, "row", axis=1, tiled=True),
    )
    at_start = lax.axis_index("frame") == 0
    lead_key = jnp.where(at_start, full_key[1], full_key[0])
    lead_value = jnp.where(at_start, full_value[1], full_value[0])
    prev_key = jnp.concatenate([lead_key[None], full_key[1:frames_here]], axis=0)
    prev_value = jnp.concatenate([lead_value[None], full_value[1:frames_here]], axis=0)
    own_key = full_key[1 : frames_here + 1]
    own_value = full_value[1 : frames_here + 1]
    anchor_key = full_key[frames_here + 1]
    anchor_value = full_value[frames_here + 1]
    scale = 1.0 / jnp.sqrt(jnp.float32(head_dim))

    def one_frame(pieces):
        q_frame, k_own, k_prev, v_own, v_prev = pieces
        keys = jnp.concatenate([k_own, k_prev, anchor_key], axis=0)
        values = jnp.concatenate([v_own, v_prev, anchor_value], axis=0)
        total = keys.shape[0]
        qh = q_frame.reshape(positions, HEADS, head_dim)
        kh = keys.reshape(total, HEADS, head_dim)
        vh = values.reshape(total, HEADS, head_dim)
        scores = jnp.einsum("qhd,khd->hqk", qh, kh, preferred_element_type=jnp.float32) * scale
        weights = jax.nn.softmax(scores, axis=-1).astype(jnp.bfloat16)
        attended = jnp.einsum("hqk,khd->qhd", weights, vh, preferred_element_type=jnp.float32)
        return attended.reshape(positions, channels).astype(jnp.bfloat16)

    attended = lax.map(one_frame, (query, own_key, prev_key, own_value, prev_value))
    update = jnp.dot(attended.reshape(-1, channels), w_out, preferred_element_type=jnp.float32)
    update = update.reshape(frames_here, positions, channels)
    return (latents.astype(jnp.float32) + update).astype(jnp.bfloat16)


def solution(mesh):
    return jax.shard_map(
        body,
        mesh=mesh,
        in_specs=(P("frame", "row", None), P(), P(), P(), P(), P()),
        out_specs=P("frame", "row", None),
        check_vma=False,
    )
```

profile of v0, /device:TPU:1, one launch (start us, length us, event | category | flops | bytes accessed | tf_op | source)
XLA Modules:
  0.0 779.2 jit_solution(8800831980262388030)
XLA Ops:
  6.6 1.1 convert_reduce_fusion
  8.9 1.3 convolution_convert_fusion
  10.2 1.6 convolution_convert_fusion.2
  13.2 7.2 collective-permute-start
  20.4 2.2 collective-permute-done
  22.7 517.6 %all-reduce.3.cloned.1.call-done = (bf16[1,128,640]{2,1,0:T(8,128)(2,1)}, bf16[1,128,640]{2,1,0:T(8,128)(2,1)}) async-done(((bf16[1,128,640]{2,1,0:T(8,128)(2,1)}, bf16[1,128,640]{2,1,0:T(8,128)(2,1)}), (bf16[1,128,640]{2,1,0:T(8,128)(2,1)}, bf16[1,128,640]{2,1,0:T(8,128)(2,1)})) %all-reduce.3.cloned.1.call-update) | async-done | bytes 327696 | tf_op jit(solution)/shard_map/psum | solution.py:17
  540.3 1.8 pad_maximum_fusion
  542.2 5.6 collective-permute-start.1
  547.9 2.3 collective-permute-done.1
  550.1 1.8 pad_maximum_fusion.1
  552.5 80.1 %all-gather.3.cloned.1.call-done = bf16[3,1024,640]{2,1,0:T(8,128)(2,1)} async-done(((bf16[3,128,640]{2,1,0:T(8,128)(2,1)}), bf16[3,1024,640]{2,1,0:T(8,128)(2,1)}) %all-gather.3.cloned.1.call-update) | async-done | bytes 3932176 | tf_op jit(solution)/shard_map/all_gather | solution.py:49
  632.7 4.0 fusion.34
  636.6 1.5 copy.17
  638.2 88.0 %all-gather.5.cloned.1.call-done = bf16[3,1024,640]{2,1,0:T(8,128)(2,1)} async-done(((bf16[3,128,640]{2,1,0:T(8,128)(2,1)}), bf16[3,1024,640]{2,1,0:T(8,128)(2,1)}) %all-gather.5.cloned.1.call-update) | async-done | bytes 3932176 | tf_op jit(solution)/shard_map/all_gather | solution.py:48
  726.1 4.0 fusion.35
  730.1 2.5 copy.21
  732.6 1.5 copy.22
  734.1 1.6 copy.20
  735.7 2.5 copy.18
  738.2 2.5 copy.16
  740.7 3.1 broadcast_select_fusion
  743.8 5.5 fusion.11
  749.3 15.8 %fusion.36 = (f32[8,128]{1,0:T(8,128)S(1)}, f32[8,128,3072]{2,1,0:T(8,128)}) fusion(f32[8,128,3072]{2,1,0:T(8,128)} %fusion.11), kind=kOutput, calls=%fused_computation.46 | output fusion | flops 12585983 | bytes 25169920 | tf_op jit(solution)/shard_map/while/body/eval_jaxpr/sub | solution.py:71
  765.1 6.6 fusion.19
  (32 shorter events, 4.2 us)
Async XLA Ops:
  6.5 2.3 copy-start
  6.5 545.4 %copy-start.1 = (bf16[1,128,640]{2,1,0:T(8,128)(2,1)S(1)}, bf16[1,128,640]{2,1,0:T(8,128)(2,1)}, u32[]{:S(2)}) copy-start(bf16[1,128,640]{2,1,0:T(8,128)(2,1)} %param.6) | copy-start | bytes 491524
  6.5 545.4 %copy-start.8 = (f32[640]{0:T(1024)S(1)}, f32[640]{0:T(1024)}, u32[]{:S(2)}) copy-start(f32[640]{0:T(1024)} %param.7) | copy-start | bytes 7684
  6.5 545.4 %copy-start.7 = (bf16[640,640]{1,0:T(8,128)(2,1)S(1)}, bf16[640,640]{1,0:T(8,128)(2,1)}, u32[]{:S(2)}) copy-start(bf16[640,640]{1,0:T(8,128)(2,1)} %param.8) | copy-start | bytes 2457604
  6.5 533.8 %all-reduce.3.cloned.1.call-start = ((), (), s32[]{:S(2)}) async-start(), calls=%async_computation.2 | async-start | bytes 655360 | tf_op jit(solution)/shard_map/psum | solution.py:17
  13.2 619.5 %all-gather.3.cloned.1.call-start = ((), (), s32[]{:S(2)}) async-start(), calls=%async_computation | async-start | bytes 4423680 | tf_op jit(solution)/shard_map/all_gather | solution.py:49
  13.2 9.4 %collective-permute-start = (bf16[128,640]{1,0:T(8,128)(2,1)S(1)}, bf16[128,640]{1,0:T(8,128)(2,1)S(1)}, u32[]{:S(2)}, u32[]{:S(2)}) collective-permute-start(bf16[128,640]{1,0:T(8,128)(2,1)S(1)} %convolution_convert_fusion.2), channel_id=1, source_target_pairs={{0,8},{8,16},{16,24},{24,32},{32,40},{40,48},{48,56},{56,64},{64,7... | collective-permute-start | bytes 491528 | tf_op jit(solution)/shard_map/ppermute | solution.py:12
  542.2 184.0 %all-gather.5.cloned.1.call-start = ((), (), s32[]{:S(2)}) async-start(), calls=%async_computation.1 | async-start | bytes 4423680 | tf_op jit(solution)/shard_map/all_gather | solution.py:48
  542.2 7.9 %collective-permute-start.1 = (bf16[128,640]{1,0:T(8,128)(2,1)S(1)}, bf16[128,640]{1,0:T(8,128)(2,1)S(1)}, u32[]{:S(2)}, u32[]{:S(2)}) collective-permute-start(bf16[128,640]{1,0:T(8,128)(2,1)S(1)} %convolution_convert_fusion), channel_id=1, source_target_pairs={{0,8},{8,16},{16,24},{24,32},{32,40},{40,48},{48,56},{56,64},{64,7... | collective-permute-start | bytes 491528 | tf_op jit(solution)/shard_map/ppermute | solution.py:12
  740.7 3.1 copy-start.3
  749.3 15.8 %copy-start.2 = (bf16[1,1024,640]{1,2,0:T(8,128)(2,1)S(1)}, bf16[1,1024,640]{1,2,0:T(8,128)(2,1)}, u32[]{:S(2)}) copy-start(bf16[1,1024,640]{1,2,0:T(8,128)(2,1)} %copy.16) | copy-start | bytes 3932164
  749.3 15.8 %copy-start.4 = (bf16[1,1024,640]{1,2,0:T(8,128)(2,1)S(1)}, bf16[1,1024,640]{1,2,0:T(8,128)(2,1)}, u32[]{:S(2)}) copy-start(bf16[1,1024,640]{1,2,0:T(8,128)(2,1)} %copy.18) | copy-start | bytes 3932164
  749.3 15.8 %copy-start.5 = (bf16[1024,8,80]{0,2,1:T(8,128)(2,1)S(1)}, bf16[1024,8,80]{0,2,1:T(8,128)(2,1)}, u32[]{:S(2)}) copy-start(bf16[1024,8,80]{0,2,1:T(8,128)(2,1)} %get-tuple-element.43) | copy-start | bytes 3932164
  765.1 6.6 copy-start.6
Sparse Core Ops, SparseCore 0:
  13.3 526.9 all-reduce.2
  542.6 90.0 all-gather.2
  635.0 91.1 all-gather.4
where the time goes:
time: 780 us; the launch traced here: 779 us
  waiting for transfers between devices  690 us (88%)
  other arithmetic  26.1 us (3%)
  local copies, waits for them, and re-layouts  20.3 us (3%)
  matrix products  16.3 us (2%)
  between operations  13.3 us (2%)
  starting transfers between devices  12.9 us (2%)
    psum x1, waiting for transfers between devices, from_root(): return lax.psum(jnp.where(mine, array, jnp.zeros_like(array)), axis)  518 us
    all_gather x1, waiting for transfers between devices, body(): lax.all_gather(stack_key, 'row', axis=1, tiled=True)  88 us
    all_gather x1, waiting for transfers between devices, body(): lax.all_gather(stack_value, 'row', axis=1, tiled=True)  80.1 us
    sub x1, other arithmetic, one_frame(): weights = jax.nn.softmax(scores, axis=-1).astype(jnp.bfloat16)  15.8 us
  transfers between devices with their start and end apart: 5, of which 5 were waited for; matrix products, arithmetic and copies ran while one was open for 1% of the time, Pallas kernels for 0%

commit v1 on v0

v1 whole, which is shorter than its diff:
```python
import math

import jax
import jax.numpy as jnp
from jax import lax
from jax.experimental import pallas as pl
from jax.experimental.pallas import tpu as pltpu
from jax.sharding import PartitionSpec as P

HEADS = 8
SPREAD = 16
VMEM = 32 * 2**20

ROUNDS = (
    ((4, 0, 0), (2, 0, 0), (6, 0, 0)),
    ((0, 2, 0), (0, 1, 0), (0, 3, 0)),
    ((1, 0, 0), (1, 0, 1), (0, 0, 1)),
)
SIZES = (8, 4, 2)


def index_of(place):
    return (place[0] * SIZES[1] + place[1]) * SIZES[2] + place[2]


def spread_plan():
    held = [(0, 0, 0)]
    plan = []
    for steps in ROUNDS:
        perms = []
        fresh = []
        for step in steps:
            pairs = []
            for place in held:
                to = tuple((a + b) % n for a, b, n in zip(place, step, SIZES))
                pairs.append((index_of(place), index_of(to)))
                fresh.append(to)
            perms.append(pairs)
        held = held + fresh
        plan.append(perms)
    return plan


def normed_of(values, gain):
    values = values.astype(jnp.float32)
    center = values - jnp.mean(values, axis=-1, keepdims=True)
    spread = jnp.mean(center * center, axis=-1, keepdims=True)
    return (center * lax.rsqrt(spread + 1e-05) * gain).astype(jnp.bfloat16)


def project(normed, weight):
    return jnp.dot(normed, weight, preferred_element_type=jnp.float32)


def by_head(rows):
    channels, positions = rows.shape[1], rows.shape[0]
    return rows.astype(jnp.bfloat16).T.reshape(HEADS, channels // HEADS, positions)


def own_kernel(flag, own, prior, gain, w_query, w_key, w_value, out):
    positions, channels = own.shape
    head = channels // HEADS
    scale = math.log2(math.e) / math.sqrt(head)
    before = jnp.where(flag[0] == 0, own[...].astype(jnp.float32), prior[...].astype(jnp.float32))
    normed = normed_of(own[...], gain[...])
    both = jnp.concatenate([normed, normed_of(before, gain[...])], axis=0)
    out[:, :head, :] = by_head(project(normed, w_query[...]) * scale)
    key = project(both, w_key[...])
    value = project(both, w_value[...])
    out[:, head : 2 * head, :] = by_head(key[:positions])
    out[:, 2 * head : 3 * head, :] = by_head(value[:positions])
    out[:, 3 * head : 4 * head, :] = by_head(key[positions:])
    out[:, 4 * head :, :] = by_head(value[positions:])


def pick_kernel(flag, held, one, two, three, out):
    for which, ref in enumerate((held, one, two, three)):

        @pl.when(flag[0] == which)
        def _():
            out[...] = ref[...]


def first_kernel(flag, held, one, two, three, gain, w_key, w_value, out, latents):
    pick_kernel(flag, held, one, two, three, latents)
    head = latents.shape[1] // HEADS
    normed = normed_of(latents[...], gain[...])
    out[:, :head, :] = by_head(project(normed, w_key[...]))
    out[:, head:, :] = by_head(project(normed, w_value[...]))


def joined(ref, start, size, blocks):
    return jnp.concatenate([ref[b, start : start + size, :] for b in blocks], axis=1)


def ones_row(count):
    return (lax.broadcasted_iota(jnp.int32, (SPREAD, count), 0) == 0).astype(jnp.float32).astype(jnp.bfloat16)


def scores_of(key, query):
    return lax.dot_general(key, query, (((0,), (0,)), ((), ())), preferred_element_type=jnp.float32)


GROUP = 4


def near_kernel(rows, peak, total):
    blocks, _, width = rows.shape
    head = rows.shape[1] // 5
    every = range(blocks)
    keys = [joined(rows, start * head, head, every) for start in (1, 3)]
    values = [
        jnp.concatenate([joined(rows, start * head, head, every), ones_row(blocks * width)], axis=0)
        for start in (2, 4)
    ]
    for g in range(0, blocks, GROUP):
        query = joined(rows, 0, head, range(g, g + GROUP))
        scores = [scores_of(key, query) for key in keys]
        top = jnp.maximum(*[jnp.max(s, axis=0, keepdims=True) for s in scores])
        span = slice(g * width, (g + GROUP) * width)
        peak[:, span] = jnp.broadcast_to(top, (8, GROUP * width))
        total[:, span] = sum(
            jnp.dot(value, jnp.exp2(s - top).astype(jnp.bfloat16), preferred_element_type=jnp.float32)
            for value, s in zip(values, scores)
        )


def far_kernel(rows, first, peak, total, out):
    blocks, _, width = rows.shape
    head = rows.shape[1] // 5
    every = range(blocks)
    key = joined(first, 0, head, every)
    value = jnp.concatenate([joined(first, head, head, every), ones_row(blocks * width)], axis=0)
    for g in range(0, blocks, GROUP):
        query = joined(rows, 0, head, range(g, g + GROUP))
        scores = scores_of(key, query)
        span = slice(g * width, (g + GROUP) * width)
        before = peak[:1, span]
        top = jnp.maximum(jnp.max(scores, axis=0, keepdims=True), before)
        weights = jnp.exp2(scores - top).astype(jnp.bfloat16)
        both = total[:, span] * jnp.exp2(before - top) + jnp.dot(
            value, weights, preferred_element_type=jnp.float32
        )
        attended = (both[:head] / both[head : head + 1]).astype(jnp.bfloat16)
        for b in range(GROUP):
            out[g + b] = attended[:, b * width : (b + 1) * width]


def mix_kernel(attended, latents, w_out, out):
    heads, head, positions = attended.shape
    rows = attended[...].reshape(heads * head, positions).T
    update = jnp.dot(rows, w_out[...], preferred_element_type=jnp.float32)
    out[...] = (latents[...].astype(jnp.float32) + update).astype(jnp.bfloat16)


def call(kernel, name, shapes, *operands, scalars=0, scratch=(), flops=0, moved=0):
    specs = [pl.BlockSpec(memory_space=pltpu.SMEM)] * scalars
    specs += [pl.BlockSpec(memory_space=pltpu.VMEM)] * (len(operands) - scalars)
    many = isinstance(shapes, (list, tuple))
    return pl.pallas_call(
        kernel,
        out_shape=shapes,
        in_specs=specs,
        out_specs=jax.tree.map(lambda _: pl.BlockSpec(memory_space=pltpu.VMEM), shapes)
        if many
        else pl.BlockSpec(memory_space=pltpu.VMEM),
        scratch_shapes=list(scratch),
        compiler_params=pltpu.CompilerParams(vmem_limit_bytes=VMEM),
        cost_estimate=pl.CostEstimate(flops=flops, bytes_accessed=moved, transcendentals=0),
        name=name,
    )(*operands)


def body(latents, norm_gain, w_query, w_key, w_value, w_out):
    _, positions, channels = latents.shape
    head = channels // HEADS
    own = latents[0]
    gain = norm_gain[None]
    frames = lax.axis_size("frame")
    frame = lax.axis_index("frame")
    row_count = lax.axis_size("row")
    total_positions = row_count * positions
    shape = lambda *dims, kind=jnp.bfloat16: jax.ShapeDtypeStruct(dims, kind)

    plan = spread_plan()
    flags = []
    for perms in plan:
        which = [0] * frames
        for k, pairs in enumerate(perms):
            for _, to in pairs:
                which[to] = k + 1
        flags.append(jnp.asarray(which, jnp.int32)[frame][None])

    held = own
    arrived = [lax.ppermute(held, "frame", pairs) for pairs in plan[0]]
    prior = lax.ppermute(own, "frame", [(i, i + 1) for i in range(frames - 1)])
    held = call(pick_kernel, "pick_a", shape(positions, channels), flags[0], held, *arrived, scalars=1)
    arrived = [lax.ppermute(held, "frame", pairs) for pairs in plan[1]]
    held = call(pick_kernel, "pick_b", shape(positions, channels), flags[1], held, *arrived, scalars=1)
    arrived = [lax.ppermute(held, "frame", pairs) for pairs in plan[2]]

    mine = call(
        own_kernel, "own_rows", shape(HEADS, 5 * head, positions),
        frame[None], own, prior, gain, w_query, w_key, w_value, scalars=1,
        flops=2 * positions * channels * channels * 5, moved=3 * 2 * channels * channels,
    )
    rows = lax.all_to_all(mine, "row", 0, 0, tiled=True)
    peak, total = call(
        near_kernel, "near", (shape(8, total_positions, kind=jnp.float32), shape(head + SPREAD, total_positions, kind=jnp.float32)),
        rows, flops=4 * head * total_positions * 2 * total_positions, moved=2 * 8 * 5 * head * positions,
    )
    theirs = call(
        first_kernel, "first_rows", shape(HEADS, 2 * head, positions),
        flags[2], held, *arrived, gain, w_key, w_value, scalars=1,
        scratch=[pltpu.VMEM((positions, channels), jnp.bfloat16)],
        flops=2 * positions * channels * channels * 2, moved=2 * 2 * channels * channels,
    )
    first = lax.all_to_all(theirs, "row", 0, 0, tiled=True)
    attended = call(
        far_kernel, "far", shape(HEADS, head, positions),
        rows, first, peak, total, flops=4 * head * total_positions * total_positions, moved=2 * 8 * 2 * head * positions,
    )
    back = lax.all_to_all(attended, "row", 0, 0, tiled=True)
    mixed = call(
        mix_kernel, "mix", shape(positions, channels),
        back, own, w_out, flops=2 * positions * channels * channels, moved=2 * channels * channels,
    )
    return mixed[None]


def solution(mesh):
    return jax.shard_map(
        body,
        mesh=mesh,
        in_specs=(P("frame", "row", None), P(), P(), P(), P(), P()),
        out_specs=P("frame", "row", None),
        check_vma=False,
    )
```

time: 780 us -> 85.5 us (0.11)
  the two profiles are of different devices: /device:TPU:1 before, /device:TPU:56 now
where the time goes in v1:
time: 85.5 us; the launch traced here: 84.8 us
  waiting for transfers between devices  37.8 us (44%)
  starting transfers between devices  18.5 us (22%)
  Pallas kernels  11.9 us (14%)
  blocking collectives  9.65 us (11%)
  local copies, waits for them, and re-layouts  6.79 us (8%)
    ppermute x3, waiting for transfers between devices, body(): arrived = [lax.ppermute(held, 'frame', pairs) for pairs in plan[2]]  18.1 us
    ppermute x1, waiting for transfers between devices, body(): prior = lax.ppermute(own, 'frame', [(i, i + 1) for i in range(frames - 1)])  14 us
    pallas_call x7, Pallas kernels, call(): pl.pallas_call(kernel, out_shape=shapes, in_specs=specs, out_specs=jax.tr...  11.9 us
    all_to_all x1, blocking collectives, body(): back = lax.all_to_all(attended, 'row', 0, 0, tiled=True)  9.65 us
    all_to_all x1, waiting for transfers between devices, body(): first = lax.all_to_all(theirs, 'row', 0, 0, tiled=True)  5.77 us
    all_to_all x1, starting transfers between devices, body(): rows = lax.all_to_all(mine, 'row', 0, 0, tiled=True)  5.52 us
    unnamed x24, local copies, waits for them, and re-layouts  5.03 us
    all_to_all x1, starting transfers between devices, body(): first = lax.all_to_all(theirs, 'row', 0, 0, tiled=True)  4.25 us
  transfers between devices with their start and end apart: 12, of which 3 were waited for; matrix products, arithmetic and copies ran while one was open for 2% of the time, Pallas kernels for 8%

profile of v1, /device:TPU:56, one launch (start us, length us, event | category | flops | bytes accessed | tf_op | source)
XLA Modules:
  0.0 84.8 jit_solution(14911291020214227185)
XLA Ops:
  0.0 2.0 %collective-permute-start = (bf16[128,640]{1,0:T(8,128)(2,1)}, bf16[128,640]{1,0:T(8,128)(2,1)S(1)}, u32[]{:S(2)}, u32[]{:S(2)}) collective-permute-start(bf16[128,640]{1,0:T(8,128)(2,1)} %bitcast.3), channel_id=1, source_target_pairs={{0,8},{8,16},{16,24},{24,32},{32,40},{40,48},{48,56},{56,64},{64,7... | collective-permute-start | bytes 491528 | tf_op jit(solution)/shard_map/ppermute | solution.py:196
  2.1 14.0 %collective-permute-done.prior = bf16[128,640]{1,0:T(8,128)(2,1)S(1)} collective-permute-done((bf16[128,640]{1,0:T(8,128)(2,1)}, bf16[128,640]{1,0:T(8,128)(2,1)S(1)}, u32[]{:S(2)}, u32[]{:S(2)}) %collective-permute-start) | collective-permute-done | bytes 163872 | tf_op jit(solution)/shard_map/ppermute | solution.py:196
  16.1 1.1 %copy-done = bf16[640,640]{1,0:T(8,128)(2,1)S(1)} copy-done((bf16[640,640]{1,0:T(8,128)(2,1)S(1)}, bf16[640,640]{1,0:T(8,128)(2,1)}, u32[]{:S(2)}) %copy-start) | copy-done | bytes 819224
  17.2 1.1 %copy-done.2 = bf16[640,640]{1,0:T(8,128)(2,1)S(1)} copy-done((bf16[640,640]{1,0:T(8,128)(2,1)S(1)}, bf16[640,640]{1,0:T(8,128)(2,1)}, u32[]{:S(2)}) %copy-start.2) | copy-done | bytes 819224
  18.4 0.9 %copy-done.4 = bf16[1,128,640]{2,1,0:T(8,128)(2,1)S(1)} copy-done((bf16[1,128,640]{2,1,0:T(8,128)(2,1)S(1)}, bf16[1,128,640]{2,1,0:T(8,128)(2,1)}, u32[]{:S(2)}) %copy-start.4) | copy-done | bytes 163864
  19.3 1.1 %copy-done.7 = bf16[640,640]{1,0:T(8,128)(2,1)S(1)} copy-done((bf16[640,640]{1,0:T(8,128)(2,1)S(1)}, bf16[640,640]{1,0:T(8,128)(2,1)}, u32[]{:S(2)}) %copy-start.7) | copy-done | bytes 819224
  20.4 2.1 %own_rows.1 = bf16[8,400,128]{2,1,0:T(8,128)(2,1)} custom-call(s32[1]{0:T(128)} %bitcast.flag, bf16[128,640]{1,0:T(8,128)(2,1)S(1)} %bitcast.4, bf16[128,640]{1,0:T(8,128)(2,1)S(1)} %collective-permute-done.prior, f32[1,640]{1,0:T(1,128)S(1)} %broadcast_in_dim.10.gain, bf16[640,640]{1,0:T(8,128)(2,1)S(1)} %copy-done.7, bf16[640,640]{1,0:T(8,128)(2,1)S(1)} %copy-done, ...), custom_call_target="tpu_custom_call" | custom-call | flops 524288000 | bytes 2457600 | tf_op jit(solution)/shard_map/own_rows/pallas_call | solution.py:160
  22.5 5.5 %all-to-all-start = ((bf16[8,400,128]{2,1,0:T(8,128)(2,1)}), bf16[8,400,128]{2,1,0:T(8,128)(2,1)S(1)}, u32[]{:S(2)}, u32[]{:S(2)}) async-start(bf16[8,400,128]{2,1,0:T(8,128)(2,1)} %own_rows.1), calls=%async_computation | async-start | bytes 1638400 | tf_op jit(solution)/shard_map/all_to_all | solution.py:207
  28.0 0.7 collective-permute-start.1
  29.4 0.7 collective-permute-start.3
  31.3 0.8 pick_a.1.held
  32.1 0.7 collective-permute-start.4
  33.5 0.7 collective-permute-start.6
  34.8 0.7 pick_b.1.held
  35.5 1.3 %collective-permute-start.7 = (bf16[128,640]{1,0:T(8,128)(2,1)S(1)}, bf16[128,640]{1,0:T(8,128)(2,1)S(1)}, u32[]{:S(2)}, u32[]{:S(2)}) collective-permute-start(bf16[128,640]{1,0:T(8,128)(2,1)S(1)} %pick_b.1.held), channel_id=1, source_target_pairs={{0,64},{256,320},{128,192},{384,448},{32,96},{288,352},{160,224},{... | collective-permute-start | bytes 491528 | tf_op jit(solution)/shard_map/ppermute | solution.py:200
  36.8 0.7 collective-permute-start.8
  38.7 18.0 %collective-permute-done.7.one = bf16[128,640]{1,0:T(8,128)(2,1)S(1)} collective-permute-done((bf16[128,640]{1,0:T(8,128)(2,1)S(1)}, bf16[128,640]{1,0:T(8,128)(2,1)S(1)}, u32[]{:S(2)}, u32[]{:S(2)}) %collective-permute-start.7) | collective-permute-done | bytes 163872 | tf_op jit(solution)/shard_map/ppermute | solution.py:200
  56.8 2.1 %first_rows.1 = bf16[8,160,128]{2,1,0:T(8,128)(2,1)} custom-call(s32[1]{0:T(128)} %dynamic_slice.9.flag, bf16[128,640]{1,0:T(8,128)(2,1)S(1)} %pick_b.1.held, bf16[128,640]{1,0:T(8,128)(2,1)S(1)} %collective-permute-done.7.one, bf16[128,640]{1,0:T(8,128)(2,1)S(1)} %collective-permute-done.8.two, bf16[128,640]{1,0:T(8,128)(2,1)S(1)} %collective-permute-done.9.three, ...), custom_call_target="tpu_custom_call" | custom-call | flops 209715200 | bytes 1638400 | tf_op jit(solution)/shard_map/first_rows/pallas_call | solution.py:160
  58.9 4.2 %all-to-all-start.1 = ((bf16[8,160,128]{2,1,0:T(8,128)(2,1)}), bf16[8,160,128]{2,1,0:T(8,128)(2,1)S(1)}, u32[]{:S(2)}, u32[]{:S(2)}) async-start(bf16[8,160,128]{2,1,0:T(8,128)(2,1)} %first_rows.1), calls=%async_computation.1 | async-start | bytes 655360 | tf_op jit(solution)/shard_map/all_to_all | solution.py:218
  63.2 3.3 %near.1 = (f32[8,1024]{1,0:T(8,128)S(1)}, f32[96,1024]{1,0:T(8,128)S(1)}) custom-call(bf16[8,400,128]{2,1,0:T(8,128)(2,1)S(1)} %all-to-all-done.rows), custom_call_target="tpu_custom_call" | custom-call | flops 671088640 | bytes 819200 | tf_op jit(solution)/shard_map/near/pallas_call | solution.py:160
  66.5 5.8 %all-to-all-done.1.first = bf16[8,160,128]{2,1,0:T(8,128)(2,1)S(1)} async-done(((bf16[8,160,128]{2,1,0:T(8,128)(2,1)}), bf16[8,160,128]{2,1,0:T(8,128)(2,1)S(1)}, u32[]{:S(2)}, u32[]{:S(2)}) %all-to-all-start.1) | async-done | bytes 327712 | tf_op jit(solution)/shard_map/all_to_all | solution.py:218
  72.2 1.9 %far.1 = bf16[8,80,128]{2,1,0:T(8,128)(2,1)S(1)} custom-call(bf16[8,400,128]{2,1,0:T(8,128)(2,1)S(1)} %all-to-all-done.rows, bf16[8,160,128]{2,1,0:T(8,128)(2,1)S(1)} %all-to-all-done.1.first, f32[8,1024]{1,0:T(8,128)S(1)} %get-tuple-element.7.peak, f32[96,1024]{1,0:T(8,128)S(1)} %get-tuple-element.8.total), custom_call_target="tpu_custom_call" | custom-call | flops 335544320 | bytes 327680 | tf_op jit(solution)/shard_map/far/pallas_call | solution.py:160
  74.2 9.7 %all_to_all.15.attended = bf16[8,80,128]{2,1,0:T(8,128)(2,1)S(1)} all-to-all(bf16[8,80,128]{2,1,0:T(8,128)(2,1)S(1)} %far.1), channel_id=1, replica_groups=mesh['frame'=64,'row'=8] {'row'}, dimensions={0} | all-to-all | bytes 327680 | tf_op jit(solution)/shard_map/all_to_all | solution.py:223
  83.8 1.0 %mix.1 = bf16[128,640]{1,0:T(8,128)(2,1)} custom-call(bf16[8,80,128]{2,1,0:T(8,128)(2,1)S(1)} %all_to_all.15.attended, bf16[128,640]{1,0:T(8,128)(2,1)S(1)} %bitcast.9, bf16[640,640]{1,0:T(8,128)(2,1)S(1)} %copy-done.6), custom_call_target="tpu_custom_call" | custom-call | flops 104857600 | bytes 819200 | tf_op jit(solution)/shard_map/mix/pallas_call | solution.py:160
  (36 shorter events, 4.5 us)
Async XLA Ops:
  0.0 2.1 %copy-start.8 = (f32[640]{0:T(1024)S(1)}, f32[640]{0:T(1024)}, u32[]{:S(2)}) copy-start(f32[640]{0:T(1024)} %param.10) | copy-start | bytes 7684
  0.0 16.1 %collective-permute-start = (bf16[128,640]{1,0:T(8,128)(2,1)}, bf16[128,640]{1,0:T(8,128)(2,1)S(1)}, u32[]{:S(2)}, u32[]{:S(2)}) collective-permute-start(bf16[128,640]{1,0:T(8,128)(2,1)} %bitcast.3), channel_id=1, source_target_pairs={{0,8},{8,16},{16,24},{24,32},{32,40},{40,48},{48,56},{56,64},{64,7... | collective-permute-start | bytes 491528 | tf_op jit(solution)/shard_map/ppermute | solution.py:196
  16.1 1.1 %copy-start = (bf16[640,640]{1,0:T(8,128)(2,1)S(1)}, bf16[640,640]{1,0:T(8,128)(2,1)}, u32[]{:S(2)}) copy-start(bf16[640,640]{1,0:T(8,128)(2,1)} %w_key.3) | copy-start | bytes 2457604
  17.2 1.1 %copy-start.2 = (bf16[640,640]{1,0:T(8,128)(2,1)S(1)}, bf16[640,640]{1,0:T(8,128)(2,1)}, u32[]{:S(2)}) copy-start(bf16[640,640]{1,0:T(8,128)(2,1)} %w_value.3) | copy-start | bytes 2457604
  18.3 0.9 %copy-start.4 = (bf16[1,128,640]{2,1,0:T(8,128)(2,1)S(1)}, bf16[1,128,640]{2,1,0:T(8,128)(2,1)}, u32[]{:S(2)}) copy-start(bf16[1,128,640]{2,1,0:T(8,128)(2,1)} %param.9) | copy-start | bytes 491524
  19.3 1.1 %copy-start.7 = (bf16[640,640]{1,0:T(8,128)(2,1)S(1)}, bf16[640,640]{1,0:T(8,128)(2,1)}, u32[]{:S(2)}) copy-start(bf16[640,640]{1,0:T(8,128)(2,1)} %w_query.1) | copy-start | bytes 2457604
  22.5 5.5 %copy-start.5 = (bf16[1,128,640]{2,1,0:T(8,128)(2,1)S(1)}, bf16[1,128,640]{2,1,0:T(8,128)(2,1)}, u32[]{:S(2)}) copy-start(bf16[1,128,640]{2,1,0:T(8,128)(2,1)} %param.9) | copy-start | bytes 491524
  22.5 36.5 %all-to-all-start = ((bf16[8,400,128]{2,1,0:T(8,128)(2,1)}), bf16[8,400,128]{2,1,0:T(8,128)(2,1)S(1)}, u32[]{:S(2)}, u32[]{:S(2)}) async-start(bf16[8,400,128]{2,1,0:T(8,128)(2,1)} %own_rows.1), calls=%async_computation | async-start | bytes 1638400 | tf_op jit(solution)/shard_map/all_to_all | solution.py:207
  28.0 3.3 %collective-permute-start.1 = (bf16[128,640]{1,0:T(8,128)(2,1)S(1)}, bf16[128,640]{1,0:T(8,128)(2,1)S(1)}, u32[]{:S(2)}, u32[]{:S(2)}) collective-permute-start(bf16[128,640]{1,0:T(8,128)(2,1)S(1)} %bitcast.5), channel_id=1, source_target_pairs={{0,256},{1,257},{2,258},{3,259},{4,260},{5,261},{6,262},{7,263}} | collective-permute-start | bytes 491528 | tf_op jit(solution)/shard_map/ppermute | solution.py:195
  28.7 2.6 %collective-permute-start.2 = (bf16[128,640]{1,0:T(8,128)(2,1)S(1)}, bf16[128,640]{1,0:T(8,128)(2,1)S(1)}, u32[]{:S(2)}, u32[]{:S(2)}) collective-permute-start(bf16[128,640]{1,0:T(8,128)(2,1)S(1)} %bitcast.6), channel_id=1, source_target_pairs={{0,128},{1,129},{2,130},{3,131},{4,132},{5,133},{6,134},{7,135}} | collective-permute-start | bytes 491528 | tf_op jit(solution)/shard_map/ppermute | solution.py:195
  29.4 1.9 %collective-permute-start.3 = (bf16[128,640]{1,0:T(8,128)(2,1)S(1)}, bf16[128,640]{1,0:T(8,128)(2,1)S(1)}, u32[]{:S(2)}, u32[]{:S(2)}) collective-permute-start(bf16[128,640]{1,0:T(8,128)(2,1)S(1)} %bitcast.7), channel_id=1, source_target_pairs={{0,384},{1,385},{2,386},{3,387},{4,388},{5,389},{6,390},{7,391}} | collective-permute-start | bytes 491528 | tf_op jit(solution)/shard_map/ppermute | solution.py:195
  30.0 0.7 copy-start.11
  30.7 3.5 %copy-start.10 = (s32[64]{0:T(128)S(1)}, s32[64]{0:T(128)}, u32[]{:S(2)}) copy-start(s32[64]{0:T(128)} %constant.17.clone) | copy-start | bytes 772
  31.3 25.5 %copy-start.1 = (bf16[640,640]{1,0:T(8,128)(2,1)S(1)}, bf16[640,640]{1,0:T(8,128)(2,1)}, u32[]{:S(2)}) copy-start(bf16[640,640]{1,0:T(8,128)(2,1)} %w_key.3) | copy-start | bytes 2457604
  31.3 25.5 %copy-start.3 = (bf16[640,640]{1,0:T(8,128)(2,1)S(1)}, bf16[640,640]{1,0:T(8,128)(2,1)}, u32[]{:S(2)}) copy-start(bf16[640,640]{1,0:T(8,128)(2,1)} %w_value.3) | copy-start | bytes 2457604
  32.1 2.6 %collective-permute-start.4 = (bf16[128,640]{1,0:T(8,128)(2,1)S(1)}, bf16[128,640]{1,0:T(8,128)(2,1)S(1)}, u32[]{:S(2)}, u32[]{:S(2)}) collective-permute-start(bf16[128,640]{1,0:T(8,128)(2,1)S(1)} %pick_a.1.held), channel_id=1, source_target_pairs={{0,32},{256,288},{128,160},{384,416},{1,33},{257,289},{129,161},{3... | collective-permute-start | bytes 491528 | tf_op jit(solution)/shard_map/ppermute | solution.py:198
  32.8 2.0 %collective-permute-start.5 = (bf16[128,640]{1,0:T(8,128)(2,1)S(1)}, bf16[128,640]{1,0:T(8,128)(2,1)S(1)}, u32[]{:S(2)}, u32[]{:S(2)}) collective-permute-start(bf16[128,640]{1,0:T(8,128)(2,1)S(1)} %pick_a.1.held), channel_id=1, source_target_pairs={{0,16},{256,272},{128,144},{384,400},{1,17},{257,273},{129,145},{3... | collective-permute-start | bytes 491528 | tf_op jit(solution)/shard_map/ppermute | solution.py:198
  33.5 1.3 %collective-permute-start.6 = (bf16[128,640]{1,0:T(8,128)(2,1)S(1)}, bf16[128,640]{1,0:T(8,128)(2,1)S(1)}, u32[]{:S(2)}, u32[]{:S(2)}) collective-permute-start(bf16[128,640]{1,0:T(8,128)(2,1)S(1)} %pick_a.1.held), channel_id=1, source_target_pairs={{0,48},{256,304},{128,176},{384,432},{1,49},{257,305},{129,177},{3... | collective-permute-start | bytes 491528 | tf_op jit(solution)/shard_map/ppermute | solution.py:198
  34.8 3.4 %copy-start.9 = (s32[64]{0:T(128)S(1)}, s32[64]{0:T(128)}, u32[]{:S(2)}) copy-start(s32[64]{0:T(128)} %constant.18.clone) | copy-start | bytes 772
  35.5 21.3 %collective-permute-start.7 = (bf16[128,640]{1,0:T(8,128)(2,1)S(1)}, bf16[128,640]{1,0:T(8,128)(2,1)S(1)}, u32[]{:S(2)}, u32[]{:S(2)}) collective-permute-start(bf16[128,640]{1,0:T(8,128)(2,1)S(1)} %pick_b.1.held), channel_id=1, source_target_pairs={{0,64},{256,320},{128,192},{384,448},{32,96},{288,352},{160,224},{... | collective-permute-start | bytes 491528 | tf_op jit(solution)/shard_map/ppermute | solution.py:200
  36.8 20.0 %collective-permute-start.8 = (bf16[128,640]{1,0:T(8,128)(2,1)S(1)}, bf16[128,640]{1,0:T(8,128)(2,1)S(1)}, u32[]{:S(2)}, u32[]{:S(2)}) collective-permute-start(bf16[128,640]{1,0:T(8,128)(2,1)S(1)} %pick_b.1.held), channel_id=1, source_target_pairs={{0,72},{256,328},{128,200},{384,456},{32,104},{288,360},{160,232},... | collective-permute-start | bytes 491528 | tf_op jit(solution)/shard_map/ppermute | solution.py:200
  37.4 19.3 %collective-permute-start.9 = (bf16[128,640]{1,0:T(8,128)(2,1)S(1)}, bf16[128,640]{1,0:T(8,128)(2,1)S(1)}, u32[]{:S(2)}, u32[]{:S(2)}) collective-permute-start(bf16[128,640]{1,0:T(8,128)(2,1)S(1)} %pick_b.1.held), channel_id=1, source_target_pairs={{0,8},{256,264},{128,136},{384,392},{32,40},{288,296},{160,168},{4... | collective-permute-start | bytes 491528 | tf_op jit(solution)/shard_map/ppermute | solution.py:200
  58.9 13.3 %all-to-all-start.1 = ((bf16[8,160,128]{2,1,0:T(8,128)(2,1)}), bf16[8,160,128]{2,1,0:T(8,128)(2,1)S(1)}, u32[]{:S(2)}, u32[]{:S(2)}) async-start(bf16[8,160,128]{2,1,0:T(8,128)(2,1)} %first_rows.1), calls=%async_computation.1 | async-start | bytes 655360 | tf_op jit(solution)/shard_map/all_to_all | solution.py:218
  72.2 11.6 %copy-start.6 = (bf16[640,640]{1,0:T(8,128)(2,1)S(1)}, bf16[640,640]{1,0:T(8,128)(2,1)}, u32[]{:S(2)}) copy-start(bf16[640,640]{1,0:T(8,128)(2,1)} %w_out.1) | copy-start | bytes 2457604

commit v2 on v1

v2 whole, which is shorter than its diff:
```python
import functools
import math

import jax
import jax.numpy as jnp
from jax import lax
from jax.experimental import pallas as pl
from jax.experimental.pallas import tpu as pltpu
from jax.sharding import PartitionSpec as P

HEADS = 8
SPREAD = 16
VMEM = 24 * 2**20
COST_A = 3 * 10**10
COST_B = 3 * 10**10

SIZES = (8, 4, 2)


def root(y, z, core):
    return (y == 0) & (z == 0) & (core == 0)


def lead(y, z, core):
    return (y % 2 == 0) & (z == 0) & (core == 0)


def wing(y, z, core):
    return (y % 2 == 0) & ((z != 0) ^ (core == 1))


def plain(y, z, core):
    return (y % 2 == 0) & (z != 0) & (core == 0)


ROUNDS = (
    ((root, (4, 0, 0)), (root, (2, 0, 0)), (root, (6, 0, 0))),
    ((lead, (0, 2, 0)), (lead, (0, 1, 0)), (lead, (0, 3, 0)), (lead, (0, 0, 1))),
    ((wing, (1, 0, 0)), (wing, (1, 0, 1)), (plain, (0, 0, 1))),
)


def place_of(frame):
    return frame // (SIZES[1] * SIZES[2]), frame // SIZES[2] % SIZES[1], frame % SIZES[2]


def pairs_of(senders, step):
    pairs = []
    for frame in range(math.prod(SIZES)):
        if senders(*place_of(frame)):
            y, z, core = ((a + b) % n for a, b, n in zip(place_of(frame), step, SIZES))
            pairs.append((frame, (y * SIZES[1] + z) * SIZES[2] + core))
    return pairs


def which_of(frame, turn):
    place = (frame >> 3, (frame >> 1) & 3, frame & 1)
    which = 0
    for k, (senders, step) in enumerate(ROUNDS[turn]):
        y, z, core = ((at - by) & (n - 1) for at, by, n in zip(place, step, SIZES))
        which = which + jnp.where(senders(y, z, core), k + 1, 0)
    return which


def normed_of(values, gain):
    values = values.astype(jnp.float32)
    center = values - jnp.mean(values, axis=-1, keepdims=True)
    spread = jnp.mean(center * center, axis=-1, keepdims=True)
    return (center * lax.rsqrt(spread + 1e-05) * gain).astype(jnp.bfloat16)


def project(normed, weight):
    return jnp.dot(normed, weight, preferred_element_type=jnp.float32)


def by_head(rows):
    channels, positions = rows.shape[1], rows.shape[0]
    return rows.astype(jnp.bfloat16).T.reshape(HEADS, channels // HEADS, positions)


def own_kernel(frame, own, prior, gain, w_query, w_key, w_value, after, out):
    del after
    positions, channels = own.shape
    head = channels // HEADS
    scale = math.log2(math.e) / math.sqrt(head)
    before = jnp.where(frame[0] == 0, own[...].astype(jnp.float32), prior[...].astype(jnp.float32))
    normed = normed_of(own[...], gain[...])
    both = jnp.concatenate([normed, normed_of(before, gain[...])], axis=0)
    out[:, :head, :] = by_head(project(normed, w_query[...]) * scale)
    for k, weight in enumerate((w_key, w_value)):
        rows = project(both, weight[...])
        out[:, (1 + k) * head : (2 + k) * head, :] = by_head(rows[:positions])
        out[:, (3 + k) * head : (4 + k) * head, :] = by_head(rows[positions:])


def pick_kernel(turn, frame, held, *rest):
    *arrived, out = rest
    which = which_of(frame[0], turn)
    for k, ref in enumerate((held, *arrived)):

        @pl.when(which == k)
        def _():
            if turn == 0 and k == 0:
                pltpu.sync_copy(ref, out)
            else:
                out[...] = ref[...]


def first_kernel(frame, held, *rest):
    *arrived, gain, w_key, w_value, out, latents = rest
    pick_kernel(2, frame, held, *arrived, latents)
    head = latents.shape[1] // HEADS
    normed = normed_of(latents[...], gain[...])
    out[:, :head, :] = by_head(project(normed, w_key[...]))
    out[:, head:, :] = by_head(project(normed, w_value[...]))


def joined(ref, start, size, blocks):
    return jnp.concatenate([ref[b, start : start + size, :] for b in blocks], axis=1)


def ones_row(count):
    return (lax.broadcasted_iota(jnp.int32, (SPREAD, count), 0) == 0).astype(jnp.float32).astype(jnp.bfloat16)


def scores_of(key, query):
    return lax.dot_general(key, query, (((0,), (0,)), ((), ())), preferred_element_type=jnp.float32)


GROUP = 4


def near_kernel(rows, peak, total, queries):
    blocks, _, width = rows.shape
    head = rows.shape[1] // 5
    every = range(blocks)
    keys = [joined(rows, start * head, head, every) for start in (1, 3)]
    values = [
        jnp.concatenate([joined(rows, start * head, head, every), ones_row(blocks * width)], axis=0)
        for start in (2, 4)
    ]
    for g in range(0, blocks, GROUP):
        query = joined(rows, 0, head, range(g, g + GROUP))
        queries[:, g * width : (g + GROUP) * width] = query
        scores = [scores_of(key, query) for key in keys]
        top = jnp.maximum(*[jnp.max(s, axis=0, keepdims=True) for s in scores])
        span = slice(g * width, (g + GROUP) * width)
        peak[:, span] = jnp.broadcast_to(top, (8, GROUP * width))
        total[:, span] = sum(
            jnp.dot(value, jnp.exp2(s - top).astype(jnp.bfloat16), preferred_element_type=jnp.float32)
            for value, s in zip(values, scores)
        )


def far_kernel(queries, first, peak, total, out):
    blocks, _, width = first.shape
    head = queries.shape[0]
    every = range(blocks)
    key = joined(first, 0, head, every)
    value = jnp.concatenate([joined(first, head, head, every), ones_row(blocks * width)], axis=0)
    for g in range(0, blocks, GROUP):
        span = slice(g * width, (g + GROUP) * width)
        scores = scores_of(key, queries[:, span])
        before = peak[:1, span]
        top = jnp.maximum(jnp.max(scores, axis=0, keepdims=True), before)
        weights = jnp.exp2(scores - top).astype(jnp.bfloat16)
        both = total[:, span] * jnp.exp2(before - top) + jnp.dot(
            value, weights, preferred_element_type=jnp.float32
        )
        attended = (both[:head] / both[head : head + 1]).astype(jnp.bfloat16)
        for b in range(GROUP):
            out[g + b] = attended[:, b * width : (b + 1) * width]


def mix_kernel(attended, latents, w_out, out):
    heads, head, positions = attended.shape
    rows = attended[...].reshape(heads * head, positions).T
    update = jnp.dot(rows, w_out[...], preferred_element_type=jnp.float32)
    out[...] = (latents[...].astype(jnp.float32) + update).astype(jnp.bfloat16)


def call(kernel, name, shapes, operands, kinds, scratch=(), flops=0, moved=0):
    spaces = {"s": pltpu.SMEM, "v": pltpu.VMEM, "a": pl.ANY}
    return pl.pallas_call(
        kernel,
        out_shape=shapes,
        in_specs=[pl.BlockSpec(memory_space=spaces[kind]) for kind in kinds],
        out_specs=jax.tree.map(lambda _: pl.BlockSpec(memory_space=pltpu.VMEM), shapes),
        scratch_shapes=list(scratch),
        compiler_params=pltpu.CompilerParams(vmem_limit_bytes=VMEM),
        cost_estimate=pl.CostEstimate(flops=int(flops), bytes_accessed=int(moved), transcendentals=0),
        name=name,
    )(*operands)


def body(latents, norm_gain, w_query, w_key, w_value, w_out):
    _, positions, channels = latents.shape
    head = channels // HEADS
    own = latents[0]
    frames = lax.axis_size("frame")
    at = lax.axis_index("frame")[None]
    total_positions = lax.axis_size("row") * positions

    def shape(*dims, kind=jnp.bfloat16):
        return jax.ShapeDtypeStruct(dims, kind)

    def send(array, turn):
        return [lax.ppermute(array, "frame", pairs_of(*permute)) for permute in ROUNDS[turn]]

    arrived = send(own, 0)
    prior = lax.ppermute(own, "frame", [(i, i + 1) for i in range(frames - 1)])
    held_a = call(
        functools.partial(pick_kernel, 0), "pick_a", shape(positions, channels),
        (at, own, *arrived), "savvv", flops=COST_A,
    )
    arrived = send(held_a, 1)
    held_b = call(
        functools.partial(pick_kernel, 1), "pick_b", shape(positions, channels),
        (at, held_a, *arrived), "svvvvv", flops=COST_B,
    )
    arrived = send(held_b, 2)

    mine = call(
        own_kernel, "own_rows", shape(HEADS, 5 * head, positions),
        (at, own, prior, norm_gain, w_query, w_key, w_value, held_a), "svvvvvva",
        flops=2 * positions * channels * channels * 5, moved=3 * 2 * channels * channels,
    )
    rows = lax.all_to_all(mine, "row", 0, 0, tiled=True)
    wide = (shape(8, total_positions, kind=jnp.float32), shape(head + SPREAD, total_positions, kind=jnp.float32))
    peak, total, queries = call(
        near_kernel, "near", (*wide, shape(head, total_positions)), (rows,), "v",
        flops=8 * head * total_positions * total_positions, moved=2 * 8 * 5 * head * positions,
    )
    theirs = call(
        first_kernel, "first_rows", shape(HEADS, 2 * head, positions),
        (at, held_b, *arrived, norm_gain, w_key, w_value), "svvvvvvv",
        scratch=[pltpu.VMEM((positions, channels), jnp.bfloat16)],
        flops=2 * positions * channels * channels * 2, moved=2 * 2 * channels * channels,
    )
    first = lax.all_to_all(theirs, "row", 0, 0, tiled=True)
    attended = call(
        far_kernel, "far", shape(HEADS, head, positions), (queries, first, peak, total), "vvvv",
        flops=4 * head * total_positions * total_positions, moved=2 * 8 * 2 * head * positions,
    )
    back = lax.all_to_all(attended, "row", 0, 0, tiled=True)
    mixed = call(
        mix_kernel, "mix", shape(positions, channels), (back, own, w_out), "vvv",
        flops=2 * positions * channels * channels, moved=2 * channels * channels,
    )
    return mixed[None]


def solution(mesh):
    return jax.shard_map(
        body,
        mesh=mesh,
        in_specs=(P("frame", "row", None), P(), P(), P(), P(), P()),
        out_specs=P("frame", "row", None),
        check_vma=False,
    )
```

time: 85.5 us -> 62.5 us (0.73)
  the two profiles are of different devices: /device:TPU:56 before, /device:TPU:48 now
where the time goes in v2:
time: 62.5 us; the launch traced here: 62 us
  starting transfers between devices  21.4 us (34%)
  waiting for transfers between devices  20 us (32%)
  Pallas kernels  9.88 us (16%)
  blocking collectives  9.46 us (15%)
  local copies, waits for them, and re-layouts  0.94 us (2%)
    ppermute x10, starting transfers between devices, send(): lax.ppermute(array, 'frame', pairs_of(*permute))  10.1 us
    pallas_call x7, Pallas kernels, call(): pl.pallas_call(kernel, out_shape=shapes, in_specs=[pl.BlockSpec(memory_sp...  9.88 us
    all_to_all x1, blocking collectives, body(): back = lax.all_to_all(attended, 'row', 0, 0, tiled=True)  9.46 us
    ppermute x10, waiting for transfers between devices, send(): lax.ppermute(array, 'frame', pairs_of(*permute))  9.13 us
    all_to_all x1, waiting for transfers between devices, body(): rows = lax.all_to_all(mine, 'row', 0, 0, tiled=True)  6.65 us
    all_to_all x1, starting transfers between devices, body(): rows = lax.all_to_all(mine, 'row', 0, 0, tiled=True)  6 us
    all_to_all x1, waiting for transfers between devices, body(): first = lax.all_to_all(theirs, 'row', 0, 0, tiled=True)  4.26 us
    all_to_all x1, starting transfers between devices, body(): first = lax.all_to_all(theirs, 'row', 0, 0, tiled=True)  3.43 us
  transfers between devices with their start and end apart: 13, of which 3 were waited for; matrix products, arithmetic and copies ran while one was open for 0% of the time, Pallas kernels for 11%

profile of v2, /device:TPU:48, one launch (start us, length us, event | category | flops | bytes accessed | tf_op | source)
XLA Modules:
  0.0 62.0 jit_solution(9872148033681129459)
XLA Ops:
  0.0 0.7 %collective-permute-start.1 = (bf16[128,640]{1,0:T(8,128)(2,1)}, bf16[128,640]{1,0:T(8,128)(2,1)S(1)}, u32[]{:S(2)}, u32[]{:S(2)}) collective-permute-start(bf16[128,640]{1,0:T(8,128)(2,1)} %bitcast.3), channel_id=1, source_target_pairs={{0,256},{1,257},{2,258},{3,259},{4,260},{5,261},{6,262},{7,263}} | collective-permute-start | bytes 491528 | tf_op jit(solution)/shard_map/ppermute | solution.py:208
  0.7 0.7 %collective-permute-start.2 = (bf16[128,640]{1,0:T(8,128)(2,1)}, bf16[128,640]{1,0:T(8,128)(2,1)S(1)}, u32[]{:S(2)}, u32[]{:S(2)}) collective-permute-start(bf16[128,640]{1,0:T(8,128)(2,1)} %bitcast.4), channel_id=1, source_target_pairs={{0,128},{1,129},{2,130},{3,131},{4,132},{5,133},{6,134},{7,135}} | collective-permute-start | bytes 491528 | tf_op jit(solution)/shard_map/ppermute | solution.py:208
  1.3 1.3 %collective-permute-start.3 = (bf16[128,640]{1,0:T(8,128)(2,1)}, bf16[128,640]{1,0:T(8,128)(2,1)S(1)}, u32[]{:S(2)}, u32[]{:S(2)}) collective-permute-start(bf16[128,640]{1,0:T(8,128)(2,1)} %bitcast.5), channel_id=1, source_target_pairs={{0,384},{1,385},{2,386},{3,387},{4,388},{5,389},{6,390},{7,391}} | collective-permute-start | bytes 491528 | tf_op jit(solution)/shard_map/ppermute | solution.py:208
  2.6 1.9 %collective-permute-start = (bf16[128,640]{1,0:T(8,128)(2,1)}, bf16[128,640]{1,0:T(8,128)(2,1)S(1)}, u32[]{:S(2)}, u32[]{:S(2)}) collective-permute-start(bf16[128,640]{1,0:T(8,128)(2,1)} %bitcast.6), channel_id=1, source_target_pairs={{0,8},{8,16},{16,24},{24,32},{32,40},{40,48},{48,56},{56,64},{64,7... | collective-permute-start | bytes 491528 | tf_op jit(solution)/shard_map/ppermute | solution.py:211
  4.6 9.1 %collective-permute-done.3.rest_2_ = bf16[128,640]{1,0:T(8,128)(2,1)S(1)} collective-permute-done((bf16[128,640]{1,0:T(8,128)(2,1)}, bf16[128,640]{1,0:T(8,128)(2,1)S(1)}, u32[]{:S(2)}, u32[]{:S(2)}) %collective-permute-start.3) | collective-permute-done | bytes 163872 | tf_op jit(solution)/shard_map/ppermute | solution.py:208
  13.7 0.9 %copy-done.4 = bf16[1,128,640]{2,1,0:T(8,128)(2,1)S(1)} copy-done((bf16[1,128,640]{2,1,0:T(8,128)(2,1)S(1)}, bf16[1,128,640]{2,1,0:T(8,128)(2,1)}, u32[]{:S(2)}) %copy-start.4) | copy-done | bytes 163864
  14.7 1.5 %collective-permute-start.4 = (bf16[128,640]{1,0:T(8,128)(2,1)S(1)}, bf16[128,640]{1,0:T(8,128)(2,1)S(1)}, u32[]{:S(2)}, u32[]{:S(2)}) collective-permute-start(bf16[128,640]{1,0:T(8,128)(2,1)S(1)} %pick_a.1.after.held), channel_id=1, source_target_pairs={{0,32},{128,160},{256,288},{384,416},{1,33},{129,161},{257,289},{3... | collective-permute-start | bytes 491528 | tf_op jit(solution)/shard_map/ppermute | solution.py:208
  16.2 1.3 %collective-permute-start.5 = (bf16[128,640]{1,0:T(8,128)(2,1)S(1)}, bf16[128,640]{1,0:T(8,128)(2,1)S(1)}, u32[]{:S(2)}, u32[]{:S(2)}) collective-permute-start(bf16[128,640]{1,0:T(8,128)(2,1)S(1)} %pick_a.1.after.held), channel_id=1, source_target_pairs={{0,16},{128,144},{256,272},{384,400},{1,17},{129,145},{257,273},{3... | collective-permute-start | bytes 491528 | tf_op jit(solution)/shard_map/ppermute | solution.py:208
  17.5 1.3 %collective-permute-start.6 = (bf16[128,640]{1,0:T(8,128)(2,1)S(1)}, bf16[128,640]{1,0:T(8,128)(2,1)S(1)}, u32[]{:S(2)}, u32[]{:S(2)}) collective-permute-start(bf16[128,640]{1,0:T(8,128)(2,1)S(1)} %pick_a.1.after.held), channel_id=1, source_target_pairs={{0,48},{128,176},{256,304},{384,432},{1,49},{129,177},{257,305},{3... | collective-permute-start | bytes 491528 | tf_op jit(solution)/shard_map/ppermute | solution.py:208
  18.9 1.3 %collective-permute-start.7 = (bf16[128,640]{1,0:T(8,128)(2,1)S(1)}, bf16[128,640]{1,0:T(8,128)(2,1)S(1)}, u32[]{:S(2)}, u32[]{:S(2)}) collective-permute-start(bf16[128,640]{1,0:T(8,128)(2,1)S(1)} %pick_a.1.after.held), channel_id=1, source_target_pairs={{0,8},{128,136},{256,264},{384,392},{1,9},{129,137},{257,265},{385... | collective-permute-start | bytes 491528 | tf_op jit(solution)/shard_map/ppermute | solution.py:208
  20.2 2.0 %own_rows.1 = bf16[8,400,128]{2,1,0:T(8,128)(2,1)} custom-call(s32[1]{0:T(128)} %bitcast.frame, bf16[128,640]{1,0:T(8,128)(2,1)S(1)} %bitcast.8, bf16[128,640]{1,0:T(8,128)(2,1)S(1)} %collective-permute-done.prior, f32[640]{0:T(1024)S(1)} %copy-done.6, bf16[640,640]{1,0:T(8,128)(2,1)S(1)} %copy-done.2, bf16[640,640]{1,0:T(8,128)(2,1)S(1)} %copy-done, ...), custom_call_target="tpu_custom_call" | custom-call | flops 524288000 | bytes 2457600 | tf_op jit(solution)/shard_map/own_rows/pallas_call | solution.py:184
  22.3 6.0 %all-to-all-start = ((bf16[8,400,128]{2,1,0:T(8,128)(2,1)}), bf16[8,400,128]{2,1,0:T(8,128)(2,1)S(1)}, u32[]{:S(2)}, u32[]{:S(2)}) async-start(bf16[8,400,128]{2,1,0:T(8,128)(2,1)} %own_rows.1), calls=%async_computation | async-start | bytes 1638400 | tf_op jit(solution)/shard_map/all_to_all | solution.py:228
  28.3 0.1 pick_b.1.held
  28.4 0.7 %collective-permute-start.8 = (bf16[128,640]{1,0:T(8,128)(2,1)S(1)}, bf16[128,640]{1,0:T(8,128)(2,1)S(1)}, u32[]{:S(2)}, u32[]{:S(2)}) collective-permute-start(bf16[128,640]{1,0:T(8,128)(2,1)S(1)} %pick_b.1.held), channel_id=1, source_target_pairs={{8,72},{16,80},{32,96},{48,112},{136,200},{144,208},{160,224},{176... | collective-permute-start | bytes 491528 | tf_op jit(solution)/shard_map/ppermute | solution.py:208
  29.0 0.7 %collective-permute-start.9 = (bf16[128,640]{1,0:T(8,128)(2,1)S(1)}, bf16[128,640]{1,0:T(8,128)(2,1)S(1)}, u32[]{:S(2)}, u32[]{:S(2)}) collective-permute-start(bf16[128,640]{1,0:T(8,128)(2,1)S(1)} %pick_b.1.held), channel_id=1, source_target_pairs={{8,64},{16,88},{32,104},{48,120},{136,192},{144,216},{160,232},{17... | collective-permute-start | bytes 491528 | tf_op jit(solution)/shard_map/ppermute | solution.py:208
  29.7 0.7 %collective-permute-start.10 = (bf16[128,640]{1,0:T(8,128)(2,1)S(1)}, bf16[128,640]{1,0:T(8,128)(2,1)S(1)}, u32[]{:S(2)}, u32[]{:S(2)}) collective-permute-start(bf16[128,640]{1,0:T(8,128)(2,1)S(1)} %pick_b.1.held), channel_id=1, source_target_pairs={{16,24},{32,40},{48,56},{144,152},{160,168},{176,184},{272,280},{2... | collective-permute-start | bytes 491528 | tf_op jit(solution)/shard_map/ppermute | solution.py:208
  30.4 1.5 %first_rows.1 = bf16[8,160,128]{2,1,0:T(8,128)(2,1)} custom-call(s32[1]{0:T(128)} %bitcast.frame, bf16[128,640]{1,0:T(8,128)(2,1)S(1)} %pick_b.1.held, bf16[128,640]{1,0:T(8,128)(2,1)S(1)} %collective-permute-done.8.rest_0_, bf16[128,640]{1,0:T(8,128)(2,1)S(1)} %collective-permute-done.9.rest_1_, bf16[128,640]{1,0:T(8,128)(2,1)S(1)} %collective-permute-done.10.rest_2_, ...), custom_call_target="tpu_custom_call" | custom-call | flops 209715200 | bytes 1638400 | tf_op jit(solution)/shard_map/first_rows/pallas_call | solution.py:184
  31.9 6.7 %all-to-all-done.rows = bf16[8,400,128]{2,1,0:T(8,128)(2,1)S(1)} async-done(((bf16[8,400,128]{2,1,0:T(8,128)(2,1)}), bf16[8,400,128]{2,1,0:T(8,128)(2,1)S(1)}, u32[]{:S(2)}, u32[]{:S(2)}) %all-to-all-start) | async-done | bytes 819232 | tf_op jit(solution)/shard_map/all_to_all | solution.py:228
  38.6 3.4 %all-to-all-start.1 = ((bf16[8,160,128]{2,1,0:T(8,128)(2,1)}), bf16[8,160,128]{2,1,0:T(8,128)(2,1)S(1)}, u32[]{:S(2)}, u32[]{:S(2)}) async-start(bf16[8,160,128]{2,1,0:T(8,128)(2,1)} %first_rows.1), calls=%async_computation.1 | async-start | bytes 655360 | tf_op jit(solution)/shard_map/all_to_all | solution.py:240
  42.0 3.3 %near.1 = (f32[8,1024]{1,0:T(8,128)S(1)}, f32[96,1024]{1,0:T(8,128)S(1)}, bf16[80,1024]{1,0:T(8,128)(2,1)S(1)}) custom-call(bf16[8,400,128]{2,1,0:T(8,128)(2,1)S(1)} %all-to-all-done.rows), custom_call_target="tpu_custom_call" | custom-call | flops 671088640 | bytes 819200 | tf_op jit(solution)/shard_map/near/pallas_call | solution.py:184
  45.3 4.3 %all-to-all-done.1.first = bf16[8,160,128]{2,1,0:T(8,128)(2,1)S(1)} async-done(((bf16[8,160,128]{2,1,0:T(8,128)(2,1)}), bf16[8,160,128]{2,1,0:T(8,128)(2,1)S(1)}, u32[]{:S(2)}, u32[]{:S(2)}) %all-to-all-start.1) | async-done | bytes 327712 | tf_op jit(solution)/shard_map/all_to_all | solution.py:240
  49.6 1.9 %far.1 = bf16[8,80,128]{2,1,0:T(8,128)(2,1)S(1)} custom-call(bf16[80,1024]{1,0:T(8,128)(2,1)S(1)} %get-tuple-element.8.queries, bf16[8,160,128]{2,1,0:T(8,128)(2,1)S(1)} %all-to-all-done.1.first, f32[8,1024]{1,0:T(8,128)S(1)} %get-tuple-element.9.peak, f32[96,1024]{1,0:T(8,128)S(1)} %get-tuple-element.10.total), custom_call_target="tpu_custom_call" | custom-call | flops 335544320 | bytes 327680 | tf_op jit(solution)/shard_map/far/pallas_call | solution.py:184
  51.5 9.5 %all_to_all.15.attended = bf16[8,80,128]{2,1,0:T(8,128)(2,1)S(1)} all-to-all(bf16[8,80,128]{2,1,0:T(8,128)(2,1)S(1)} %far.1), channel_id=1, replica_groups=mesh['frame'=64,'row'=8] {'row'}, dimensions={0} | all-to-all | bytes 327680 | tf_op jit(solution)/shard_map/all_to_all | solution.py:245
  61.0 1.0 %mix.1 = bf16[128,640]{1,0:T(8,128)(2,1)} custom-call(bf16[8,80,128]{2,1,0:T(8,128)(2,1)S(1)} %all_to_all.15.attended, bf16[128,640]{1,0:T(8,128)(2,1)S(1)} %bitcast.9, bf16[640,640]{1,0:T(8,128)(2,1)S(1)} %copy-done.3), custom_call_target="tpu_custom_call" | custom-call | flops 104857600 | bytes 819200 | tf_op jit(solution)/shard_map/mix/pallas_call | solution.py:184
  (24 shorter events, 0.1 us)
Async XLA Ops:
  0.0 4.6 %collective-permute-start.1 = (bf16[128,640]{1,0:T(8,128)(2,1)}, bf16[128,640]{1,0:T(8,128)(2,1)S(1)}, u32[]{:S(2)}, u32[]{:S(2)}) collective-permute-start(bf16[128,640]{1,0:T(8,128)(2,1)} %bitcast.3), channel_id=1, source_target_pairs={{0,256},{1,257},{2,258},{3,259},{4,260},{5,261},{6,262},{7,263}} | collective-permute-start | bytes 491528 | tf_op jit(solution)/shard_map/ppermute | solution.py:208
  0.7 3.9 %collective-permute-start.2 = (bf16[128,640]{1,0:T(8,128)(2,1)}, bf16[128,640]{1,0:T(8,128)(2,1)S(1)}, u32[]{:S(2)}, u32[]{:S(2)}) collective-permute-start(bf16[128,640]{1,0:T(8,128)(2,1)} %bitcast.4), channel_id=1, source_target_pairs={{0,128},{1,129},{2,130},{3,131},{4,132},{5,133},{6,134},{7,135}} | collective-permute-start | bytes 491528 | tf_op jit(solution)/shard_map/ppermute | solution.py:208
  1.3 12.4 %collective-permute-start.3 = (bf16[128,640]{1,0:T(8,128)(2,1)}, bf16[128,640]{1,0:T(8,128)(2,1)S(1)}, u32[]{:S(2)}, u32[]{:S(2)}) collective-permute-start(bf16[128,640]{1,0:T(8,128)(2,1)} %bitcast.5), channel_id=1, source_target_pairs={{0,384},{1,385},{2,386},{3,387},{4,388},{5,389},{6,390},{7,391}} | collective-permute-start | bytes 491528 | tf_op jit(solution)/shard_map/ppermute | solution.py:208
  2.6 17.5 %collective-permute-start = (bf16[128,640]{1,0:T(8,128)(2,1)}, bf16[128,640]{1,0:T(8,128)(2,1)S(1)}, u32[]{:S(2)}, u32[]{:S(2)}) collective-permute-start(bf16[128,640]{1,0:T(8,128)(2,1)} %bitcast.6), channel_id=1, source_target_pairs={{0,8},{8,16},{16,24},{24,32},{32,40},{40,48},{48,56},{56,64},{64,7... | collective-permute-start | bytes 491528 | tf_op jit(solution)/shard_map/ppermute | solution.py:211
  13.7 0.9 %copy-start.4 = (bf16[1,128,640]{2,1,0:T(8,128)(2,1)S(1)}, bf16[1,128,640]{2,1,0:T(8,128)(2,1)}, u32[]{:S(2)}) copy-start(bf16[1,128,640]{2,1,0:T(8,128)(2,1)} %param.6) | copy-start | bytes 491524
  14.6 5.5 %copy-start = (bf16[640,640]{1,0:T(8,128)(2,1)S(1)}, bf16[640,640]{1,0:T(8,128)(2,1)}, u32[]{:S(2)}) copy-start(bf16[640,640]{1,0:T(8,128)(2,1)} %rest_4_.1) | copy-start | bytes 2457604
  14.6 5.5 %copy-start.1 = (bf16[640,640]{1,0:T(8,128)(2,1)S(1)}, bf16[640,640]{1,0:T(8,128)(2,1)}, u32[]{:S(2)}) copy-start(bf16[640,640]{1,0:T(8,128)(2,1)} %rest_5_.1) | copy-start | bytes 2457604
  14.6 5.6 %copy-start.2 = (bf16[640,640]{1,0:T(8,128)(2,1)S(1)}, bf16[640,640]{1,0:T(8,128)(2,1)}, u32[]{:S(2)}) copy-start(bf16[640,640]{1,0:T(8,128)(2,1)} %w_query.1) | copy-start | bytes 2457604
  14.6 5.6 %copy-start.6 = (f32[640]{0:T(1024)S(1)}, f32[640]{0:T(1024)}, u32[]{:S(2)}) copy-start(f32[640]{0:T(1024)} %rest_3_.1) | copy-start | bytes 7684
  14.7 13.6 %collective-permute-start.4 = (bf16[128,640]{1,0:T(8,128)(2,1)S(1)}, bf16[128,640]{1,0:T(8,128)(2,1)S(1)}, u32[]{:S(2)}, u32[]{:S(2)}) collective-permute-start(bf16[128,640]{1,0:T(8,128)(2,1)S(1)} %pick_a.1.after.held), channel_id=1, source_target_pairs={{0,32},{128,160},{256,288},{384,416},{1,33},{129,161},{257,289},{3... | collective-permute-start | bytes 491528 | tf_op jit(solution)/shard_map/ppermute | solution.py:208
  16.2 12.0 %collective-permute-start.5 = (bf16[128,640]{1,0:T(8,128)(2,1)S(1)}, bf16[128,640]{1,0:T(8,128)(2,1)S(1)}, u32[]{:S(2)}, u32[]{:S(2)}) collective-permute-start(bf16[128,640]{1,0:T(8,128)(2,1)S(1)} %pick_a.1.after.held), channel_id=1, source_target_pairs={{0,16},{128,144},{256,272},{384,400},{1,17},{129,145},{257,273},{3... | collective-permute-start | bytes 491528 | tf_op jit(solution)/shard_map/ppermute | solution.py:208
  17.5 10.7 %collective-permute-start.6 = (bf16[128,640]{1,0:T(8,128)(2,1)S(1)}, bf16[128,640]{1,0:T(8,128)(2,1)S(1)}, u32[]{:S(2)}, u32[]{:S(2)}) collective-permute-start(bf16[128,640]{1,0:T(8,128)(2,1)S(1)} %pick_a.1.after.held), channel_id=1, source_target_pairs={{0,48},{128,176},{256,304},{384,432},{1,49},{129,177},{257,305},{3... | collective-permute-start | bytes 491528 | tf_op jit(solution)/shard_map/ppermute | solution.py:208
  18.9 9.4 %collective-permute-start.7 = (bf16[128,640]{1,0:T(8,128)(2,1)S(1)}, bf16[128,640]{1,0:T(8,128)(2,1)S(1)}, u32[]{:S(2)}, u32[]{:S(2)}) collective-permute-start(bf16[128,640]{1,0:T(8,128)(2,1)S(1)} %pick_a.1.after.held), channel_id=1, source_target_pairs={{0,8},{128,136},{256,264},{384,392},{1,9},{129,137},{257,265},{385... | collective-permute-start | bytes 491528 | tf_op jit(solution)/shard_map/ppermute | solution.py:208
  22.3 16.3 %all-to-all-start = ((bf16[8,400,128]{2,1,0:T(8,128)(2,1)}), bf16[8,400,128]{2,1,0:T(8,128)(2,1)S(1)}, u32[]{:S(2)}, u32[]{:S(2)}) async-start(bf16[8,400,128]{2,1,0:T(8,128)(2,1)} %own_rows.1), calls=%async_computation | async-start | bytes 1638400 | tf_op jit(solution)/shard_map/all_to_all | solution.py:228
  28.4 2.0 %collective-permute-start.8 = (bf16[128,640]{1,0:T(8,128)(2,1)S(1)}, bf16[128,640]{1,0:T(8,128)(2,1)S(1)}, u32[]{:S(2)}, u32[]{:S(2)}) collective-permute-start(bf16[128,640]{1,0:T(8,128)(2,1)S(1)} %pick_b.1.held), channel_id=1, source_target_pairs={{8,72},{16,80},{32,96},{48,112},{136,200},{144,208},{160,224},{176... | collective-permute-start | bytes 491528 | tf_op jit(solution)/shard_map/ppermute | solution.py:208
  29.0 1.4 %collective-permute-start.9 = (bf16[128,640]{1,0:T(8,128)(2,1)S(1)}, bf16[128,640]{1,0:T(8,128)(2,1)S(1)}, u32[]{:S(2)}, u32[]{:S(2)}) collective-permute-start(bf16[128,640]{1,0:T(8,128)(2,1)S(1)} %pick_b.1.held), channel_id=1, source_target_pairs={{8,64},{16,88},{32,104},{48,120},{136,192},{144,216},{160,232},{17... | collective-permute-start | bytes 491528 | tf_op jit(solution)/shard_map/ppermute | solution.py:208
  29.7 0.7 %collective-permute-start.10 = (bf16[128,640]{1,0:T(8,128)(2,1)S(1)}, bf16[128,640]{1,0:T(8,128)(2,1)S(1)}, u32[]{:S(2)}, u32[]{:S(2)}) collective-permute-start(bf16[128,640]{1,0:T(8,128)(2,1)S(1)} %pick_b.1.held), channel_id=1, source_target_pairs={{16,24},{32,40},{48,56},{144,152},{160,168},{176,184},{272,280},{2... | collective-permute-start | bytes 491528 | tf_op jit(solution)/shard_map/ppermute | solution.py:208
  38.6 11.0 %all-to-all-start.1 = ((bf16[8,160,128]{2,1,0:T(8,128)(2,1)}), bf16[8,160,128]{2,1,0:T(8,128)(2,1)S(1)}, u32[]{:S(2)}, u32[]{:S(2)}) async-start(bf16[8,160,128]{2,1,0:T(8,128)(2,1)} %first_rows.1), calls=%async_computation.1 | async-start | bytes 655360 | tf_op jit(solution)/shard_map/all_to_all | solution.py:240
  45.3 15.7 %copy-start.3 = (bf16[640,640]{1,0:T(8,128)(2,1)S(1)}, bf16[640,640]{1,0:T(8,128)(2,1)}, u32[]{:S(2)}) copy-start(bf16[640,640]{1,0:T(8,128)(2,1)} %w_out.1) | copy-start | bytes 2457604
  51.5 9.5 %copy-start.5 = (bf16[1,128,640]{2,1,0:T(8,128)(2,1)S(1)}, bf16[1,128,640]{2,1,0:T(8,128)(2,1)}, u32[]{:S(2)}) copy-start(bf16[1,128,640]{2,1,0:T(8,128)(2,1)} %param.6) | copy-start | bytes 491524

commit v3 on v2

--- a/solution.py
+++ b/solution.py
@@ -11,6 +11,7 @@
 HEADS = 8
 SPREAD = 16
 VMEM = 24 * 2**20
+COST_STAGE = 10**9
 COST_A = 3 * 10**10
 COST_B = 3 * 10**10
 
@@ -25,18 +26,14 @@
     return (y % 2 == 0) & (z == 0) & (core == 0)
 
 
-def wing(y, z, core):
-    return (y % 2 == 0) & ((z != 0) ^ (core == 1))
-
-
-def plain(y, z, core):
-    return (y % 2 == 0) & (z != 0) & (core == 0)
+def even(y, z, core):
+    return (y % 2 == 0) & (core == 0)
 
 
 ROUNDS = (
     ((root, (4, 0, 0)), (root, (2, 0, 0)), (root, (6, 0, 0))),
-    ((lead, (0, 2, 0)), (lead, (0, 1, 0)), (lead, (0, 3, 0)), (lead, (0, 0, 1))),
-    ((wing, (1, 0, 0)), (wing, (1, 0, 1)), (plain, (0, 0, 1))),
+    ((lead, (0, 1, 0)), (lead, (0, 2, 0)), (lead, (0, 3, 0))),
+    ((even, (1, 0, 0)), (even, (1, 0, 1)), (even, (0, 0, 1))),
 )
 
 
@@ -78,19 +75,33 @@
     return rows.astype(jnp.bfloat16).T.reshape(HEADS, channels // HEADS, positions)
 
 
-def own_kernel(frame, own, prior, gain, w_query, w_key, w_value, after, out):
+def own_kernel(own, gain, w_query, w_key, w_value, out):
+    head = own.shape[1] // HEADS
+    normed = normed_of(own[...], gain[...])
+    scale = math.log2(math.e) / math.sqrt(head)
+    out[:, :head, :] = by_head(project(normed, w_query[...]) * scale)
+    out[:, head : 2 * head, :] = by_head(project(normed, w_key[...]))
+    out[:, 2 * head :, :] = by_head(project(normed, w_value[...]))
+
+
+def prior_kernel(frame, mine, own, prior, gain, w_key, w_value, after, out, rows, done):
     del after
-    positions, channels = own.shape
-    head = channels // HEADS
-    scale = math.log2(math.e) / math.sqrt(head)
+    head = own.shape[1] // HEADS
+    copies = [pltpu.make_async_copy(mine, out.at[:, : 3 * head, :], done.at[2])]
+    copies[0].start()
     before = jnp.where(frame[0] == 0, own[...].astype(jnp.float32), prior[...].astype(jnp.float32))
-    normed = normed_of(own[...], gain[...])
-    both = jnp.concatenate([normed, normed_of(before, gain[...])], axis=0)
-    out[:, :head, :] = by_head(project(normed, w_query[...]) * scale)
+    normed = normed_of(before, gain[...])
     for k, weight in enumerate((w_key, w_value)):
-        rows = project(both, weight[...])
-        out[:, (1 + k) * head : (2 + k) * head, :] = by_head(rows[:positions])
-        out[:, (3 + k) * head : (4 + k) * head, :] = by_head(rows[positions:])
+        rows[k] = by_head(project(normed, weight[...]))
+        copy = pltpu.make_async_copy(rows.at[k], out.at[:, (3 + k) * head : (4 + k) * head, :], done.at[k])
+        copy.start()
+        copies.append(copy)
+    for copy in copies:
+        copy.wait()
+
+
+def stage_kernel(latents, out):
+    pltpu.sync_copy(latents, out)
 
 
 def pick_kernel(turn, frame, held, *rest):
@@ -100,10 +111,7 @@
 
         @pl.when(which == k)
         def _():
-            if turn == 0 and k == 0:
-                pltpu.sync_copy(ref, out)
-            else:
-                out[...] = ref[...]
+            out[...] = ref[...]
 
 
 def first_kernel(frame, held, *rest):
@@ -156,20 +164,15 @@
     blocks, _, width = first.shape
     head = queries.shape[0]
     every = range(blocks)
-    key = joined(first, 0, head, every)
     value = jnp.concatenate([joined(first, head, head, every), ones_row(blocks * width)], axis=0)
-    for g in range(0, blocks, GROUP):
-        span = slice(g * width, (g + GROUP) * width)
-        scores = scores_of(key, queries[:, span])
-        before = peak[:1, span]
-        top = jnp.maximum(jnp.max(scores, axis=0, keepdims=True), before)
-        weights = jnp.exp2(scores - top).astype(jnp.bfloat16)
-        both = total[:, span] * jnp.exp2(before - top) + jnp.dot(
-            value, weights, preferred_element_type=jnp.float32
-        )
-        attended = (both[:head] / both[head : head + 1]).astype(jnp.bfloat16)
-        for b in range(GROUP):
-            out[g + b] = attended[:, b * width : (b + 1) * width]
+    scores = scores_of(joined(first, 0, head, every), queries[...])
+    before = peak[:1, :]
+    top = jnp.maximum(jnp.max(scores, axis=0, keepdims=True), before)
+    weights = jnp.exp2(scores - top).astype(jnp.bfloat16)
+    both = total[...] * jnp.exp2(before - top) + jnp.dot(value, weights, preferred_element_type=jnp.float32)
+    attended = (both[:head] / both[head : head + 1]).astype(jnp.bfloat16)
+    for b in every:
+        out[b] = attended[:, b * width : (b + 1) * width]
 
 
 def mix_kernel(attended, latents, w_out, out):
@@ -179,13 +182,13 @@
     out[...] = (latents[...].astype(jnp.float32) + update).astype(jnp.bfloat16)
 
 
-def call(kernel, name, shapes, operands, kinds, scratch=(), flops=0, moved=0):
+def call(kernel, name, shapes, operands, kinds, to=pltpu.VMEM, scratch=(), flops=0, moved=0):
     spaces = {"s": pltpu.SMEM, "v": pltpu.VMEM, "a": pl.ANY}
     return pl.pallas_call(
         kernel,
         out_shape=shapes,
         in_specs=[pl.BlockSpec(memory_space=spaces[kind]) for kind in kinds],
-        out_specs=jax.tree.map(lambda _: pl.BlockSpec(memory_space=pltpu.VMEM), shapes),
+        out_specs=jax.tree.map(lambda _: pl.BlockSpec(memory_space=to), shapes),
         scratch_shapes=list(scratch),
         compiler_params=pltpu.CompilerParams(vmem_limit_bytes=VMEM),
         cost_estimate=pl.CostEstimate(flops=int(flops), bytes_accessed=int(moved), transcendentals=0),
@@ -209,21 +212,28 @@
 
     arrived = send(own, 0)
     prior = lax.ppermute(own, "frame", [(i, i + 1) for i in range(frames - 1)])
+    own = call(stage_kernel, "stage", shape(positions, channels), (own,), "a", flops=COST_STAGE)
     held_a = call(
         functools.partial(pick_kernel, 0), "pick_a", shape(positions, channels),
-        (at, own, *arrived), "savvv", flops=COST_A,
+        (at, own, *arrived), "svvvv", flops=COST_A,
     )
     arrived = send(held_a, 1)
     held_b = call(
         functools.partial(pick_kernel, 1), "pick_b", shape(positions, channels),
-        (at, held_a, *arrived), "svvvvv", flops=COST_B,
+        (at, held_a, *arrived), "svvvv", flops=COST_B,
     )
     arrived = send(held_b, 2)
 
     mine = call(
-        own_kernel, "own_rows", shape(HEADS, 5 * head, positions),
-        (at, own, prior, norm_gain, w_query, w_key, w_value, held_a), "svvvvvva",
-        flops=2 * positions * channels * channels * 5, moved=3 * 2 * channels * channels,
+        own_kernel, "own_rows", shape(HEADS, 3 * head, positions),
+        (own, norm_gain, w_query, w_key, w_value), "vvvvv",
+        flops=2 * positions * channels * channels * 3, moved=3 * 2 * channels * channels,
+    )
+    mine = call(
+        prior_kernel, "prior_rows", shape(HEADS, 5 * head, positions),
+        (at, mine, own, prior, norm_gain, w_key, w_value, held_a), "svvvvvva", to=pl.ANY,
+        scratch=[pltpu.VMEM((2, HEADS, head, positions), jnp.bfloat16), pltpu.SemaphoreType.DMA((3,))],
+        flops=2 * positions * channels * channels * 2, moved=2 * 2 * channels * channels,
     )
     rows = lax.all_to_all(mine, "row", 0, 0, tiled=True)
     wide = (shape(8, total_positions, kind=jnp.float32), shape(head + SPREAD, total_positions, kind=jnp.float32))

time: 62.5 us -> 61.2 us (0.979)
  the two profiles are of different devices: /device:TPU:48 before, /device:TPU:56 now
where the time goes in v3:
time: 61.2 us; the launch traced here: 60.7 us
  waiting for transfers between devices  21.6 us (35%)
  starting transfers between devices  18.5 us (30%)
  Pallas kernels  9.83 us (16%)
  blocking collectives  9.67 us (16%)
  local copies, waits for them, and re-layouts  0.94 us (2%)
    pallas_call x9, Pallas kernels, call(): pl.pallas_call(kernel, out_shape=shapes, in_specs=[pl.BlockSpec(memory_sp...  9.83 us
    ppermute x1, waiting for transfers between devices, body(): prior = lax.ppermute(own, 'frame', [(i, i + 1) for i in range(frames - 1)])  9.7 us
    all_to_all x1, blocking collectives, body(): back = lax.all_to_all(attended, 'row', 0, 0, tiled=True)  9.67 us
    ppermute x9, starting transfers between devices, send(): lax.ppermute(array, 'frame', pairs_of(*permute))  6.78 us
    all_to_all x1, waiting for transfers between devices, body(): first = lax.all_to_all(theirs, 'row', 0, 0, tiled=True)  5.75 us
    all_to_all x1, starting transfers between devices, body(): rows = lax.all_to_all(mine, 'row', 0, 0, tiled=True)  5.4 us
    ppermute x9, waiting for transfers between devices, send(): lax.ppermute(array, 'frame', pairs_of(*permute))  4.79 us
    all_to_all x1, starting transfers between devices, body(): first = lax.all_to_all(theirs, 'row', 0, 0, tiled=True)  4.35 us
  transfers between devices with their start and end apart: 12, of which 4 were waited for; matrix products, arithmetic and copies ran while one was open for 0% of the time, Pallas kernels for 12%

profile of v3, /device:TPU:56, one launch (start us, length us, event | category | flops | bytes accessed | tf_op | source)
XLA Modules:
  0.0 60.7 jit_solution(3038343134215367600)
XLA Ops:
  0.0 0.7 %collective-permute-start.1 = (bf16[128,640]{1,0:T(8,128)(2,1)}, bf16[128,640]{1,0:T(8,128)(2,1)S(1)}, u32[]{:S(2)}, u32[]{:S(2)}) collective-permute-start(bf16[128,640]{1,0:T(8,128)(2,1)} %bitcast.3), channel_id=1, source_target_pairs={{0,256},{1,257},{2,258},{3,259},{4,260},{5,261},{6,262},{7,263}} | collective-permute-start | bytes 491528 | tf_op jit(solution)/shard_map/ppermute | solution.py:211
  0.7 0.7 %collective-permute-start.2 = (bf16[128,640]{1,0:T(8,128)(2,1)}, bf16[128,640]{1,0:T(8,128)(2,1)S(1)}, u32[]{:S(2)}, u32[]{:S(2)}) collective-permute-start(bf16[128,640]{1,0:T(8,128)(2,1)} %bitcast.4), channel_id=1, source_target_pairs={{0,128},{1,129},{2,130},{3,131},{4,132},{5,133},{6,134},{7,135}} | collective-permute-start | bytes 491528 | tf_op jit(solution)/shard_map/ppermute | solution.py:211
  1.3 0.7 %collective-permute-start.3 = (bf16[128,640]{1,0:T(8,128)(2,1)}, bf16[128,640]{1,0:T(8,128)(2,1)S(1)}, u32[]{:S(2)}, u32[]{:S(2)}) collective-permute-start(bf16[128,640]{1,0:T(8,128)(2,1)} %bitcast.5), channel_id=1, source_target_pairs={{0,384},{1,385},{2,386},{3,387},{4,388},{5,389},{6,390},{7,391}} | collective-permute-start | bytes 491528 | tf_op jit(solution)/shard_map/ppermute | solution.py:211
  2.0 1.9 %collective-permute-start = (bf16[128,640]{1,0:T(8,128)(2,1)}, bf16[128,640]{1,0:T(8,128)(2,1)S(1)}, u32[]{:S(2)}, u32[]{:S(2)}) collective-permute-start(bf16[128,640]{1,0:T(8,128)(2,1)} %bitcast.6), channel_id=1, source_target_pairs={{0,8},{8,16},{16,24},{24,32},{32,40},{40,48},{48,56},{56,64},{64,7... | collective-permute-start | bytes 491528 | tf_op jit(solution)/shard_map/ppermute | solution.py:214
  4.0 0.9 %copy-done.5 = bf16[1,128,640]{2,1,0:T(8,128)(2,1)S(1)} copy-done((bf16[1,128,640]{2,1,0:T(8,128)(2,1)S(1)}, bf16[1,128,640]{2,1,0:T(8,128)(2,1)}, u32[]{:S(2)}) %copy-start.5) | copy-done | bytes 163864
  5.2 0.8 %collective-permute-start.4 = (bf16[128,640]{1,0:T(8,128)(2,1)S(1)}, bf16[128,640]{1,0:T(8,128)(2,1)S(1)}, u32[]{:S(2)}, u32[]{:S(2)}) collective-permute-start(bf16[128,640]{1,0:T(8,128)(2,1)S(1)} %pick_a.1.after.held), channel_id=1, source_target_pairs={{0,16},{128,144},{256,272},{384,400},{1,17},{129,145},{257,273},{3... | collective-permute-start | bytes 491528 | tf_op jit(solution)/shard_map/ppermute | solution.py:211
  6.0 0.7 %collective-permute-start.5 = (bf16[128,640]{1,0:T(8,128)(2,1)S(1)}, bf16[128,640]{1,0:T(8,128)(2,1)S(1)}, u32[]{:S(2)}, u32[]{:S(2)}) collective-permute-start(bf16[128,640]{1,0:T(8,128)(2,1)S(1)} %pick_a.1.after.held), channel_id=1, source_target_pairs={{0,32},{128,160},{256,288},{384,416},{1,33},{129,161},{257,289},{3... | collective-permute-start | bytes 491528 | tf_op jit(solution)/shard_map/ppermute | solution.py:211
  6.7 0.7 %collective-permute-start.6 = (bf16[128,640]{1,0:T(8,128)(2,1)S(1)}, bf16[128,640]{1,0:T(8,128)(2,1)S(1)}, u32[]{:S(2)}, u32[]{:S(2)}) collective-permute-start(bf16[128,640]{1,0:T(8,128)(2,1)S(1)} %pick_a.1.after.held), channel_id=1, source_target_pairs={{0,48},{128,176},{256,304},{384,432},{1,49},{129,177},{257,305},{3... | collective-permute-start | bytes 491528 | tf_op jit(solution)/shard_map/ppermute | solution.py:211
  7.4 0.8 %own_rows.1.mine = bf16[8,240,128]{2,1,0:T(8,128)(2,1)S(1)} custom-call(bf16[128,640]{1,0:T(8,128)(2,1)S(1)} %stage.1.own.held.latents, f32[640]{0:T(1024)S(1)} %copy-done.4, bf16[640,640]{1,0:T(8,128)(2,1)S(1)} %copy-done.2, bf16[640,640]{1,0:T(8,128)(2,1)S(1)} %copy-done, bf16[640,640]{1,0:T(8,128)(2,1)S(1)} %copy-done.1), custom_call_target="tpu_custom_call" | custom-call | flops 314572800 | bytes 2457600 | tf_op jit(solution)/shard_map/own_rows/pallas_call | solution.py:187
  8.3 9.7 %collective-permute-done.prior = bf16[128,640]{1,0:T(8,128)(2,1)S(1)} collective-permute-done((bf16[128,640]{1,0:T(8,128)(2,1)}, bf16[128,640]{1,0:T(8,128)(2,1)S(1)}, u32[]{:S(2)}, u32[]{:S(2)}) %collective-permute-start) | collective-permute-done | bytes 163872 | tf_op jit(solution)/shard_map/ppermute | solution.py:214
  18.0 1.4 %prior_rows.1 = bf16[8,400,128]{2,1,0:T(8,128)(2,1)} custom-call(s32[1]{0:T(128)} %bitcast.frame, bf16[8,240,128]{2,1,0:T(8,128)(2,1)S(1)} %own_rows.1.mine, bf16[128,640]{1,0:T(8,128)(2,1)S(1)} %stage.1.own.held.latents, bf16[128,640]{1,0:T(8,128)(2,1)S(1)} %collective-permute-done.prior, f32[640]{0:T(1024)S(1)} %copy-done.4, bf16[640,640]{1,0:T(8,128)(2,1)S(1)} %copy-done, ...), custom_call_target="tpu_custom_call" | custom-call | flops 209715200 | bytes 1638400 | tf_op jit(solution)/shard_map/prior_rows/pallas_call | solution.py:187
  19.4 5.4 %all-to-all-start = ((bf16[8,400,128]{2,1,0:T(8,128)(2,1)}), bf16[8,400,128]{2,1,0:T(8,128)(2,1)S(1)}, u32[]{:S(2)}, u32[]{:S(2)}) async-start(bf16[8,400,128]{2,1,0:T(8,128)(2,1)} %prior_rows.1), calls=%async_computation | async-start | bytes 1638400 | tf_op jit(solution)/shard_map/all_to_all | solution.py:238
  24.8 1.3 %collective-permute-start.7 = (bf16[128,640]{1,0:T(8,128)(2,1)S(1)}, bf16[128,640]{1,0:T(8,128)(2,1)S(1)}, u32[]{:S(2)}, u32[]{:S(2)}) collective-permute-start(bf16[128,640]{1,0:T(8,128)(2,1)S(1)} %pick_b.1.held), channel_id=1, source_target_pairs={{0,64},{16,80},{32,96},{48,112},{128,192},{144,208},{160,224},{176... | collective-permute-start | bytes 491528 | tf_op jit(solution)/shard_map/ppermute | solution.py:211
  26.1 0.7 %collective-permute-start.8 = (bf16[128,640]{1,0:T(8,128)(2,1)S(1)}, bf16[128,640]{1,0:T(8,128)(2,1)S(1)}, u32[]{:S(2)}, u32[]{:S(2)}) collective-permute-start(bf16[128,640]{1,0:T(8,128)(2,1)S(1)} %pick_b.1.held), channel_id=1, source_target_pairs={{0,72},{16,88},{32,104},{48,120},{128,200},{144,216},{160,232},{17... | collective-permute-start | bytes 491528 | tf_op jit(solution)/shard_map/ppermute | solution.py:211
  26.8 0.7 %collective-permute-start.9 = (bf16[128,640]{1,0:T(8,128)(2,1)S(1)}, bf16[128,640]{1,0:T(8,128)(2,1)S(1)}, u32[]{:S(2)}, u32[]{:S(2)}) collective-permute-start(bf16[128,640]{1,0:T(8,128)(2,1)S(1)} %pick_b.1.held), channel_id=1, source_target_pairs={{0,8},{16,24},{32,40},{48,56},{128,136},{144,152},{160,168},{176,1... | collective-permute-start | bytes 491528 | tf_op jit(solution)/shard_map/ppermute | solution.py:211
  27.5 4.8 %collective-permute-done.7.rest_0_ = bf16[128,640]{1,0:T(8,128)(2,1)S(1)} collective-permute-done((bf16[128,640]{1,0:T(8,128)(2,1)S(1)}, bf16[128,640]{1,0:T(8,128)(2,1)S(1)}, u32[]{:S(2)}, u32[]{:S(2)}) %collective-permute-start.7) | collective-permute-done | bytes 163872 | tf_op jit(solution)/shard_map/ppermute | solution.py:211
  32.3 1.4 %first_rows.1 = bf16[8,160,128]{2,1,0:T(8,128)(2,1)} custom-call(s32[1]{0:T(128)} %bitcast.frame, bf16[128,640]{1,0:T(8,128)(2,1)S(1)} %pick_b.1.held, bf16[128,640]{1,0:T(8,128)(2,1)S(1)} %collective-permute-done.7.rest_0_, bf16[128,640]{1,0:T(8,128)(2,1)S(1)} %collective-permute-done.8.rest_1_, bf16[128,640]{1,0:T(8,128)(2,1)S(1)} %collective-permute-done.9.rest_2_, ...), custom_call_target="tpu_custom_call" | custom-call | flops 209715200 | bytes 1638400 | tf_op jit(solution)/shard_map/first_rows/pallas_call | solution.py:187
  33.7 1.3 %all-to-all-done.rows = bf16[8,400,128]{2,1,0:T(8,128)(2,1)S(1)} async-done(((bf16[8,400,128]{2,1,0:T(8,128)(2,1)}), bf16[8,400,128]{2,1,0:T(8,128)(2,1)S(1)}, u32[]{:S(2)}, u32[]{:S(2)}) %all-to-all-start) | async-done | bytes 819232 | tf_op jit(solution)/shard_map/all_to_all | solution.py:238
  35.1 4.3 %all-to-all-start.1 = ((bf16[8,160,128]{2,1,0:T(8,128)(2,1)}), bf16[8,160,128]{2,1,0:T(8,128)(2,1)S(1)}, u32[]{:S(2)}, u32[]{:S(2)}) async-start(bf16[8,160,128]{2,1,0:T(8,128)(2,1)} %first_rows.1), calls=%async_computation.1 | async-start | bytes 655360 | tf_op jit(solution)/shard_map/all_to_all | solution.py:250
  39.4 3.3 %near.1 = (f32[8,1024]{1,0:T(8,128)S(1)}, f32[96,1024]{1,0:T(8,128)S(1)}, bf16[80,1024]{1,0:T(8,128)(2,1)S(1)}) custom-call(bf16[8,400,128]{2,1,0:T(8,128)(2,1)S(1)} %all-to-all-done.rows), custom_call_target="tpu_custom_call" | custom-call | flops 671088640 | bytes 819200 | tf_op jit(solution)/shard_map/near/pallas_call | solution.py:187
  42.7 5.8 %all-to-all-done.1.first = bf16[8,160,128]{2,1,0:T(8,128)(2,1)S(1)} async-done(((bf16[8,160,128]{2,1,0:T(8,128)(2,1)}), bf16[8,160,128]{2,1,0:T(8,128)(2,1)S(1)}, u32[]{:S(2)}, u32[]{:S(2)}) %all-to-all-start.1) | async-done | bytes 327712 | tf_op jit(solution)/shard_map/all_to_all | solution.py:250
  48.5 1.6 %far.1 = bf16[8,80,128]{2,1,0:T(8,128)(2,1)S(1)} custom-call(bf16[80,1024]{1,0:T(8,128)(2,1)S(1)} %get-tuple-element.8.queries, bf16[8,160,128]{2,1,0:T(8,128)(2,1)S(1)} %all-to-all-done.1.first, f32[8,1024]{1,0:T(8,128)S(1)} %get-tuple-element.9.peak, f32[96,1024]{1,0:T(8,128)S(1)} %get-tuple-element.10.total), custom_call_target="tpu_custom_call" | custom-call | flops 335544320 | bytes 327680 | tf_op jit(solution)/shard_map/far/pallas_call | solution.py:187
  50.1 9.7 %all_to_all.15.attended = bf16[8,80,128]{2,1,0:T(8,128)(2,1)S(1)} all-to-all(bf16[8,80,128]{2,1,0:T(8,128)(2,1)S(1)} %far.1), channel_id=1, replica_groups=mesh['frame'=64,'row'=8] {'row'}, dimensions={0} | all-to-all | bytes 327680 | tf_op jit(solution)/shard_map/all_to_all | solution.py:255
  59.7 1.0 %mix.1 = bf16[128,640]{1,0:T(8,128)(2,1)} custom-call(bf16[8,80,128]{2,1,0:T(8,128)(2,1)S(1)} %all_to_all.15.attended, bf16[128,640]{1,0:T(8,128)(2,1)S(1)} %stage.1.own.held.latents, bf16[640,640]{1,0:T(8,128)(2,1)S(1)} %copy-done.3), custom_call_target="tpu_custom_call" | custom-call | flops 104857600 | bytes 819200 | tf_op jit(solution)/shard_map/mix/pallas_call | solution.py:187
  (22 shorter events, 0.3 us)
Async XLA Ops:
  0.0 5.1 %collective-permute-start.1 = (bf16[128,640]{1,0:T(8,128)(2,1)}, bf16[128,640]{1,0:T(8,128)(2,1)S(1)}, u32[]{:S(2)}, u32[]{:S(2)}) collective-permute-start(bf16[128,640]{1,0:T(8,128)(2,1)} %bitcast.3), channel_id=1, source_target_pairs={{0,256},{1,257},{2,258},{3,259},{4,260},{5,261},{6,262},{7,263}} | collective-permute-start | bytes 491528 | tf_op jit(solution)/shard_map/ppermute | solution.py:211
  0.7 4.4 %collective-permute-start.2 = (bf16[128,640]{1,0:T(8,128)(2,1)}, bf16[128,640]{1,0:T(8,128)(2,1)S(1)}, u32[]{:S(2)}, u32[]{:S(2)}) collective-permute-start(bf16[128,640]{1,0:T(8,128)(2,1)} %bitcast.4), channel_id=1, source_target_pairs={{0,128},{1,129},{2,130},{3,131},{4,132},{5,133},{6,134},{7,135}} | collective-permute-start | bytes 491528 | tf_op jit(solution)/shard_map/ppermute | solution.py:211
  1.3 3.7 %collective-permute-start.3 = (bf16[128,640]{1,0:T(8,128)(2,1)}, bf16[128,640]{1,0:T(8,128)(2,1)S(1)}, u32[]{:S(2)}, u32[]{:S(2)}) collective-permute-start(bf16[128,640]{1,0:T(8,128)(2,1)} %bitcast.5), channel_id=1, source_target_pairs={{0,384},{1,385},{2,386},{3,387},{4,388},{5,389},{6,390},{7,391}} | collective-permute-start | bytes 491528 | tf_op jit(solution)/shard_map/ppermute | solution.py:211
  2.0 15.9 %collective-permute-start = (bf16[128,640]{1,0:T(8,128)(2,1)}, bf16[128,640]{1,0:T(8,128)(2,1)S(1)}, u32[]{:S(2)}, u32[]{:S(2)}) collective-permute-start(bf16[128,640]{1,0:T(8,128)(2,1)} %bitcast.6), channel_id=1, source_target_pairs={{0,8},{8,16},{16,24},{24,32},{32,40},{40,48},{48,56},{56,64},{64,7... | collective-permute-start | bytes 491528 | tf_op jit(solution)/shard_map/ppermute | solution.py:214
  4.0 0.9 %copy-start.5 = (bf16[1,128,640]{2,1,0:T(8,128)(2,1)S(1)}, bf16[1,128,640]{2,1,0:T(8,128)(2,1)}, u32[]{:S(2)}) copy-start(bf16[1,128,640]{2,1,0:T(8,128)(2,1)} %param.6) | copy-start | bytes 491524
  5.1 2.3 %copy-start = (bf16[640,640]{1,0:T(8,128)(2,1)S(1)}, bf16[640,640]{1,0:T(8,128)(2,1)}, u32[]{:S(2)}) copy-start(bf16[640,640]{1,0:T(8,128)(2,1)} %rest_4_.1) | copy-start | bytes 2457604
  5.1 2.3 %copy-start.1 = (bf16[640,640]{1,0:T(8,128)(2,1)S(1)}, bf16[640,640]{1,0:T(8,128)(2,1)}, u32[]{:S(2)}) copy-start(bf16[640,640]{1,0:T(8,128)(2,1)} %rest_5_.1) | copy-start | bytes 2457604
  5.1 2.3 %copy-start.2 = (bf16[640,640]{1,0:T(8,128)(2,1)S(1)}, bf16[640,640]{1,0:T(8,128)(2,1)}, u32[]{:S(2)}) copy-start(bf16[640,640]{1,0:T(8,128)(2,1)} %w_query.1) | copy-start | bytes 2457604
  5.1 2.3 %copy-start.4 = (f32[640]{0:T(1024)S(1)}, f32[640]{0:T(1024)}, u32[]{:S(2)}) copy-start(f32[640]{0:T(1024)} %rest_3_.1) | copy-start | bytes 7684
  5.2 19.6 %collective-permute-start.4 = (bf16[128,640]{1,0:T(8,128)(2,1)S(1)}, bf16[128,640]{1,0:T(8,128)(2,1)S(1)}, u32[]{:S(2)}, u32[]{:S(2)}) collective-permute-start(bf16[128,640]{1,0:T(8,128)(2,1)S(1)} %pick_a.1.after.held), channel_id=1, source_target_pairs={{0,16},{128,144},{256,272},{384,400},{1,17},{129,145},{257,273},{3... | collective-permute-start | bytes 491528 | tf_op jit(solution)/shard_map/ppermute | solution.py:211
  6.0 18.8 %collective-permute-start.5 = (bf16[128,640]{1,0:T(8,128)(2,1)S(1)}, bf16[128,640]{1,0:T(8,128)(2,1)S(1)}, u32[]{:S(2)}, u32[]{:S(2)}) collective-permute-start(bf16[128,640]{1,0:T(8,128)(2,1)S(1)} %pick_a.1.after.held), channel_id=1, source_target_pairs={{0,32},{128,160},{256,288},{384,416},{1,33},{129,161},{257,289},{3... | collective-permute-start | bytes 491528 | tf_op jit(solution)/shard_map/ppermute | solution.py:211
  6.7 18.1 %collective-permute-start.6 = (bf16[128,640]{1,0:T(8,128)(2,1)S(1)}, bf16[128,640]{1,0:T(8,128)(2,1)S(1)}, u32[]{:S(2)}, u32[]{:S(2)}) collective-permute-start(bf16[128,640]{1,0:T(8,128)(2,1)S(1)} %pick_a.1.after.held), channel_id=1, source_target_pairs={{0,48},{128,176},{256,304},{384,432},{1,49},{129,177},{257,305},{3... | collective-permute-start | bytes 491528 | tf_op jit(solution)/shard_map/ppermute | solution.py:211
  19.4 15.7 %all-to-all-start = ((bf16[8,400,128]{2,1,0:T(8,128)(2,1)}), bf16[8,400,128]{2,1,0:T(8,128)(2,1)S(1)}, u32[]{:S(2)}, u32[]{:S(2)}) async-start(bf16[8,400,128]{2,1,0:T(8,128)(2,1)} %prior_rows.1), calls=%async_computation | async-start | bytes 1638400 | tf_op jit(solution)/shard_map/all_to_all | solution.py:238
  24.8 7.4 %collective-permute-start.7 = (bf16[128,640]{1,0:T(8,128)(2,1)S(1)}, bf16[128,640]{1,0:T(8,128)(2,1)S(1)}, u32[]{:S(2)}, u32[]{:S(2)}) collective-permute-start(bf16[128,640]{1,0:T(8,128)(2,1)S(1)} %pick_b.1.held), channel_id=1, source_target_pairs={{0,64},{16,80},{32,96},{48,112},{128,192},{144,208},{160,224},{176... | collective-permute-start | bytes 491528 | tf_op jit(solution)/shard_map/ppermute | solution.py:211
  26.1 6.1 %collective-permute-start.8 = (bf16[128,640]{1,0:T(8,128)(2,1)S(1)}, bf16[128,640]{1,0:T(8,128)(2,1)S(1)}, u32[]{:S(2)}, u32[]{:S(2)}) collective-permute-start(bf16[128,640]{1,0:T(8,128)(2,1)S(1)} %pick_b.1.held), channel_id=1, source_target_pairs={{0,72},{16,88},{32,104},{48,120},{128,200},{144,216},{160,232},{17... | collective-permute-start | bytes 491528 | tf_op jit(solution)/shard_map/ppermute | solution.py:211
  26.8 5.5 %collective-permute-start.9 = (bf16[128,640]{1,0:T(8,128)(2,1)S(1)}, bf16[128,640]{1,0:T(8,128)(2,1)S(1)}, u32[]{:S(2)}, u32[]{:S(2)}) collective-permute-start(bf16[128,640]{1,0:T(8,128)(2,1)S(1)} %pick_b.1.held), channel_id=1, source_target_pairs={{0,8},{16,24},{32,40},{48,56},{128,136},{144,152},{160,168},{176,1... | collective-permute-start | bytes 491528 | tf_op jit(solution)/shard_map/ppermute | solution.py:211
  35.1 13.4 %all-to-all-start.1 = ((bf16[8,160,128]{2,1,0:T(8,128)(2,1)}), bf16[8,160,128]{2,1,0:T(8,128)(2,1)S(1)}, u32[]{:S(2)}, u32[]{:S(2)}) async-start(bf16[8,160,128]{2,1,0:T(8,128)(2,1)} %first_rows.1), calls=%async_computation.1 | async-start | bytes 655360 | tf_op jit(solution)/shard_map/all_to_all | solution.py:250
  42.7 17.0 %copy-start.3 = (bf16[640,640]{1,0:T(8,128)(2,1)S(1)}, bf16[640,640]{1,0:T(8,128)(2,1)}, u32[]{:S(2)}) copy-start(bf16[640,640]{1,0:T(8,128)(2,1)} %w_out.1) | copy-start | bytes 2457604

commit v4 on v3

--- a/solution.py
+++ b/solution.py
@@ -30,10 +30,14 @@
     return (y % 2 == 0) & (core == 0)
 
 
+def upper(y, z, core):
+    return even(y, z, core) & (z != 0)
+
+
 ROUNDS = (
-    ((root, (4, 0, 0)), (root, (2, 0, 0)), (root, (6, 0, 0))),
-    ((lead, (0, 1, 0)), (lead, (0, 2, 0)), (lead, (0, 3, 0))),
-    ((even, (1, 0, 0)), (even, (1, 0, 1)), (even, (0, 0, 1))),
+    ((root, (2, 0, 0)), (root, (4, 0, 0)), (root, (6, 0, 0))),
+    ((lead, (1, 0, 0)), (lead, (0, 1, 0)), (lead, (0, 2, 0)), (lead, (0, 3, 0))),
+    ((upper, (1, 0, 0)), (even, (1, 0, 1)), (even, (0, 0, 1))),
 )
 
 
@@ -220,7 +224,7 @@
     arrived = send(held_a, 1)
     held_b = call(
         functools.partial(pick_kernel, 1), "pick_b", shape(positions, channels),
-        (at, held_a, *arrived), "svvvv", flops=COST_B,
+        (at, held_a, *arrived), "svvvvv", flops=COST_B,
     )
     arrived = send(held_b, 2)
 

time: 61.2 us -> 60.7 us (level)
  the two profiles are of different devices: /device:TPU:56 before, /device:TPU:48 now
where the time goes in v4:
time: 60.7 us; the launch traced here: 60.2 us
  starting transfers between devices  22.7 us (37%)
  waiting for transfers between devices  17.1 us (28%)
  Pallas kernels  9.85 us (16%)
  blocking collectives  9.34 us (15%)
  local copies, waits for them, and re-layouts  0.93 us (2%)
    ppermute x10, starting transfers between devices, send(): lax.ppermute(array, 'frame', pairs_of(*permute))  11.6 us
    pallas_call x9, Pallas kernels, call(): pl.pallas_call(kernel, out_shape=shapes, in_specs=[pl.BlockSpec(memory_sp...  9.85 us
    all_to_all x1, blocking collectives, body(): back = lax.all_to_all(attended, 'row', 0, 0, tiled=True)  9.34 us
    ppermute x10, waiting for transfers between devices, send(): lax.ppermute(array, 'frame', pairs_of(*permute))  8.89 us
    all_to_all x1, starting transfers between devices, body(): rows = lax.all_to_all(mine, 'row', 0, 0, tiled=True)  5.7 us
    all_to_all x1, waiting for transfers between devices, body(): first = lax.all_to_all(theirs, 'row', 0, 0, tiled=True)  4.25 us
    all_to_all x1, waiting for transfers between devices, body(): rows = lax.all_to_all(mine, 'row', 0, 0, tiled=True)  3.95 us
    all_to_all x1, starting transfers between devices, body(): first = lax.all_to_all(theirs, 'row', 0, 0, tiled=True)  3.43 us
  transfers between devices with their start and end apart: 13, of which 4 were waited for; matrix products, arithmetic and copies ran while one was open for 0% of the time, Pallas kernels for 12%

profile of v4, /device:TPU:48, one launch (start us, length us, event | category | flops | bytes accessed | tf_op | source)
XLA Modules:
  0.0 60.2 jit_solution(14208648370721410629)
XLA Ops:
  0.7 0.7 %collective-permute-start.2 = (bf16[128,640]{1,0:T(8,128)(2,1)}, bf16[128,640]{1,0:T(8,128)(2,1)S(1)}, u32[]{:S(2)}, u32[]{:S(2)}) collective-permute-start(bf16[128,640]{1,0:T(8,128)(2,1)} %bitcast.4), channel_id=1, source_target_pairs={{0,256},{1,257},{2,258},{3,259},{4,260},{5,261},{6,262},{7,263}} | collective-permute-start | bytes 491528 | tf_op jit(solution)/shard_map/ppermute | solution.py:215
  1.3 1.3 %collective-permute-start.3 = (bf16[128,640]{1,0:T(8,128)(2,1)}, bf16[128,640]{1,0:T(8,128)(2,1)S(1)}, u32[]{:S(2)}, u32[]{:S(2)}) collective-permute-start(bf16[128,640]{1,0:T(8,128)(2,1)} %bitcast.5), channel_id=1, source_target_pairs={{0,384},{1,385},{2,386},{3,387},{4,388},{5,389},{6,390},{7,391}} | collective-permute-start | bytes 491528 | tf_op jit(solution)/shard_map/ppermute | solution.py:215
  2.6 1.9 %collective-permute-start = (bf16[128,640]{1,0:T(8,128)(2,1)}, bf16[128,640]{1,0:T(8,128)(2,1)S(1)}, u32[]{:S(2)}, u32[]{:S(2)}) collective-permute-start(bf16[128,640]{1,0:T(8,128)(2,1)} %bitcast.6), channel_id=1, source_target_pairs={{0,8},{8,16},{16,24},{24,32},{32,40},{40,48},{48,56},{56,64},{64,7... | collective-permute-start | bytes 491528 | tf_op jit(solution)/shard_map/ppermute | solution.py:218
  4.6 0.9 %copy-done.5 = bf16[1,128,640]{2,1,0:T(8,128)(2,1)S(1)} copy-done((bf16[1,128,640]{2,1,0:T(8,128)(2,1)S(1)}, bf16[1,128,640]{2,1,0:T(8,128)(2,1)}, u32[]{:S(2)}) %copy-start.5) | copy-done | bytes 163864
  5.7 7.4 %collective-permute-done.3.rest_2_ = bf16[128,640]{1,0:T(8,128)(2,1)S(1)} collective-permute-done((bf16[128,640]{1,0:T(8,128)(2,1)}, bf16[128,640]{1,0:T(8,128)(2,1)S(1)}, u32[]{:S(2)}, u32[]{:S(2)}) %collective-permute-start.3) | collective-permute-done | bytes 163872 | tf_op jit(solution)/shard_map/ppermute | solution.py:215
  13.1 1.4 %collective-permute-start.4 = (bf16[128,640]{1,0:T(8,128)(2,1)S(1)}, bf16[128,640]{1,0:T(8,128)(2,1)S(1)}, u32[]{:S(2)}, u32[]{:S(2)}) collective-permute-start(bf16[128,640]{1,0:T(8,128)(2,1)S(1)} %pick_a.1.after.held), channel_id=1, source_target_pairs={{0,64},{128,192},{256,320},{384,448},{1,65},{129,193},{257,321},{3... | collective-permute-start | bytes 491528 | tf_op jit(solution)/shard_map/ppermute | solution.py:215
  14.6 1.3 %collective-permute-start.5 = (bf16[128,640]{1,0:T(8,128)(2,1)S(1)}, bf16[128,640]{1,0:T(8,128)(2,1)S(1)}, u32[]{:S(2)}, u32[]{:S(2)}) collective-permute-start(bf16[128,640]{1,0:T(8,128)(2,1)S(1)} %pick_a.1.after.held), channel_id=1, source_target_pairs={{0,16},{128,144},{256,272},{384,400},{1,17},{129,145},{257,273},{3... | collective-permute-start | bytes 491528 | tf_op jit(solution)/shard_map/ppermute | solution.py:215
  15.9 1.7 %collective-permute-start.6 = (bf16[128,640]{1,0:T(8,128)(2,1)S(1)}, bf16[128,640]{1,0:T(8,128)(2,1)S(1)}, u32[]{:S(2)}, u32[]{:S(2)}) collective-permute-start(bf16[128,640]{1,0:T(8,128)(2,1)S(1)} %pick_a.1.after.held), channel_id=1, source_target_pairs={{0,32},{128,160},{256,288},{384,416},{1,33},{129,161},{257,289},{3... | collective-permute-start | bytes 491528 | tf_op jit(solution)/shard_map/ppermute | solution.py:215
  17.6 1.3 %collective-permute-start.7 = (bf16[128,640]{1,0:T(8,128)(2,1)S(1)}, bf16[128,640]{1,0:T(8,128)(2,1)S(1)}, u32[]{:S(2)}, u32[]{:S(2)}) collective-permute-start(bf16[128,640]{1,0:T(8,128)(2,1)S(1)} %pick_a.1.after.held), channel_id=1, source_target_pairs={{0,48},{128,176},{256,304},{384,432},{1,49},{129,177},{257,305},{3... | collective-permute-start | bytes 491528 | tf_op jit(solution)/shard_map/ppermute | solution.py:215
  19.0 0.9 %own_rows.1.mine = bf16[8,240,128]{2,1,0:T(8,128)(2,1)S(1)} custom-call(bf16[128,640]{1,0:T(8,128)(2,1)S(1)} %stage.1.own.held.latents, f32[640]{0:T(1024)S(1)} %copy-done.4, bf16[640,640]{1,0:T(8,128)(2,1)S(1)} %copy-done.2, bf16[640,640]{1,0:T(8,128)(2,1)S(1)} %copy-done, bf16[640,640]{1,0:T(8,128)(2,1)S(1)} %copy-done.1), custom_call_target="tpu_custom_call" | custom-call | flops 314572800 | bytes 2457600 | tf_op jit(solution)/shard_map/own_rows/pallas_call | solution.py:191
  19.8 1.4 %prior_rows.1 = bf16[8,400,128]{2,1,0:T(8,128)(2,1)} custom-call(s32[1]{0:T(128)} %bitcast.frame, bf16[8,240,128]{2,1,0:T(8,128)(2,1)S(1)} %own_rows.1.mine, bf16[128,640]{1,0:T(8,128)(2,1)S(1)} %stage.1.own.held.latents, bf16[128,640]{1,0:T(8,128)(2,1)S(1)} %collective-permute-done.prior, f32[640]{0:T(1024)S(1)} %copy-done.4, bf16[640,640]{1,0:T(8,128)(2,1)S(1)} %copy-done, ...), custom_call_target="tpu_custom_call" | custom-call | flops 209715200 | bytes 1638400 | tf_op jit(solution)/shard_map/prior_rows/pallas_call | solution.py:191
  21.2 5.7 %all-to-all-start = ((bf16[8,400,128]{2,1,0:T(8,128)(2,1)}), bf16[8,400,128]{2,1,0:T(8,128)(2,1)S(1)}, u32[]{:S(2)}, u32[]{:S(2)}) async-start(bf16[8,400,128]{2,1,0:T(8,128)(2,1)} %prior_rows.1), calls=%async_computation | async-start | bytes 1638400 | tf_op jit(solution)/shard_map/all_to_all | solution.py:242
  27.0 0.7 %collective-permute-start.8 = (bf16[128,640]{1,0:T(8,128)(2,1)S(1)}, bf16[128,640]{1,0:T(8,128)(2,1)S(1)}, u32[]{:S(2)}, u32[]{:S(2)}) collective-permute-start(bf16[128,640]{1,0:T(8,128)(2,1)S(1)} %pick_b.1.held), channel_id=1, source_target_pairs={{16,80},{32,96},{48,112},{144,208},{160,224},{176,240},{272,336},{... | collective-permute-start | bytes 491528 | tf_op jit(solution)/shard_map/ppermute | solution.py:215
  27.7 1.3 %collective-permute-start.9 = (bf16[128,640]{1,0:T(8,128)(2,1)S(1)}, bf16[128,640]{1,0:T(8,128)(2,1)S(1)}, u32[]{:S(2)}, u32[]{:S(2)}) collective-permute-start(bf16[128,640]{1,0:T(8,128)(2,1)S(1)} %pick_b.1.held), channel_id=1, source_target_pairs={{0,72},{16,88},{32,104},{48,120},{128,200},{144,216},{160,232},{17... | collective-permute-start | bytes 491528 | tf_op jit(solution)/shard_map/ppermute | solution.py:215
  29.0 1.3 %collective-permute-start.10 = (bf16[128,640]{1,0:T(8,128)(2,1)S(1)}, bf16[128,640]{1,0:T(8,128)(2,1)S(1)}, u32[]{:S(2)}, u32[]{:S(2)}) collective-permute-start(bf16[128,640]{1,0:T(8,128)(2,1)S(1)} %pick_b.1.held), channel_id=1, source_target_pairs={{0,8},{16,24},{32,40},{48,56},{128,136},{144,152},{160,168},{176,1... | collective-permute-start | bytes 491528 | tf_op jit(solution)/shard_map/ppermute | solution.py:215
  30.3 1.5 %collective-permute-done.9.rest_1_ = bf16[128,640]{1,0:T(8,128)(2,1)S(1)} collective-permute-done((bf16[128,640]{1,0:T(8,128)(2,1)S(1)}, bf16[128,640]{1,0:T(8,128)(2,1)S(1)}, u32[]{:S(2)}, u32[]{:S(2)}) %collective-permute-start.9) | collective-permute-done | bytes 163872 | tf_op jit(solution)/shard_map/ppermute | solution.py:215
  31.8 1.5 %first_rows.1 = bf16[8,160,128]{2,1,0:T(8,128)(2,1)} custom-call(s32[1]{0:T(128)} %bitcast.frame, bf16[128,640]{1,0:T(8,128)(2,1)S(1)} %pick_b.1.held, bf16[128,640]{1,0:T(8,128)(2,1)S(1)} %collective-permute-done.8.rest_0_, bf16[128,640]{1,0:T(8,128)(2,1)S(1)} %collective-permute-done.9.rest_1_, bf16[128,640]{1,0:T(8,128)(2,1)S(1)} %collective-permute-done.10.rest_2_, ...), custom_call_target="tpu_custom_call" | custom-call | flops 209715200 | bytes 1638400 | tf_op jit(solution)/shard_map/first_rows/pallas_call | solution.py:191
  33.3 4.0 %all-to-all-done.rows = bf16[8,400,128]{2,1,0:T(8,128)(2,1)S(1)} async-done(((bf16[8,400,128]{2,1,0:T(8,128)(2,1)}), bf16[8,400,128]{2,1,0:T(8,128)(2,1)S(1)}, u32[]{:S(2)}, u32[]{:S(2)}) %all-to-all-start) | async-done | bytes 819232 | tf_op jit(solution)/shard_map/all_to_all | solution.py:242
  37.2 3.4 %all-to-all-start.1 = ((bf16[8,160,128]{2,1,0:T(8,128)(2,1)}), bf16[8,160,128]{2,1,0:T(8,128)(2,1)S(1)}, u32[]{:S(2)}, u32[]{:S(2)}) async-start(bf16[8,160,128]{2,1,0:T(8,128)(2,1)} %first_rows.1), calls=%async_computation.1 | async-start | bytes 655360 | tf_op jit(solution)/shard_map/all_to_all | solution.py:254
  40.7 3.3 %near.1 = (f32[8,1024]{1,0:T(8,128)S(1)}, f32[96,1024]{1,0:T(8,128)S(1)}, bf16[80,1024]{1,0:T(8,128)(2,1)S(1)}) custom-call(bf16[8,400,128]{2,1,0:T(8,128)(2,1)S(1)} %all-to-all-done.rows), custom_call_target="tpu_custom_call" | custom-call | flops 671088640 | bytes 819200 | tf_op jit(solution)/shard_map/near/pallas_call | solution.py:191
  44.0 4.3 %all-to-all-done.1.first = bf16[8,160,128]{2,1,0:T(8,128)(2,1)S(1)} async-done(((bf16[8,160,128]{2,1,0:T(8,128)(2,1)}), bf16[8,160,128]{2,1,0:T(8,128)(2,1)S(1)}, u32[]{:S(2)}, u32[]{:S(2)}) %all-to-all-start.1) | async-done | bytes 327712 | tf_op jit(solution)/shard_map/all_to_all | solution.py:254
  48.2 1.6 %far.1 = bf16[8,80,128]{2,1,0:T(8,128)(2,1)S(1)} custom-call(bf16[80,1024]{1,0:T(8,128)(2,1)S(1)} %get-tuple-element.8.queries, bf16[8,160,128]{2,1,0:T(8,128)(2,1)S(1)} %all-to-all-done.1.first, f32[8,1024]{1,0:T(8,128)S(1)} %get-tuple-element.9.peak, f32[96,1024]{1,0:T(8,128)S(1)} %get-tuple-element.10.total), custom_call_target="tpu_custom_call" | custom-call | flops 335544320 | bytes 327680 | tf_op jit(solution)/shard_map/far/pallas_call | solution.py:191
  49.8 9.3 %all_to_all.15.attended = bf16[8,80,128]{2,1,0:T(8,128)(2,1)S(1)} all-to-all(bf16[8,80,128]{2,1,0:T(8,128)(2,1)S(1)} %far.1), channel_id=1, replica_groups=mesh['frame'=64,'row'=8] {'row'}, dimensions={0} | all-to-all | bytes 327680 | tf_op jit(solution)/shard_map/all_to_all | solution.py:259
  59.2 1.0 %mix.1 = bf16[128,640]{1,0:T(8,128)(2,1)} custom-call(bf16[8,80,128]{2,1,0:T(8,128)(2,1)S(1)} %all_to_all.15.attended, bf16[128,640]{1,0:T(8,128)(2,1)S(1)} %stage.1.own.held.latents, bf16[640,640]{1,0:T(8,128)(2,1)S(1)} %copy-done.3), custom_call_target="tpu_custom_call" | custom-call | flops 104857600 | bytes 819200 | tf_op jit(solution)/shard_map/mix/pallas_call | solution.py:191
  (24 shorter events, 1.0 us)
Async XLA Ops:
  0.0 5.7 %collective-permute-start.1 = (bf16[128,640]{1,0:T(8,128)(2,1)}, bf16[128,640]{1,0:T(8,128)(2,1)S(1)}, u32[]{:S(2)}, u32[]{:S(2)}) collective-permute-start(bf16[128,640]{1,0:T(8,128)(2,1)} %bitcast.3), channel_id=1, source_target_pairs={{0,128},{1,129},{2,130},{3,131},{4,132},{5,133},{6,134},{7,135}} | collective-permute-start | bytes 491528 | tf_op jit(solution)/shard_map/ppermute | solution.py:215
  0.7 5.0 %collective-permute-start.2 = (bf16[128,640]{1,0:T(8,128)(2,1)}, bf16[128,640]{1,0:T(8,128)(2,1)S(1)}, u32[]{:S(2)}, u32[]{:S(2)}) collective-permute-start(bf16[128,640]{1,0:T(8,128)(2,1)} %bitcast.4), channel_id=1, source_target_pairs={{0,256},{1,257},{2,258},{3,259},{4,260},{5,261},{6,262},{7,263}} | collective-permute-start | bytes 491528 | tf_op jit(solution)/shard_map/ppermute | solution.py:215
  1.3 11.7 %collective-permute-start.3 = (bf16[128,640]{1,0:T(8,128)(2,1)}, bf16[128,640]{1,0:T(8,128)(2,1)S(1)}, u32[]{:S(2)}, u32[]{:S(2)}) collective-permute-start(bf16[128,640]{1,0:T(8,128)(2,1)} %bitcast.5), channel_id=1, source_target_pairs={{0,384},{1,385},{2,386},{3,387},{4,388},{5,389},{6,390},{7,391}} | collective-permute-start | bytes 491528 | tf_op jit(solution)/shard_map/ppermute | solution.py:215
  2.6 17.2 %collective-permute-start = (bf16[128,640]{1,0:T(8,128)(2,1)}, bf16[128,640]{1,0:T(8,128)(2,1)S(1)}, u32[]{:S(2)}, u32[]{:S(2)}) collective-permute-start(bf16[128,640]{1,0:T(8,128)(2,1)} %bitcast.6), channel_id=1, source_target_pairs={{0,8},{8,16},{16,24},{24,32},{32,40},{40,48},{48,56},{56,64},{64,7... | collective-permute-start | bytes 491528 | tf_op jit(solution)/shard_map/ppermute | solution.py:218
  4.6 0.9 %copy-start.5 = (bf16[1,128,640]{2,1,0:T(8,128)(2,1)S(1)}, bf16[1,128,640]{2,1,0:T(8,128)(2,1)}, u32[]{:S(2)}) copy-start(bf16[1,128,640]{2,1,0:T(8,128)(2,1)} %param.6) | copy-start | bytes 491524
  13.1 5.8 %copy-start = (bf16[640,640]{1,0:T(8,128)(2,1)S(1)}, bf16[640,640]{1,0:T(8,128)(2,1)}, u32[]{:S(2)}) copy-start(bf16[640,640]{1,0:T(8,128)(2,1)} %rest_4_.1) | copy-start | bytes 2457604
  13.1 5.9 %copy-start.1 = (bf16[640,640]{1,0:T(8,128)(2,1)S(1)}, bf16[640,640]{1,0:T(8,128)(2,1)}, u32[]{:S(2)}) copy-start(bf16[640,640]{1,0:T(8,128)(2,1)} %rest_5_.1) | copy-start | bytes 2457604
  13.1 5.9 %copy-start.2 = (bf16[640,640]{1,0:T(8,128)(2,1)S(1)}, bf16[640,640]{1,0:T(8,128)(2,1)}, u32[]{:S(2)}) copy-start(bf16[640,640]{1,0:T(8,128)(2,1)} %w_query.1) | copy-start | bytes 2457604
  13.1 5.9 %copy-start.4 = (f32[640]{0:T(1024)S(1)}, f32[640]{0:T(1024)}, u32[]{:S(2)}) copy-start(f32[640]{0:T(1024)} %rest_3_.1) | copy-start | bytes 7684
  13.1 13.8 %collective-permute-start.4 = (bf16[128,640]{1,0:T(8,128)(2,1)S(1)}, bf16[128,640]{1,0:T(8,128)(2,1)S(1)}, u32[]{:S(2)}, u32[]{:S(2)}) collective-permute-start(bf16[128,640]{1,0:T(8,128)(2,1)S(1)} %pick_a.1.after.held), channel_id=1, source_target_pairs={{0,64},{128,192},{256,320},{384,448},{1,65},{129,193},{257,321},{3... | collective-permute-start | bytes 491528 | tf_op jit(solution)/shard_map/ppermute | solution.py:215
  14.6 12.3 %collective-permute-start.5 = (bf16[128,640]{1,0:T(8,128)(2,1)S(1)}, bf16[128,640]{1,0:T(8,128)(2,1)S(1)}, u32[]{:S(2)}, u32[]{:S(2)}) collective-permute-start(bf16[128,640]{1,0:T(8,128)(2,1)S(1)} %pick_a.1.after.held), channel_id=1, source_target_pairs={{0,16},{128,144},{256,272},{384,400},{1,17},{129,145},{257,273},{3... | collective-permute-start | bytes 491528 | tf_op jit(solution)/shard_map/ppermute | solution.py:215
  15.9 11.0 %collective-permute-start.6 = (bf16[128,640]{1,0:T(8,128)(2,1)S(1)}, bf16[128,640]{1,0:T(8,128)(2,1)S(1)}, u32[]{:S(2)}, u32[]{:S(2)}) collective-permute-start(bf16[128,640]{1,0:T(8,128)(2,1)S(1)} %pick_a.1.after.held), channel_id=1, source_target_pairs={{0,32},{128,160},{256,288},{384,416},{1,33},{129,161},{257,289},{3... | collective-permute-start | bytes 491528 | tf_op jit(solution)/shard_map/ppermute | solution.py:215
  17.6 9.3 %collective-permute-start.7 = (bf16[128,640]{1,0:T(8,128)(2,1)S(1)}, bf16[128,640]{1,0:T(8,128)(2,1)S(1)}, u32[]{:S(2)}, u32[]{:S(2)}) collective-permute-start(bf16[128,640]{1,0:T(8,128)(2,1)S(1)} %pick_a.1.after.held), channel_id=1, source_target_pairs={{0,48},{128,176},{256,304},{384,432},{1,49},{129,177},{257,305},{3... | collective-permute-start | bytes 491528 | tf_op jit(solution)/shard_map/ppermute | solution.py:215
  21.2 16.0 %all-to-all-start = ((bf16[8,400,128]{2,1,0:T(8,128)(2,1)}), bf16[8,400,128]{2,1,0:T(8,128)(2,1)S(1)}, u32[]{:S(2)}, u32[]{:S(2)}) async-start(bf16[8,400,128]{2,1,0:T(8,128)(2,1)} %prior_rows.1), calls=%async_computation | async-start | bytes 1638400 | tf_op jit(solution)/shard_map/all_to_all | solution.py:242
  27.0 3.3 %collective-permute-start.8 = (bf16[128,640]{1,0:T(8,128)(2,1)S(1)}, bf16[128,640]{1,0:T(8,128)(2,1)S(1)}, u32[]{:S(2)}, u32[]{:S(2)}) collective-permute-start(bf16[128,640]{1,0:T(8,128)(2,1)S(1)} %pick_b.1.held), channel_id=1, source_target_pairs={{16,80},{32,96},{48,112},{144,208},{160,224},{176,240},{272,336},{... | collective-permute-start | bytes 491528 | tf_op jit(solution)/shard_map/ppermute | solution.py:215
  27.7 4.1 %collective-permute-start.9 = (bf16[128,640]{1,0:T(8,128)(2,1)S(1)}, bf16[128,640]{1,0:T(8,128)(2,1)S(1)}, u32[]{:S(2)}, u32[]{:S(2)}) collective-permute-start(bf16[128,640]{1,0:T(8,128)(2,1)S(1)} %pick_b.1.held), channel_id=1, source_target_pairs={{0,72},{16,88},{32,104},{48,120},{128,200},{144,216},{160,232},{17... | collective-permute-start | bytes 491528 | tf_op jit(solution)/shard_map/ppermute | solution.py:215
  29.0 2.8 %collective-permute-start.10 = (bf16[128,640]{1,0:T(8,128)(2,1)S(1)}, bf16[128,640]{1,0:T(8,128)(2,1)S(1)}, u32[]{:S(2)}, u32[]{:S(2)}) collective-permute-start(bf16[128,640]{1,0:T(8,128)(2,1)S(1)} %pick_b.1.held), channel_id=1, source_target_pairs={{0,8},{16,24},{32,40},{48,56},{128,136},{144,152},{160,168},{176,1... | collective-permute-start | bytes 491528 | tf_op jit(solution)/shard_map/ppermute | solution.py:215
  37.2 11.0 %all-to-all-start.1 = ((bf16[8,160,128]{2,1,0:T(8,128)(2,1)}), bf16[8,160,128]{2,1,0:T(8,128)(2,1)S(1)}, u32[]{:S(2)}, u32[]{:S(2)}) async-start(bf16[8,160,128]{2,1,0:T(8,128)(2,1)} %first_rows.1), calls=%async_computation.1 | async-start | bytes 655360 | tf_op jit(solution)/shard_map/all_to_all | solution.py:254
  44.0 15.2 %copy-start.3 = (bf16[640,640]{1,0:T(8,128)(2,1)S(1)}, bf16[640,640]{1,0:T(8,128)(2,1)}, u32[]{:S(2)}) copy-start(bf16[640,640]{1,0:T(8,128)(2,1)} %w_out.1) | copy-start | bytes 2457604

commit v5 on v4

--- a/solution.py
+++ b/solution.py
@@ -164,17 +164,31 @@
         )
 
 
-def far_kernel(queries, first, peak, total, out):
+FAR = 60.0
+
+
+def far_kernel(queries, first, peak, total, out, sums):
     blocks, _, width = first.shape
     head = queries.shape[0]
     every = range(blocks)
+    key = joined(first, 0, head, every)
     value = jnp.concatenate([joined(first, head, head, every), ones_row(blocks * width)], axis=0)
-    scores = scores_of(joined(first, 0, head, every), queries[...])
     before = peak[:1, :]
-    top = jnp.maximum(jnp.max(scores, axis=0, keepdims=True), before)
-    weights = jnp.exp2(scores - top).astype(jnp.bfloat16)
-    both = total[...] * jnp.exp2(before - top) + jnp.dot(value, weights, preferred_element_type=jnp.float32)
-    attended = (both[:head] / both[head : head + 1]).astype(jnp.bfloat16)
+
+    def weighted(scores, top):
+        weights = jnp.exp2(scores - top).astype(jnp.bfloat16)
+        return jnp.dot(value, weights, preferred_element_type=jnp.float32)
+
+    scores = scores_of(key, queries[...])
+    top = jnp.max(scores, axis=0, keepdims=True)
+    sums[...] = total[...] + weighted(scores, before)
+
+    @pl.when(jnp.max(top - before) > FAR)
+    def _():
+        both = jnp.maximum(top, before)
+        sums[...] = total[...] * jnp.exp2(before - both) + weighted(scores_of(key, queries[...]), both)
+
+    attended = (sums[:head, :] * (1.0 / sums[head : head + 1, :])).astype(jnp.bfloat16)
     for b in every:
         out[b] = attended[:, b * width : (b + 1) * width]
 
@@ -254,6 +268,7 @@
     first = lax.all_to_all(theirs, "row", 0, 0, tiled=True)
     attended = call(
         far_kernel, "far", shape(HEADS, head, positions), (queries, first, peak, total), "vvvv",
+        scratch=[pltpu.VMEM((head + SPREAD, total_positions), jnp.float32)],
         flops=4 * head * total_positions * total_positions, moved=2 * 8 * 2 * head * positions,
     )
     back = lax.all_to_all(attended, "row", 0, 0, tiled=True)

time: 60.7 us -> 60.2 us (level)
  no operation moved by 1% of the time
where the time goes in v5:
time: 60.2 us; the launch traced here: 59.7 us
  starting transfers between devices  22.7 us (38%)
  waiting for transfers between devices  17.1 us (28%)
  Pallas kernels  9.41 us (16%)
  blocking collectives  9.33 us (15%)
  local copies, waits for them, and re-layouts  0.93 us (2%)
    ppermute x10, starting transfers between devices, send(): lax.ppermute(array, 'frame', pairs_of(*permute))  11.6 us
    pallas_call x9, Pallas kernels, call(): pl.pallas_call(kernel, out_shape=shapes, in_specs=[pl.BlockSpec(memory_sp...  9.41 us
    all_to_all x1, blocking collectives, body(): back = lax.all_to_all(attended, 'row', 0, 0, tiled=True)  9.33 us
    ppermute x10, waiting for transfers between devices, send(): lax.ppermute(array, 'frame', pairs_of(*permute))  8.89 us
    all_to_all x1, starting transfers between devices, body(): rows = lax.all_to_all(mine, 'row', 0, 0, tiled=True)  5.7 us
    all_to_all x1, waiting for transfers between devices, body(): first = lax.all_to_all(theirs, 'row', 0, 0, tiled=True)  4.25 us
    all_to_all x1, waiting for transfers between devices, body(): rows = lax.all_to_all(mine, 'row', 0, 0, tiled=True)  3.95 us
    all_to_all x1, starting transfers between devices, body(): first = lax.all_to_all(theirs, 'row', 0, 0, tiled=True)  3.43 us
  transfers between devices with their start and end apart: 13, of which 4 were waited for; matrix products, arithmetic and copies ran while one was open for 0% of the time, Pallas kernels for 12%

profile of v5, /device:TPU:48, one launch (start us, length us, event | category | flops | bytes accessed | tf_op | source)
XLA Modules:
  0.0 59.7 jit_solution(17505527926566365816)
XLA Ops:
  0.7 0.7 %collective-permute-start.2 = (bf16[128,640]{1,0:T(8,128)(2,1)}, bf16[128,640]{1,0:T(8,128)(2,1)S(1)}, u32[]{:S(2)}, u32[]{:S(2)}) collective-permute-start(bf16[128,640]{1,0:T(8,128)(2,1)} %bitcast.4), channel_id=1, source_target_pairs={{0,256},{1,257},{2,258},{3,259},{4,260},{5,261},{6,262},{7,263}} | collective-permute-start | bytes 491528 | tf_op jit(solution)/shard_map/ppermute | solution.py:229
  1.3 1.3 %collective-permute-start.3 = (bf16[128,640]{1,0:T(8,128)(2,1)}, bf16[128,640]{1,0:T(8,128)(2,1)S(1)}, u32[]{:S(2)}, u32[]{:S(2)}) collective-permute-start(bf16[128,640]{1,0:T(8,128)(2,1)} %bitcast.5), channel_id=1, source_target_pairs={{0,384},{1,385},{2,386},{3,387},{4,388},{5,389},{6,390},{7,391}} | collective-permute-start | bytes 491528 | tf_op jit(solution)/shard_map/ppermute | solution.py:229
  2.6 1.9 %collective-permute-start = (bf16[128,640]{1,0:T(8,128)(2,1)}, bf16[128,640]{1,0:T(8,128)(2,1)S(1)}, u32[]{:S(2)}, u32[]{:S(2)}) collective-permute-start(bf16[128,640]{1,0:T(8,128)(2,1)} %bitcast.6), channel_id=1, source_target_pairs={{0,8},{8,16},{16,24},{24,32},{32,40},{40,48},{48,56},{56,64},{64,7... | collective-permute-start | bytes 491528 | tf_op jit(solution)/shard_map/ppermute | solution.py:232
  4.6 0.9 %copy-done.5 = bf16[1,128,640]{2,1,0:T(8,128)(2,1)S(1)} copy-done((bf16[1,128,640]{2,1,0:T(8,128)(2,1)S(1)}, bf16[1,128,640]{2,1,0:T(8,128)(2,1)}, u32[]{:S(2)}) %copy-start.5) | copy-done | bytes 163864
  5.7 7.4 %collective-permute-done.3.rest_2_ = bf16[128,640]{1,0:T(8,128)(2,1)S(1)} collective-permute-done((bf16[128,640]{1,0:T(8,128)(2,1)}, bf16[128,640]{1,0:T(8,128)(2,1)S(1)}, u32[]{:S(2)}, u32[]{:S(2)}) %collective-permute-start.3) | collective-permute-done | bytes 163872 | tf_op jit(solution)/shard_map/ppermute | solution.py:229
  13.1 1.4 %collective-permute-start.4 = (bf16[128,640]{1,0:T(8,128)(2,1)S(1)}, bf16[128,640]{1,0:T(8,128)(2,1)S(1)}, u32[]{:S(2)}, u32[]{:S(2)}) collective-permute-start(bf16[128,640]{1,0:T(8,128)(2,1)S(1)} %pick_a.1.after.held), channel_id=1, source_target_pairs={{0,64},{128,192},{256,320},{384,448},{1,65},{129,193},{257,321},{3... | collective-permute-start | bytes 491528 | tf_op jit(solution)/shard_map/ppermute | solution.py:229
  14.6 1.3 %collective-permute-start.5 = (bf16[128,640]{1,0:T(8,128)(2,1)S(1)}, bf16[128,640]{1,0:T(8,128)(2,1)S(1)}, u32[]{:S(2)}, u32[]{:S(2)}) collective-permute-start(bf16[128,640]{1,0:T(8,128)(2,1)S(1)} %pick_a.1.after.held), channel_id=1, source_target_pairs={{0,16},{128,144},{256,272},{384,400},{1,17},{129,145},{257,273},{3... | collective-permute-start | bytes 491528 | tf_op jit(solution)/shard_map/ppermute | solution.py:229
  15.9 1.7 %collective-permute-start.6 = (bf16[128,640]{1,0:T(8,128)(2,1)S(1)}, bf16[128,640]{1,0:T(8,128)(2,1)S(1)}, u32[]{:S(2)}, u32[]{:S(2)}) collective-permute-start(bf16[128,640]{1,0:T(8,128)(2,1)S(1)} %pick_a.1.after.held), channel_id=1, source_target_pairs={{0,32},{128,160},{256,288},{384,416},{1,33},{129,161},{257,289},{3... | collective-permute-start | bytes 491528 | tf_op jit(solution)/shard_map/ppermute | solution.py:229
  17.6 1.3 %collective-permute-start.7 = (bf16[128,640]{1,0:T(8,128)(2,1)S(1)}, bf16[128,640]{1,0:T(8,128)(2,1)S(1)}, u32[]{:S(2)}, u32[]{:S(2)}) collective-permute-start(bf16[128,640]{1,0:T(8,128)(2,1)S(1)} %pick_a.1.after.held), channel_id=1, source_target_pairs={{0,48},{128,176},{256,304},{384,432},{1,49},{129,177},{257,305},{3... | collective-permute-start | bytes 491528 | tf_op jit(solution)/shard_map/ppermute | solution.py:229
  19.0 0.9 %own_rows.1.mine = bf16[8,240,128]{2,1,0:T(8,128)(2,1)S(1)} custom-call(bf16[128,640]{1,0:T(8,128)(2,1)S(1)} %stage.1.own.held.latents, f32[640]{0:T(1024)S(1)} %copy-done.4, bf16[640,640]{1,0:T(8,128)(2,1)S(1)} %copy-done.2, bf16[640,640]{1,0:T(8,128)(2,1)S(1)} %copy-done, bf16[640,640]{1,0:T(8,128)(2,1)S(1)} %copy-done.1), custom_call_target="tpu_custom_call" | custom-call | flops 314572800 | bytes 2457600 | tf_op jit(solution)/shard_map/own_rows/pallas_call | solution.py:205
  19.8 1.4 %prior_rows.1 = bf16[8,400,128]{2,1,0:T(8,128)(2,1)} custom-call(s32[1]{0:T(128)} %bitcast.frame, bf16[8,240,128]{2,1,0:T(8,128)(2,1)S(1)} %own_rows.1.mine, bf16[128,640]{1,0:T(8,128)(2,1)S(1)} %stage.1.own.held.latents, bf16[128,640]{1,0:T(8,128)(2,1)S(1)} %collective-permute-done.prior, f32[640]{0:T(1024)S(1)} %copy-done.4, bf16[640,640]{1,0:T(8,128)(2,1)S(1)} %copy-done, ...), custom_call_target="tpu_custom_call" | custom-call | flops 209715200 | bytes 1638400 | tf_op jit(solution)/shard_map/prior_rows/pallas_call | solution.py:205
  21.2 5.7 %all-to-all-start = ((bf16[8,400,128]{2,1,0:T(8,128)(2,1)}), bf16[8,400,128]{2,1,0:T(8,128)(2,1)S(1)}, u32[]{:S(2)}, u32[]{:S(2)}) async-start(bf16[8,400,128]{2,1,0:T(8,128)(2,1)} %prior_rows.1), calls=%async_computation | async-start | bytes 1638400 | tf_op jit(solution)/shard_map/all_to_all | solution.py:256
  27.0 0.7 %collective-permute-start.8 = (bf16[128,640]{1,0:T(8,128)(2,1)S(1)}, bf16[128,640]{1,0:T(8,128)(2,1)S(1)}, u32[]{:S(2)}, u32[]{:S(2)}) collective-permute-start(bf16[128,640]{1,0:T(8,128)(2,1)S(1)} %pick_b.1.held), channel_id=1, source_target_pairs={{16,80},{32,96},{48,112},{144,208},{160,224},{176,240},{272,336},{... | collective-permute-start | bytes 491528 | tf_op jit(solution)/shard_map/ppermute | solution.py:229
  27.7 1.3 %collective-permute-start.9 = (bf16[128,640]{1,0:T(8,128)(2,1)S(1)}, bf16[128,640]{1,0:T(8,128)(2,1)S(1)}, u32[]{:S(2)}, u32[]{:S(2)}) collective-permute-start(bf16[128,640]{1,0:T(8,128)(2,1)S(1)} %pick_b.1.held), channel_id=1, source_target_pairs={{0,72},{16,88},{32,104},{48,120},{128,200},{144,216},{160,232},{17... | collective-permute-start | bytes 491528 | tf_op jit(solution)/shard_map/ppermute | solution.py:229
  29.0 1.3 %collective-permute-start.10 = (bf16[128,640]{1,0:T(8,128)(2,1)S(1)}, bf16[128,640]{1,0:T(8,128)(2,1)S(1)}, u32[]{:S(2)}, u32[]{:S(2)}) collective-permute-start(bf16[128,640]{1,0:T(8,128)(2,1)S(1)} %pick_b.1.held), channel_id=1, source_target_pairs={{0,8},{16,24},{32,40},{48,56},{128,136},{144,152},{160,168},{176,1... | collective-permute-start | bytes 491528 | tf_op jit(solution)/shard_map/ppermute | solution.py:229
  30.3 1.5 %collective-permute-done.9.rest_1_ = bf16[128,640]{1,0:T(8,128)(2,1)S(1)} collective-permute-done((bf16[128,640]{1,0:T(8,128)(2,1)S(1)}, bf16[128,640]{1,0:T(8,128)(2,1)S(1)}, u32[]{:S(2)}, u32[]{:S(2)}) %collective-permute-start.9) | collective-permute-done | bytes 163872 | tf_op jit(solution)/shard_map/ppermute | solution.py:229
  31.8 1.5 %first_rows.1 = bf16[8,160,128]{2,1,0:T(8,128)(2,1)} custom-call(s32[1]{0:T(128)} %bitcast.frame, bf16[128,640]{1,0:T(8,128)(2,1)S(1)} %pick_b.1.held, bf16[128,640]{1,0:T(8,128)(2,1)S(1)} %collective-permute-done.8.rest_0_, bf16[128,640]{1,0:T(8,128)(2,1)S(1)} %collective-permute-done.9.rest_1_, bf16[128,640]{1,0:T(8,128)(2,1)S(1)} %collective-permute-done.10.rest_2_, ...), custom_call_target="tpu_custom_call" | custom-call | flops 209715200 | bytes 1638400 | tf_op jit(solution)/shard_map/first_rows/pallas_call | solution.py:205
  33.3 4.0 %all-to-all-done.rows = bf16[8,400,128]{2,1,0:T(8,128)(2,1)S(1)} async-done(((bf16[8,400,128]{2,1,0:T(8,128)(2,1)}), bf16[8,400,128]{2,1,0:T(8,128)(2,1)S(1)}, u32[]{:S(2)}, u32[]{:S(2)}) %all-to-all-start) | async-done | bytes 819232 | tf_op jit(solution)/shard_map/all_to_all | solution.py:256
  37.2 3.4 %all-to-all-start.1 = ((bf16[8,160,128]{2,1,0:T(8,128)(2,1)}), bf16[8,160,128]{2,1,0:T(8,128)(2,1)S(1)}, u32[]{:S(2)}, u32[]{:S(2)}) async-start(bf16[8,160,128]{2,1,0:T(8,128)(2,1)} %first_rows.1), calls=%async_computation.1 | async-start | bytes 655360 | tf_op jit(solution)/shard_map/all_to_all | solution.py:268
  40.7 3.3 %near.1 = (f32[8,1024]{1,0:T(8,128)S(1)}, f32[96,1024]{1,0:T(8,128)S(1)}, bf16[80,1024]{1,0:T(8,128)(2,1)S(1)}) custom-call(bf16[8,400,128]{2,1,0:T(8,128)(2,1)S(1)} %all-to-all-done.rows), custom_call_target="tpu_custom_call" | custom-call | flops 671088640 | bytes 819200 | tf_op jit(solution)/shard_map/near/pallas_call | solution.py:205
  44.0 4.3 %all-to-all-done.1.first = bf16[8,160,128]{2,1,0:T(8,128)(2,1)S(1)} async-done(((bf16[8,160,128]{2,1,0:T(8,128)(2,1)}), bf16[8,160,128]{2,1,0:T(8,128)(2,1)S(1)}, u32[]{:S(2)}, u32[]{:S(2)}) %all-to-all-start.1) | async-done | bytes 327712 | tf_op jit(solution)/shard_map/all_to_all | solution.py:268
  48.2 1.1 %far.1 = bf16[8,80,128]{2,1,0:T(8,128)(2,1)S(1)} custom-call(bf16[80,1024]{1,0:T(8,128)(2,1)S(1)} %get-tuple-element.8.queries, bf16[8,160,128]{2,1,0:T(8,128)(2,1)S(1)} %all-to-all-done.1.first, f32[8,1024]{1,0:T(8,128)S(1)} %get-tuple-element.9.peak, f32[96,1024]{1,0:T(8,128)S(1)} %get-tuple-element.10.total), custom_call_target="tpu_custom_call" | custom-call | flops 335544320 | bytes 327680 | tf_op jit(solution)/shard_map/far/pallas_call | solution.py:205
  49.4 9.3 %all_to_all.15.attended = bf16[8,80,128]{2,1,0:T(8,128)(2,1)S(1)} all-to-all(bf16[8,80,128]{2,1,0:T(8,128)(2,1)S(1)} %far.1), channel_id=1, replica_groups=mesh['frame'=64,'row'=8] {'row'}, dimensions={0} | all-to-all | bytes 327680 | tf_op jit(solution)/shard_map/all_to_all | solution.py:274
  58.7 1.0 %mix.1 = bf16[128,640]{1,0:T(8,128)(2,1)} custom-call(bf16[8,80,128]{2,1,0:T(8,128)(2,1)S(1)} %all_to_all.15.attended, bf16[128,640]{1,0:T(8,128)(2,1)S(1)} %stage.1.own.held.latents, bf16[640,640]{1,0:T(8,128)(2,1)S(1)} %copy-done.3), custom_call_target="tpu_custom_call" | custom-call | flops 104857600 | bytes 819200 | tf_op jit(solution)/shard_map/mix/pallas_call | solution.py:205
  (24 shorter events, 1.0 us)
Async XLA Ops:
  0.0 5.7 %collective-permute-start.1 = (bf16[128,640]{1,0:T(8,128)(2,1)}, bf16[128,640]{1,0:T(8,128)(2,1)S(1)}, u32[]{:S(2)}, u32[]{:S(2)}) collective-permute-start(bf16[128,640]{1,0:T(8,128)(2,1)} %bitcast.3), channel_id=1, source_target_pairs={{0,128},{1,129},{2,130},{3,131},{4,132},{5,133},{6,134},{7,135}} | collective-permute-start | bytes 491528 | tf_op jit(solution)/shard_map/ppermute | solution.py:229
  0.7 5.0 %collective-permute-start.2 = (bf16[128,640]{1,0:T(8,128)(2,1)}, bf16[128,640]{1,0:T(8,128)(2,1)S(1)}, u32[]{:S(2)}, u32[]{:S(2)}) collective-permute-start(bf16[128,640]{1,0:T(8,128)(2,1)} %bitcast.4), channel_id=1, source_target_pairs={{0,256},{1,257},{2,258},{3,259},{4,260},{5,261},{6,262},{7,263}} | collective-permute-start | bytes 491528 | tf_op jit(solution)/shard_map/ppermute | solution.py:229
  1.3 11.7 %collective-permute-start.3 = (bf16[128,640]{1,0:T(8,128)(2,1)}, bf16[128,640]{1,0:T(8,128)(2,1)S(1)}, u32[]{:S(2)}, u32[]{:S(2)}) collective-permute-start(bf16[128,640]{1,0:T(8,128)(2,1)} %bitcast.5), channel_id=1, source_target_pairs={{0,384},{1,385},{2,386},{3,387},{4,388},{5,389},{6,390},{7,391}} | collective-permute-start | bytes 491528 | tf_op jit(solution)/shard_map/ppermute | solution.py:229
  2.6 17.2 %collective-permute-start = (bf16[128,640]{1,0:T(8,128)(2,1)}, bf16[128,640]{1,0:T(8,128)(2,1)S(1)}, u32[]{:S(2)}, u32[]{:S(2)}) collective-permute-start(bf16[128,640]{1,0:T(8,128)(2,1)} %bitcast.6), channel_id=1, source_target_pairs={{0,8},{8,16},{16,24},{24,32},{32,40},{40,48},{48,56},{56,64},{64,7... | collective-permute-start | bytes 491528 | tf_op jit(solution)/shard_map/ppermute | solution.py:232
  4.6 0.9 %copy-start.5 = (bf16[1,128,640]{2,1,0:T(8,128)(2,1)S(1)}, bf16[1,128,640]{2,1,0:T(8,128)(2,1)}, u32[]{:S(2)}) copy-start(bf16[1,128,640]{2,1,0:T(8,128)(2,1)} %param.6) | copy-start | bytes 491524
  13.1 5.8 %copy-start = (bf16[640,640]{1,0:T(8,128)(2,1)S(1)}, bf16[640,640]{1,0:T(8,128)(2,1)}, u32[]{:S(2)}) copy-start(bf16[640,640]{1,0:T(8,128)(2,1)} %rest_4_.1) | copy-start | bytes 2457604
  13.1 5.9 %copy-start.1 = (bf16[640,640]{1,0:T(8,128)(2,1)S(1)}, bf16[640,640]{1,0:T(8,128)(2,1)}, u32[]{:S(2)}) copy-start(bf16[640,640]{1,0:T(8,128)(2,1)} %rest_5_.1) | copy-start | bytes 2457604
  13.1 5.9 %copy-start.2 = (bf16[640,640]{1,0:T(8,128)(2,1)S(1)}, bf16[640,640]{1,0:T(8,128)(2,1)}, u32[]{:S(2)}) copy-start(bf16[640,640]{1,0:T(8,128)(2,1)} %w_query.1) | copy-start | bytes 2457604
  13.1 5.9 %copy-start.4 = (f32[640]{0:T(1024)S(1)}, f32[640]{0:T(1024)}, u32[]{:S(2)}) copy-start(f32[640]{0:T(1024)} %rest_3_.1) | copy-start | bytes 7684
  13.1 13.8 %collective-permute-start.4 = (bf16[128,640]{1,0:T(8,128)(2,1)S(1)}, bf16[128,640]{1,0:T(8,128)(2,1)S(1)}, u32[]{:S(2)}, u32[]{:S(2)}) collective-permute-start(bf16[128,640]{1,0:T(8,128)(2,1)S(1)} %pick_a.1.after.held), channel_id=1, source_target_pairs={{0,64},{128,192},{256,320},{384,448},{1,65},{129,193},{257,321},{3... | collective-permute-start | bytes 491528 | tf_op jit(solution)/shard_map/ppermute | solution.py:229
  14.6 12.3 %collective-permute-start.5 = (bf16[128,640]{1,0:T(8,128)(2,1)S(1)}, bf16[128,640]{1,0:T(8,128)(2,1)S(1)}, u32[]{:S(2)}, u32[]{:S(2)}) collective-permute-start(bf16[128,640]{1,0:T(8,128)(2,1)S(1)} %pick_a.1.after.held), channel_id=1, source_target_pairs={{0,16},{128,144},{256,272},{384,400},{1,17},{129,145},{257,273},{3... | collective-permute-start | bytes 491528 | tf_op jit(solution)/shard_map/ppermute | solution.py:229
  15.9 11.0 %collective-permute-start.6 = (bf16[128,640]{1,0:T(8,128)(2,1)S(1)}, bf16[128,640]{1,0:T(8,128)(2,1)S(1)}, u32[]{:S(2)}, u32[]{:S(2)}) collective-permute-start(bf16[128,640]{1,0:T(8,128)(2,1)S(1)} %pick_a.1.after.held), channel_id=1, source_target_pairs={{0,32},{128,160},{256,288},{384,416},{1,33},{129,161},{257,289},{3... | collective-permute-start | bytes 491528 | tf_op jit(solution)/shard_map/ppermute | solution.py:229
  17.6 9.3 %collective-permute-start.7 = (bf16[128,640]{1,0:T(8,128)(2,1)S(1)}, bf16[128,640]{1,0:T(8,128)(2,1)S(1)}, u32[]{:S(2)}, u32[]{:S(2)}) collective-permute-start(bf16[128,640]{1,0:T(8,128)(2,1)S(1)} %pick_a.1.after.held), channel_id=1, source_target_pairs={{0,48},{128,176},{256,304},{384,432},{1,49},{129,177},{257,305},{3... | collective-permute-start | bytes 491528 | tf_op jit(solution)/shard_map/ppermute | solution.py:229
  21.2 16.0 %all-to-all-start = ((bf16[8,400,128]{2,1,0:T(8,128)(2,1)}), bf16[8,400,128]{2,1,0:T(8,128)(2,1)S(1)}, u32[]{:S(2)}, u32[]{:S(2)}) async-start(bf16[8,400,128]{2,1,0:T(8,128)(2,1)} %prior_rows.1), calls=%async_computation | async-start | bytes 1638400 | tf_op jit(solution)/shard_map/all_to_all | solution.py:256
  27.0 3.3 %collective-permute-start.8 = (bf16[128,640]{1,0:T(8,128)(2,1)S(1)}, bf16[128,640]{1,0:T(8,128)(2,1)S(1)}, u32[]{:S(2)}, u32[]{:S(2)}) collective-permute-start(bf16[128,640]{1,0:T(8,128)(2,1)S(1)} %pick_b.1.held), channel_id=1, source_target_pairs={{16,80},{32,96},{48,112},{144,208},{160,224},{176,240},{272,336},{... | collective-permute-start | bytes 491528 | tf_op jit(solution)/shard_map/ppermute | solution.py:229
  27.7 4.1 %collective-permute-start.9 = (bf16[128,640]{1,0:T(8,128)(2,1)S(1)}, bf16[128,640]{1,0:T(8,128)(2,1)S(1)}, u32[]{:S(2)}, u32[]{:S(2)}) collective-permute-start(bf16[128,640]{1,0:T(8,128)(2,1)S(1)} %pick_b.1.held), channel_id=1, source_target_pairs={{0,72},{16,88},{32,104},{48,120},{128,200},{144,216},{160,232},{17... | collective-permute-start | bytes 491528 | tf_op jit(solution)/shard_map/ppermute | solution.py:229
  29.0 2.8 %collective-permute-start.10 = (bf16[128,640]{1,0:T(8,128)(2,1)S(1)}, bf16[128,640]{1,0:T(8,128)(2,1)S(1)}, u32[]{:S(2)}, u32[]{:S(2)}) collective-permute-start(bf16[128,640]{1,0:T(8,128)(2,1)S(1)} %pick_b.1.held), channel_id=1, source_target_pairs={{0,8},{16,24},{32,40},{48,56},{128,136},{144,152},{160,168},{176,1... | collective-permute-start | bytes 491528 | tf_op jit(solution)/shard_map/ppermute | solution.py:229
  37.2 11.0 %all-to-all-start.1 = ((bf16[8,160,128]{2,1,0:T(8,128)(2,1)}), bf16[8,160,128]{2,1,0:T(8,128)(2,1)S(1)}, u32[]{:S(2)}, u32[]{:S(2)}) async-start(bf16[8,160,128]{2,1,0:T(8,128)(2,1)} %first_rows.1), calls=%async_computation.1 | async-start | bytes 655360 | tf_op jit(solution)/shard_map/all_to_all | solution.py:268
  44.0 14.7 %copy-start.3 = (bf16[640,640]{1,0:T(8,128)(2,1)S(1)}, bf16[640,640]{1,0:T(8,128)(2,1)}, u32[]{:S(2)}) copy-start(bf16[640,640]{1,0:T(8,128)(2,1)} %w_out.1) | copy-start | bytes 2457604

commit v6 on v5

--- a/solution.py
+++ b/solution.py
@@ -11,6 +11,7 @@
 HEADS = 8
 SPREAD = 16
 VMEM = 24 * 2**20
+STAGE_VMEM = 62 * 2**20
 COST_STAGE = 10**9
 COST_A = 3 * 10**10
 COST_B = 3 * 10**10
@@ -200,7 +201,7 @@
     out[...] = (latents[...].astype(jnp.float32) + update).astype(jnp.bfloat16)
 
 
-def call(kernel, name, shapes, operands, kinds, to=pltpu.VMEM, scratch=(), flops=0, moved=0):
+def call(kernel, name, shapes, operands, kinds, to=pltpu.VMEM, scratch=(), vmem=VMEM, flops=0, moved=0):
     spaces = {"s": pltpu.SMEM, "v": pltpu.VMEM, "a": pl.ANY}
     return pl.pallas_call(
         kernel,
@@ -208,7 +209,7 @@
         in_specs=[pl.BlockSpec(memory_space=spaces[kind]) for kind in kinds],
         out_specs=jax.tree.map(lambda _: pl.BlockSpec(memory_space=to), shapes),
         scratch_shapes=list(scratch),
-        compiler_params=pltpu.CompilerParams(vmem_limit_bytes=VMEM),
+        compiler_params=pltpu.CompilerParams(vmem_limit_bytes=vmem),
         cost_estimate=pl.CostEstimate(flops=int(flops), bytes_accessed=int(moved), transcendentals=0),
         name=name,
     )(*operands)
@@ -230,7 +231,7 @@
 
     arrived = send(own, 0)
     prior = lax.ppermute(own, "frame", [(i, i + 1) for i in range(frames - 1)])
-    own = call(stage_kernel, "stage", shape(positions, channels), (own,), "a", flops=COST_STAGE)
+    own = call(stage_kernel, "stage", shape(positions, channels), (own,), "a", vmem=STAGE_VMEM, flops=COST_STAGE)
     held_a = call(
         functools.partial(pick_kernel, 0), "pick_a", shape(positions, channels),
         (at, own, *arrived), "svvvv", flops=COST_A,

time: 60.2 us -> 61.3 us (1.018)
  Pallas kernels: 9.41 us -> 10.8 us
    pallas_call x9, Pallas kernels: 9.41 us -> 10.8 us  [call(): pl.pallas_call(kernel, out_shape=shapes, in_specs=[pl.BlockSpec(memory_sp...]
  transfers between devices with their start and end apart: 13 -> 13, of which waited for: 4 -> 4; matrix products, arithmetic and copies ran while one was open for 0% -> 0% of each run, Pallas kernels for 12% -> 14%
where the time goes in v6:
time: 61.3 us; the launch traced here: 60.8 us
  starting transfers between devices  22.7 us (37%)
  waiting for transfers between devices  16.6 us (27%)
  Pallas kernels  10.8 us (18%)
  blocking collectives  9.46 us (15%)
  local copies, waits for them, and re-layouts  0.94 us (2%)
    ppermute x10, starting transfers between devices, send(): lax.ppermute(array, 'frame', pairs_of(*permute))  12.1 us
    pallas_call x9, Pallas kernels, call(): pl.pallas_call(kernel, out_shape=shapes, in_specs=[pl.BlockSpec(memory_sp...  10.8 us
    all_to_all x1, blocking collectives, body(): back = lax.all_to_all(attended, 'row', 0, 0, tiled=True)  9.46 us
    ppermute x10, waiting for transfers between devices, send(): lax.ppermute(array, 'frame', pairs_of(*permute))  8.42 us
    all_to_all x1, starting transfers between devices, body(): rows = lax.all_to_all(mine, 'row', 0, 0, tiled=True)  5.28 us
    all_to_all x1, waiting for transfers between devices, body(): first = lax.all_to_all(theirs, 'row', 0, 0, tiled=True)  4.25 us
    all_to_all x1, waiting for transfers between devices, body(): rows = lax.all_to_all(mine, 'row', 0, 0, tiled=True)  3.94 us
    all_to_all x1, starting transfers between devices, body(): first = lax.all_to_all(theirs, 'row', 0, 0, tiled=True)  3.43 us
  transfers between devices with their start and end apart: 13, of which 4 were waited for; matrix products, arithmetic and copies ran while one was open for 0% of the time, Pallas kernels for 14%

profile of v6, /device:TPU:48, one launch (start us, length us, event | category | flops | bytes accessed | tf_op | source)
XLA Modules:
  0.0 60.8 jit_solution(4574736742024790428)
XLA Ops:
  0.7 0.7 %collective-permute-start.2 = (bf16[128,640]{1,0:T(8,128)(2,1)}, bf16[128,640]{1,0:T(8,128)(2,1)S(1)}, u32[]{:S(2)}, u32[]{:S(2)}) collective-permute-start(bf16[128,640]{1,0:T(8,128)(2,1)} %bitcast.4), channel_id=1, source_target_pairs={{0,256},{1,257},{2,258},{3,259},{4,260},{5,261},{6,262},{7,263}} | collective-permute-start | bytes 491528 | tf_op jit(solution)/shard_map/ppermute | solution.py:230
  1.3 1.3 %collective-permute-start.3 = (bf16[128,640]{1,0:T(8,128)(2,1)}, bf16[128,640]{1,0:T(8,128)(2,1)S(1)}, u32[]{:S(2)}, u32[]{:S(2)}) collective-permute-start(bf16[128,640]{1,0:T(8,128)(2,1)} %bitcast.5), channel_id=1, source_target_pairs={{0,384},{1,385},{2,386},{3,387},{4,388},{5,389},{6,390},{7,391}} | collective-permute-start | bytes 491528 | tf_op jit(solution)/shard_map/ppermute | solution.py:230
  2.6 1.9 %collective-permute-start = (bf16[128,640]{1,0:T(8,128)(2,1)}, bf16[128,640]{1,0:T(8,128)(2,1)S(1)}, u32[]{:S(2)}, u32[]{:S(2)}) collective-permute-start(bf16[128,640]{1,0:T(8,128)(2,1)} %bitcast.6), channel_id=1, source_target_pairs={{0,8},{8,16},{16,24},{24,32},{32,40},{40,48},{48,56},{56,64},{64,7... | collective-permute-start | bytes 491528 | tf_op jit(solution)/shard_map/ppermute | solution.py:233
  4.6 1.6 %stage.1.own.held.latents = bf16[128,640]{1,0:T(8,128)(2,1)} custom-call(bf16[128,640]{1,0:T(8,128)(2,1)} %bitcast.7), custom_call_target="tpu_custom_call" | custom-call | flops 1000000000 | tf_op jit(solution)/shard_map/stage/pallas_call | solution.py:206
  6.2 6.9 %collective-permute-done.3.rest_2_ = bf16[128,640]{1,0:T(8,128)(2,1)S(1)} collective-permute-done((bf16[128,640]{1,0:T(8,128)(2,1)}, bf16[128,640]{1,0:T(8,128)(2,1)S(1)}, u32[]{:S(2)}, u32[]{:S(2)}) %collective-permute-start.3) | collective-permute-done | bytes 163872 | tf_op jit(solution)/shard_map/ppermute | solution.py:230
  13.1 0.9 %copy-done.2 = bf16[128,640]{1,0:T(8,128)(2,1)S(1)} copy-done((bf16[128,640]{1,0:T(8,128)(2,1)S(1)}, bf16[128,640]{1,0:T(8,128)(2,1)}, u32[]{:S(2)}) %copy-start.2) | copy-done | bytes 163864
  14.1 1.4 %collective-permute-start.4 = (bf16[128,640]{1,0:T(8,128)(2,1)S(1)}, bf16[128,640]{1,0:T(8,128)(2,1)S(1)}, u32[]{:S(2)}, u32[]{:S(2)}) collective-permute-start(bf16[128,640]{1,0:T(8,128)(2,1)S(1)} %pick_a.1.after.held), channel_id=1, source_target_pairs={{0,64},{128,192},{256,320},{384,448},{1,65},{129,193},{257,321},{3... | collective-permute-start | bytes 491528 | tf_op jit(solution)/shard_map/ppermute | solution.py:230
  15.5 1.3 %collective-permute-start.5 = (bf16[128,640]{1,0:T(8,128)(2,1)S(1)}, bf16[128,640]{1,0:T(8,128)(2,1)S(1)}, u32[]{:S(2)}, u32[]{:S(2)}) collective-permute-start(bf16[128,640]{1,0:T(8,128)(2,1)S(1)} %pick_a.1.after.held), channel_id=1, source_target_pairs={{0,16},{128,144},{256,272},{384,400},{1,17},{129,145},{257,273},{3... | collective-permute-start | bytes 491528 | tf_op jit(solution)/shard_map/ppermute | solution.py:230
  16.8 2.1 %collective-permute-start.6 = (bf16[128,640]{1,0:T(8,128)(2,1)S(1)}, bf16[128,640]{1,0:T(8,128)(2,1)S(1)}, u32[]{:S(2)}, u32[]{:S(2)}) collective-permute-start(bf16[128,640]{1,0:T(8,128)(2,1)S(1)} %pick_a.1.after.held), channel_id=1, source_target_pairs={{0,32},{128,160},{256,288},{384,416},{1,33},{129,161},{257,289},{3... | collective-permute-start | bytes 491528 | tf_op jit(solution)/shard_map/ppermute | solution.py:230
  19.0 1.3 %collective-permute-start.7 = (bf16[128,640]{1,0:T(8,128)(2,1)S(1)}, bf16[128,640]{1,0:T(8,128)(2,1)S(1)}, u32[]{:S(2)}, u32[]{:S(2)}) collective-permute-start(bf16[128,640]{1,0:T(8,128)(2,1)S(1)} %pick_a.1.after.held), channel_id=1, source_target_pairs={{0,48},{128,176},{256,304},{384,432},{1,49},{129,177},{257,305},{3... | collective-permute-start | bytes 491528 | tf_op jit(solution)/shard_map/ppermute | solution.py:230
  20.3 0.9 %own_rows.1.mine = bf16[8,240,128]{2,1,0:T(8,128)(2,1)S(1)} custom-call(bf16[128,640]{1,0:T(8,128)(2,1)S(1)} %copy-done.2, f32[640]{0:T(1024)S(1)} %copy-done.6, bf16[640,640]{1,0:T(8,128)(2,1)S(1)} %copy-done.4, bf16[640,640]{1,0:T(8,128)(2,1)S(1)} %copy-done, bf16[640,640]{1,0:T(8,128)(2,1)S(1)} %copy-done.1), custom_call_target="tpu_custom_call" | custom-call | flops 314572800 | bytes 2457600 | tf_op jit(solution)/shard_map/own_rows/pallas_call | solution.py:206
  21.2 1.4 %prior_rows.1 = bf16[8,400,128]{2,1,0:T(8,128)(2,1)} custom-call(s32[1]{0:T(128)} %bitcast.frame, bf16[8,240,128]{2,1,0:T(8,128)(2,1)S(1)} %own_rows.1.mine, bf16[128,640]{1,0:T(8,128)(2,1)S(1)} %copy-done.2, bf16[128,640]{1,0:T(8,128)(2,1)S(1)} %collective-permute-done.prior, f32[640]{0:T(1024)S(1)} %copy-done.6, bf16[640,640]{1,0:T(8,128)(2,1)S(1)} %copy-done, ...), custom_call_target="tpu_custom_call" | custom-call | flops 209715200 | bytes 1638400 | tf_op jit(solution)/shard_map/prior_rows/pallas_call | solution.py:206
  22.6 5.3 %all-to-all-start = ((bf16[8,400,128]{2,1,0:T(8,128)(2,1)}), bf16[8,400,128]{2,1,0:T(8,128)(2,1)S(1)}, u32[]{:S(2)}, u32[]{:S(2)}) async-start(bf16[8,400,128]{2,1,0:T(8,128)(2,1)} %prior_rows.1), calls=%async_computation | async-start | bytes 1638400 | tf_op jit(solution)/shard_map/all_to_all | solution.py:257
  28.6 1.3 %collective-permute-start.9 = (bf16[128,640]{1,0:T(8,128)(2,1)S(1)}, bf16[128,640]{1,0:T(8,128)(2,1)S(1)}, u32[]{:S(2)}, u32[]{:S(2)}) collective-permute-start(bf16[128,640]{1,0:T(8,128)(2,1)S(1)} %pick_b.1.held), channel_id=1, source_target_pairs={{0,72},{16,88},{32,104},{48,120},{128,200},{144,216},{160,232},{17... | collective-permute-start | bytes 491528 | tf_op jit(solution)/shard_map/ppermute | solution.py:230
  29.9 1.3 %collective-permute-start.10 = (bf16[128,640]{1,0:T(8,128)(2,1)S(1)}, bf16[128,640]{1,0:T(8,128)(2,1)S(1)}, u32[]{:S(2)}, u32[]{:S(2)}) collective-permute-start(bf16[128,640]{1,0:T(8,128)(2,1)S(1)} %pick_b.1.held), channel_id=1, source_target_pairs={{0,8},{16,24},{32,40},{48,56},{128,136},{144,152},{160,168},{176,1... | collective-permute-start | bytes 491528 | tf_op jit(solution)/shard_map/ppermute | solution.py:230
  31.3 1.5 %collective-permute-done.9.rest_1_ = bf16[128,640]{1,0:T(8,128)(2,1)S(1)} collective-permute-done((bf16[128,640]{1,0:T(8,128)(2,1)S(1)}, bf16[128,640]{1,0:T(8,128)(2,1)S(1)}, u32[]{:S(2)}, u32[]{:S(2)}) %collective-permute-start.9) | collective-permute-done | bytes 163872 | tf_op jit(solution)/shard_map/ppermute | solution.py:230
  32.8 1.5 %first_rows.1 = bf16[8,160,128]{2,1,0:T(8,128)(2,1)} custom-call(s32[1]{0:T(128)} %bitcast.frame, bf16[128,640]{1,0:T(8,128)(2,1)S(1)} %pick_b.1.held, bf16[128,640]{1,0:T(8,128)(2,1)S(1)} %collective-permute-done.8.rest_0_, bf16[128,640]{1,0:T(8,128)(2,1)S(1)} %collective-permute-done.9.rest_1_, bf16[128,640]{1,0:T(8,128)(2,1)S(1)} %collective-permute-done.10.rest_2_, ...), custom_call_target="tpu_custom_call" | custom-call | flops 209715200 | bytes 1638400 | tf_op jit(solution)/shard_map/first_rows/pallas_call | solution.py:206
  34.2 3.9 %all-to-all-done.rows = bf16[8,400,128]{2,1,0:T(8,128)(2,1)S(1)} async-done(((bf16[8,400,128]{2,1,0:T(8,128)(2,1)}), bf16[8,400,128]{2,1,0:T(8,128)(2,1)S(1)}, u32[]{:S(2)}, u32[]{:S(2)}) %all-to-all-start) | async-done | bytes 819232 | tf_op jit(solution)/shard_map/all_to_all | solution.py:257
  38.2 3.4 %all-to-all-start.1 = ((bf16[8,160,128]{2,1,0:T(8,128)(2,1)}), bf16[8,160,128]{2,1,0:T(8,128)(2,1)S(1)}, u32[]{:S(2)}, u32[]{:S(2)}) async-start(bf16[8,160,128]{2,1,0:T(8,128)(2,1)} %first_rows.1), calls=%async_computation.1 | async-start | bytes 655360 | tf_op jit(solution)/shard_map/all_to_all | solution.py:269
  41.6 3.3 %near.1 = (f32[8,1024]{1,0:T(8,128)S(1)}, f32[96,1024]{1,0:T(8,128)S(1)}, bf16[80,1024]{1,0:T(8,128)(2,1)S(1)}) custom-call(bf16[8,400,128]{2,1,0:T(8,128)(2,1)S(1)} %all-to-all-done.rows), custom_call_target="tpu_custom_call" | custom-call | flops 671088640 | bytes 819200 | tf_op jit(solution)/shard_map/near/pallas_call | solution.py:206
  44.9 4.3 %all-to-all-done.1.first = bf16[8,160,128]{2,1,0:T(8,128)(2,1)S(1)} async-done(((bf16[8,160,128]{2,1,0:T(8,128)(2,1)}), bf16[8,160,128]{2,1,0:T(8,128)(2,1)S(1)}, u32[]{:S(2)}, u32[]{:S(2)}) %all-to-all-start.1) | async-done | bytes 327712 | tf_op jit(solution)/shard_map/all_to_all | solution.py:269
  49.2 1.1 %far.1 = bf16[8,80,128]{2,1,0:T(8,128)(2,1)S(1)} custom-call(bf16[80,1024]{1,0:T(8,128)(2,1)S(1)} %get-tuple-element.8.queries, bf16[8,160,128]{2,1,0:T(8,128)(2,1)S(1)} %all-to-all-done.1.first, f32[8,1024]{1,0:T(8,128)S(1)} %get-tuple-element.9.peak, f32[96,1024]{1,0:T(8,128)S(1)} %get-tuple-element.10.total), custom_call_target="tpu_custom_call" | custom-call | flops 335544320 | bytes 327680 | tf_op jit(solution)/shard_map/far/pallas_call | solution.py:206
  50.3 9.5 %all_to_all.15.attended = bf16[8,80,128]{2,1,0:T(8,128)(2,1)S(1)} all-to-all(bf16[8,80,128]{2,1,0:T(8,128)(2,1)S(1)} %far.1), channel_id=1, replica_groups=mesh['frame'=64,'row'=8] {'row'}, dimensions={0} | all-to-all | bytes 327680 | tf_op jit(solution)/shard_map/all_to_all | solution.py:275
  59.8 1.0 %mix.1 = bf16[128,640]{1,0:T(8,128)(2,1)} custom-call(bf16[8,80,128]{2,1,0:T(8,128)(2,1)S(1)} %all_to_all.15.attended, bf16[128,640]{1,0:T(8,128)(2,1)S(1)} %copy-done.3, bf16[640,640]{1,0:T(8,128)(2,1)S(1)} %copy-done.5), custom_call_target="tpu_custom_call" | custom-call | flops 104857600 | bytes 819200 | tf_op jit(solution)/shard_map/mix/pallas_call | solution.py:206
  (26 shorter events, 1.5 us)
Async XLA Ops:
  0.0 6.2 %collective-permute-start.1 = (bf16[128,640]{1,0:T(8,128)(2,1)}, bf16[128,640]{1,0:T(8,128)(2,1)S(1)}, u32[]{:S(2)}, u32[]{:S(2)}) collective-permute-start(bf16[128,640]{1,0:T(8,128)(2,1)} %bitcast.3), channel_id=1, source_target_pairs={{0,128},{1,129},{2,130},{3,131},{4,132},{5,133},{6,134},{7,135}} | collective-permute-start | bytes 491528 | tf_op jit(solution)/shard_map/ppermute | solution.py:230
  0.7 5.5 %collective-permute-start.2 = (bf16[128,640]{1,0:T(8,128)(2,1)}, bf16[128,640]{1,0:T(8,128)(2,1)S(1)}, u32[]{:S(2)}, u32[]{:S(2)}) collective-permute-start(bf16[128,640]{1,0:T(8,128)(2,1)} %bitcast.4), channel_id=1, source_target_pairs={{0,256},{1,257},{2,258},{3,259},{4,260},{5,261},{6,262},{7,263}} | collective-permute-start | bytes 491528 | tf_op jit(solution)/shard_map/ppermute | solution.py:230
  1.3 11.7 %collective-permute-start.3 = (bf16[128,640]{1,0:T(8,128)(2,1)}, bf16[128,640]{1,0:T(8,128)(2,1)S(1)}, u32[]{:S(2)}, u32[]{:S(2)}) collective-permute-start(bf16[128,640]{1,0:T(8,128)(2,1)} %bitcast.5), channel_id=1, source_target_pairs={{0,384},{1,385},{2,386},{3,387},{4,388},{5,389},{6,390},{7,391}} | collective-permute-start | bytes 491528 | tf_op jit(solution)/shard_map/ppermute | solution.py:230
  2.6 18.5 %collective-permute-start = (bf16[128,640]{1,0:T(8,128)(2,1)}, bf16[128,640]{1,0:T(8,128)(2,1)S(1)}, u32[]{:S(2)}, u32[]{:S(2)}) collective-permute-start(bf16[128,640]{1,0:T(8,128)(2,1)} %bitcast.6), channel_id=1, source_target_pairs={{0,8},{8,16},{16,24},{24,32},{32,40},{40,48},{48,56},{56,64},{64,7... | collective-permute-start | bytes 491528 | tf_op jit(solution)/shard_map/ppermute | solution.py:233
  13.1 0.9 %copy-start.2 = (bf16[128,640]{1,0:T(8,128)(2,1)S(1)}, bf16[128,640]{1,0:T(8,128)(2,1)}, u32[]{:S(2)}) copy-start(bf16[128,640]{1,0:T(8,128)(2,1)} %stage.1.own.held.latents) | copy-start | bytes 491524
  14.0 6.3 %copy-start = (bf16[640,640]{1,0:T(8,128)(2,1)S(1)}, bf16[640,640]{1,0:T(8,128)(2,1)}, u32[]{:S(2)}) copy-start(bf16[640,640]{1,0:T(8,128)(2,1)} %rest_4_.1) | copy-start | bytes 2457604
  14.0 6.3 %copy-start.1 = (bf16[640,640]{1,0:T(8,128)(2,1)S(1)}, bf16[640,640]{1,0:T(8,128)(2,1)}, u32[]{:S(2)}) copy-start(bf16[640,640]{1,0:T(8,128)(2,1)} %rest_5_.1) | copy-start | bytes 2457604
  14.0 6.3 %copy-start.4 = (bf16[640,640]{1,0:T(8,128)(2,1)S(1)}, bf16[640,640]{1,0:T(8,128)(2,1)}, u32[]{:S(2)}) copy-start(bf16[640,640]{1,0:T(8,128)(2,1)} %w_query.1) | copy-start | bytes 2457604
  14.0 6.3 %copy-start.6 = (f32[640]{0:T(1024)S(1)}, f32[640]{0:T(1024)}, u32[]{:S(2)}) copy-start(f32[640]{0:T(1024)} %rest_3_.1) | copy-start | bytes 7684
  14.1 13.8 %collective-permute-start.4 = (bf16[128,640]{1,0:T(8,128)(2,1)S(1)}, bf16[128,640]{1,0:T(8,128)(2,1)S(1)}, u32[]{:S(2)}, u32[]{:S(2)}) collective-permute-start(bf16[128,640]{1,0:T(8,128)(2,1)S(1)} %pick_a.1.after.held), channel_id=1, source_target_pairs={{0,64},{128,192},{256,320},{384,448},{1,65},{129,193},{257,321},{3... | collective-permute-start | bytes 491528 | tf_op jit(solution)/shard_map/ppermute | solution.py:230
  15.5 12.4 %collective-permute-start.5 = (bf16[128,640]{1,0:T(8,128)(2,1)S(1)}, bf16[128,640]{1,0:T(8,128)(2,1)S(1)}, u32[]{:S(2)}, u32[]{:S(2)}) collective-permute-start(bf16[128,640]{1,0:T(8,128)(2,1)S(1)} %pick_a.1.after.held), channel_id=1, source_target_pairs={{0,16},{128,144},{256,272},{384,400},{1,17},{129,145},{257,273},{3... | collective-permute-start | bytes 491528 | tf_op jit(solution)/shard_map/ppermute | solution.py:230
  16.8 11.1 %collective-permute-start.6 = (bf16[128,640]{1,0:T(8,128)(2,1)S(1)}, bf16[128,640]{1,0:T(8,128)(2,1)S(1)}, u32[]{:S(2)}, u32[]{:S(2)}) collective-permute-start(bf16[128,640]{1,0:T(8,128)(2,1)S(1)} %pick_a.1.after.held), channel_id=1, source_target_pairs={{0,32},{128,160},{256,288},{384,416},{1,33},{129,161},{257,289},{3... | collective-permute-start | bytes 491528 | tf_op jit(solution)/shard_map/ppermute | solution.py:230
  19.0 8.9 %collective-permute-start.7 = (bf16[128,640]{1,0:T(8,128)(2,1)S(1)}, bf16[128,640]{1,0:T(8,128)(2,1)S(1)}, u32[]{:S(2)}, u32[]{:S(2)}) collective-permute-start(bf16[128,640]{1,0:T(8,128)(2,1)S(1)} %pick_a.1.after.held), channel_id=1, source_target_pairs={{0,48},{128,176},{256,304},{384,432},{1,49},{129,177},{257,305},{3... | collective-permute-start | bytes 491528 | tf_op jit(solution)/shard_map/ppermute | solution.py:230
  22.6 15.6 %all-to-all-start = ((bf16[8,400,128]{2,1,0:T(8,128)(2,1)}), bf16[8,400,128]{2,1,0:T(8,128)(2,1)S(1)}, u32[]{:S(2)}, u32[]{:S(2)}) async-start(bf16[8,400,128]{2,1,0:T(8,128)(2,1)} %prior_rows.1), calls=%async_computation | async-start | bytes 1638400 | tf_op jit(solution)/shard_map/all_to_all | solution.py:257
  28.0 3.3 %collective-permute-start.8 = (bf16[128,640]{1,0:T(8,128)(2,1)S(1)}, bf16[128,640]{1,0:T(8,128)(2,1)S(1)}, u32[]{:S(2)}, u32[]{:S(2)}) collective-permute-start(bf16[128,640]{1,0:T(8,128)(2,1)S(1)} %pick_b.1.held), channel_id=1, source_target_pairs={{16,80},{32,96},{48,112},{144,208},{160,224},{176,240},{272,336},{... | collective-permute-start | bytes 491528 | tf_op jit(solution)/shard_map/ppermute | solution.py:230
  28.6 4.1 %collective-permute-start.9 = (bf16[128,640]{1,0:T(8,128)(2,1)S(1)}, bf16[128,640]{1,0:T(8,128)(2,1)S(1)}, u32[]{:S(2)}, u32[]{:S(2)}) collective-permute-start(bf16[128,640]{1,0:T(8,128)(2,1)S(1)} %pick_b.1.held), channel_id=1, source_target_pairs={{0,72},{16,88},{32,104},{48,120},{128,200},{144,216},{160,232},{17... | collective-permute-start | bytes 491528 | tf_op jit(solution)/shard_map/ppermute | solution.py:230
  29.9 2.8 %collective-permute-start.10 = (bf16[128,640]{1,0:T(8,128)(2,1)S(1)}, bf16[128,640]{1,0:T(8,128)(2,1)S(1)}, u32[]{:S(2)}, u32[]{:S(2)}) collective-permute-start(bf16[128,640]{1,0:T(8,128)(2,1)S(1)} %pick_b.1.held), channel_id=1, source_target_pairs={{0,8},{16,24},{32,40},{48,56},{128,136},{144,152},{160,168},{176,1... | collective-permute-start | bytes 491528 | tf_op jit(solution)/shard_map/ppermute | solution.py:230
  38.2 11.0 %all-to-all-start.1 = ((bf16[8,160,128]{2,1,0:T(8,128)(2,1)}), bf16[8,160,128]{2,1,0:T(8,128)(2,1)S(1)}, u32[]{:S(2)}, u32[]{:S(2)}) async-start(bf16[8,160,128]{2,1,0:T(8,128)(2,1)} %first_rows.1), calls=%async_computation.1 | async-start | bytes 655360 | tf_op jit(solution)/shard_map/all_to_all | solution.py:269
  44.9 14.9 %copy-start.5 = (bf16[640,640]{1,0:T(8,128)(2,1)S(1)}, bf16[640,640]{1,0:T(8,128)(2,1)}, u32[]{:S(2)}) copy-start(bf16[640,640]{1,0:T(8,128)(2,1)} %w_out.1) | copy-start | bytes 2457604
  50.3 9.5 %copy-start.3 = (bf16[128,640]{1,0:T(8,128)(2,1)S(1)}, bf16[128,640]{1,0:T(8,128)(2,1)}, u32[]{:S(2)}) copy-start(bf16[128,640]{1,0:T(8,128)(2,1)} %stage.1.own.held.latents) | copy-start | bytes 491524

commit v7 on v5

--- a/solution.py
+++ b/solution.py
@@ -139,7 +139,7 @@
     return lax.dot_general(key, query, (((0,), (0,)), ((), ())), preferred_element_type=jnp.float32)
 
 
-GROUP = 4
+GROUP = 8
 
 
 def near_kernel(rows, peak, total, queries):

time: 60.2 us -> 60.2 us (level)
  no operation moved by 1% of the time
where the time goes in v7:
time: 60.2 us; the launch traced here: 59.7 us
  starting transfers between devices  22.7 us (38%)
  waiting for transfers between devices  17.4 us (29%)
  blocking collectives  9.33 us (15%)
  Pallas kernels  9.12 us (15%)
  local copies, waits for them, and re-layouts  0.93 us (2%)
    ppermute x10, starting transfers between devices, send(): lax.ppermute(array, 'frame', pairs_of(*permute))  11.6 us
    all_to_all x1, blocking collectives, body(): back = lax.all_to_all(attended, 'row', 0, 0, tiled=True)  9.33 us
    pallas_call x9, Pallas kernels, call(): pl.pallas_call(kernel, out_shape=shapes, in_specs=[pl.BlockSpec(memory_sp...  9.12 us
    ppermute x10, waiting for transfers between devices, send(): lax.ppermute(array, 'frame', pairs_of(*permute))  8.89 us
    all_to_all x1, starting transfers between devices, body(): rows = lax.all_to_all(mine, 'row', 0, 0, tiled=True)  5.7 us
    all_to_all x1, waiting for transfers between devices, body(): first = lax.all_to_all(theirs, 'row', 0, 0, tiled=True)  4.54 us
    all_to_all x1, waiting for transfers between devices, body(): rows = lax.all_to_all(mine, 'row', 0, 0, tiled=True)  3.95 us
    all_to_all x1, starting transfers between devices, body(): first = lax.all_to_all(theirs, 'row', 0, 0, tiled=True)  3.43 us
  transfers between devices with their start and end apart: 13, of which 4 were waited for; matrix products, arithmetic and copies ran while one was open for 0% of the time, Pallas kernels for 12%

profile of v7, /device:TPU:48, one launch (start us, length us, event | category | flops | bytes accessed | tf_op | source)
XLA Modules:
  0.0 59.7 jit_solution(16309194893947164385)
XLA Ops:
  0.7 0.7 %collective-permute-start.2 = (bf16[128,640]{1,0:T(8,128)(2,1)}, bf16[128,640]{1,0:T(8,128)(2,1)S(1)}, u32[]{:S(2)}, u32[]{:S(2)}) collective-permute-start(bf16[128,640]{1,0:T(8,128)(2,1)} %bitcast.4), channel_id=1, source_target_pairs={{0,256},{1,257},{2,258},{3,259},{4,260},{5,261},{6,262},{7,263}} | collective-permute-start | bytes 491528 | tf_op jit(solution)/shard_map/ppermute | solution.py:229
  1.3 1.3 %collective-permute-start.3 = (bf16[128,640]{1,0:T(8,128)(2,1)}, bf16[128,640]{1,0:T(8,128)(2,1)S(1)}, u32[]{:S(2)}, u32[]{:S(2)}) collective-permute-start(bf16[128,640]{1,0:T(8,128)(2,1)} %bitcast.5), channel_id=1, source_target_pairs={{0,384},{1,385},{2,386},{3,387},{4,388},{5,389},{6,390},{7,391}} | collective-permute-start | bytes 491528 | tf_op jit(solution)/shard_map/ppermute | solution.py:229
  2.6 1.9 %collective-permute-start = (bf16[128,640]{1,0:T(8,128)(2,1)}, bf16[128,640]{1,0:T(8,128)(2,1)S(1)}, u32[]{:S(2)}, u32[]{:S(2)}) collective-permute-start(bf16[128,640]{1,0:T(8,128)(2,1)} %bitcast.6), channel_id=1, source_target_pairs={{0,8},{8,16},{16,24},{24,32},{32,40},{40,48},{48,56},{56,64},{64,7... | collective-permute-start | bytes 491528 | tf_op jit(solution)/shard_map/ppermute | solution.py:232
  4.6 0.9 %copy-done.5 = bf16[1,128,640]{2,1,0:T(8,128)(2,1)S(1)} copy-done((bf16[1,128,640]{2,1,0:T(8,128)(2,1)S(1)}, bf16[1,128,640]{2,1,0:T(8,128)(2,1)}, u32[]{:S(2)}) %copy-start.5) | copy-done | bytes 163864
  5.7 7.4 %collective-permute-done.3.rest_2_ = bf16[128,640]{1,0:T(8,128)(2,1)S(1)} collective-permute-done((bf16[128,640]{1,0:T(8,128)(2,1)}, bf16[128,640]{1,0:T(8,128)(2,1)S(1)}, u32[]{:S(2)}, u32[]{:S(2)}) %collective-permute-start.3) | collective-permute-done | bytes 163872 | tf_op jit(solution)/shard_map/ppermute | solution.py:229
  13.1 1.4 %collective-permute-start.4 = (bf16[128,640]{1,0:T(8,128)(2,1)S(1)}, bf16[128,640]{1,0:T(8,128)(2,1)S(1)}, u32[]{:S(2)}, u32[]{:S(2)}) collective-permute-start(bf16[128,640]{1,0:T(8,128)(2,1)S(1)} %pick_a.1.after.held), channel_id=1, source_target_pairs={{0,64},{128,192},{256,320},{384,448},{1,65},{129,193},{257,321},{3... | collective-permute-start | bytes 491528 | tf_op jit(solution)/shard_map/ppermute | solution.py:229
  14.6 1.3 %collective-permute-start.5 = (bf16[128,640]{1,0:T(8,128)(2,1)S(1)}, bf16[128,640]{1,0:T(8,128)(2,1)S(1)}, u32[]{:S(2)}, u32[]{:S(2)}) collective-permute-start(bf16[128,640]{1,0:T(8,128)(2,1)S(1)} %pick_a.1.after.held), channel_id=1, source_target_pairs={{0,16},{128,144},{256,272},{384,400},{1,17},{129,145},{257,273},{3... | collective-permute-start | bytes 491528 | tf_op jit(solution)/shard_map/ppermute | solution.py:229
  15.9 1.7 %collective-permute-start.6 = (bf16[128,640]{1,0:T(8,128)(2,1)S(1)}, bf16[128,640]{1,0:T(8,128)(2,1)S(1)}, u32[]{:S(2)}, u32[]{:S(2)}) collective-permute-start(bf16[128,640]{1,0:T(8,128)(2,1)S(1)} %pick_a.1.after.held), channel_id=1, source_target_pairs={{0,32},{128,160},{256,288},{384,416},{1,33},{129,161},{257,289},{3... | collective-permute-start | bytes 491528 | tf_op jit(solution)/shard_map/ppermute | solution.py:229
  17.6 1.3 %collective-permute-start.7 = (bf16[128,640]{1,0:T(8,128)(2,1)S(1)}, bf16[128,640]{1,0:T(8,128)(2,1)S(1)}, u32[]{:S(2)}, u32[]{:S(2)}) collective-permute-start(bf16[128,640]{1,0:T(8,128)(2,1)S(1)} %pick_a.1.after.held), channel_id=1, source_target_pairs={{0,48},{128,176},{256,304},{384,432},{1,49},{129,177},{257,305},{3... | collective-permute-start | bytes 491528 | tf_op jit(solution)/shard_map/ppermute | solution.py:229
  19.0 0.9 %own_rows.1.mine = bf16[8,240,128]{2,1,0:T(8,128)(2,1)S(1)} custom-call(bf16[128,640]{1,0:T(8,128)(2,1)S(1)} %stage.1.own.held.latents, f32[640]{0:T(1024)S(1)} %copy-done.4, bf16[640,640]{1,0:T(8,128)(2,1)S(1)} %copy-done.2, bf16[640,640]{1,0:T(8,128)(2,1)S(1)} %copy-done, bf16[640,640]{1,0:T(8,128)(2,1)S(1)} %copy-done.1), custom_call_target="tpu_custom_call" | custom-call | flops 314572800 | bytes 2457600 | tf_op jit(solution)/shard_map/own_rows/pallas_call | solution.py:205
  19.8 1.4 %prior_rows.1 = bf16[8,400,128]{2,1,0:T(8,128)(2,1)} custom-call(s32[1]{0:T(128)} %bitcast.frame, bf16[8,240,128]{2,1,0:T(8,128)(2,1)S(1)} %own_rows.1.mine, bf16[128,640]{1,0:T(8,128)(2,1)S(1)} %stage.1.own.held.latents, bf16[128,640]{1,0:T(8,128)(2,1)S(1)} %collective-permute-done.prior, f32[640]{0:T(1024)S(1)} %copy-done.4, bf16[640,640]{1,0:T(8,128)(2,1)S(1)} %copy-done, ...), custom_call_target="tpu_custom_call" | custom-call | flops 209715200 | bytes 1638400 | tf_op jit(solution)/shard_map/prior_rows/pallas_call | solution.py:205
  21.2 5.7 %all-to-all-start = ((bf16[8,400,128]{2,1,0:T(8,128)(2,1)}), bf16[8,400,128]{2,1,0:T(8,128)(2,1)S(1)}, u32[]{:S(2)}, u32[]{:S(2)}) async-start(bf16[8,400,128]{2,1,0:T(8,128)(2,1)} %prior_rows.1), calls=%async_computation | async-start | bytes 1638400 | tf_op jit(solution)/shard_map/all_to_all | solution.py:256
  27.0 0.7 %collective-permute-start.8 = (bf16[128,640]{1,0:T(8,128)(2,1)S(1)}, bf16[128,640]{1,0:T(8,128)(2,1)S(1)}, u32[]{:S(2)}, u32[]{:S(2)}) collective-permute-start(bf16[128,640]{1,0:T(8,128)(2,1)S(1)} %pick_b.1.held), channel_id=1, source_target_pairs={{16,80},{32,96},{48,112},{144,208},{160,224},{176,240},{272,336},{... | collective-permute-start | bytes 491528 | tf_op jit(solution)/shard_map/ppermute | solution.py:229
  27.7 1.3 %collective-permute-start.9 = (bf16[128,640]{1,0:T(8,128)(2,1)S(1)}, bf16[128,640]{1,0:T(8,128)(2,1)S(1)}, u32[]{:S(2)}, u32[]{:S(2)}) collective-permute-start(bf16[128,640]{1,0:T(8,128)(2,1)S(1)} %pick_b.1.held), channel_id=1, source_target_pairs={{0,72},{16,88},{32,104},{48,120},{128,200},{144,216},{160,232},{17... | collective-permute-start | bytes 491528 | tf_op jit(solution)/shard_map/ppermute | solution.py:229
  29.0 1.3 %collective-permute-start.10 = (bf16[128,640]{1,0:T(8,128)(2,1)S(1)}, bf16[128,640]{1,0:T(8,128)(2,1)S(1)}, u32[]{:S(2)}, u32[]{:S(2)}) collective-permute-start(bf16[128,640]{1,0:T(8,128)(2,1)S(1)} %pick_b.1.held), channel_id=1, source_target_pairs={{0,8},{16,24},{32,40},{48,56},{128,136},{144,152},{160,168},{176,1... | collective-permute-start | bytes 491528 | tf_op jit(solution)/shard_map/ppermute | solution.py:229
  30.3 1.5 %collective-permute-done.9.rest_1_ = bf16[128,640]{1,0:T(8,128)(2,1)S(1)} collective-permute-done((bf16[128,640]{1,0:T(8,128)(2,1)S(1)}, bf16[128,640]{1,0:T(8,128)(2,1)S(1)}, u32[]{:S(2)}, u32[]{:S(2)}) %collective-permute-start.9) | collective-permute-done | bytes 163872 | tf_op jit(solution)/shard_map/ppermute | solution.py:229
  31.8 1.5 %first_rows.1 = bf16[8,160,128]{2,1,0:T(8,128)(2,1)} custom-call(s32[1]{0:T(128)} %bitcast.frame, bf16[128,640]{1,0:T(8,128)(2,1)S(1)} %pick_b.1.held, bf16[128,640]{1,0:T(8,128)(2,1)S(1)} %collective-permute-done.8.rest_0_, bf16[128,640]{1,0:T(8,128)(2,1)S(1)} %collective-permute-done.9.rest_1_, bf16[128,640]{1,0:T(8,128)(2,1)S(1)} %collective-permute-done.10.rest_2_, ...), custom_call_target="tpu_custom_call" | custom-call | flops 209715200 | bytes 1638400 | tf_op jit(solution)/shard_map/first_rows/pallas_call | solution.py:205
  33.3 4.0 %all-to-all-done.rows = bf16[8,400,128]{2,1,0:T(8,128)(2,1)S(1)} async-done(((bf16[8,400,128]{2,1,0:T(8,128)(2,1)}), bf16[8,400,128]{2,1,0:T(8,128)(2,1)S(1)}, u32[]{:S(2)}, u32[]{:S(2)}) %all-to-all-start) | async-done | bytes 819232 | tf_op jit(solution)/shard_map/all_to_all | solution.py:256
  37.2 3.4 %all-to-all-start.1 = ((bf16[8,160,128]{2,1,0:T(8,128)(2,1)}), bf16[8,160,128]{2,1,0:T(8,128)(2,1)S(1)}, u32[]{:S(2)}, u32[]{:S(2)}) async-start(bf16[8,160,128]{2,1,0:T(8,128)(2,1)} %first_rows.1), calls=%async_computation.1 | async-start | bytes 655360 | tf_op jit(solution)/shard_map/all_to_all | solution.py:268
  40.7 3.0 %near.1 = (f32[8,1024]{1,0:T(8,128)S(1)}, f32[96,1024]{1,0:T(8,128)S(1)}, bf16[80,1024]{1,0:T(8,128)(2,1)S(1)}) custom-call(bf16[8,400,128]{2,1,0:T(8,128)(2,1)S(1)} %all-to-all-done.rows), custom_call_target="tpu_custom_call" | custom-call | flops 671088640 | bytes 819200 | tf_op jit(solution)/shard_map/near/pallas_call | solution.py:205
  43.7 4.5 %all-to-all-done.1.first = bf16[8,160,128]{2,1,0:T(8,128)(2,1)S(1)} async-done(((bf16[8,160,128]{2,1,0:T(8,128)(2,1)}), bf16[8,160,128]{2,1,0:T(8,128)(2,1)S(1)}, u32[]{:S(2)}, u32[]{:S(2)}) %all-to-all-start.1) | async-done | bytes 327712 | tf_op jit(solution)/shard_map/all_to_all | solution.py:268
  48.2 1.1 %far.1 = bf16[8,80,128]{2,1,0:T(8,128)(2,1)S(1)} custom-call(bf16[80,1024]{1,0:T(8,128)(2,1)S(1)} %get-tuple-element.8.queries, bf16[8,160,128]{2,1,0:T(8,128)(2,1)S(1)} %all-to-all-done.1.first, f32[8,1024]{1,0:T(8,128)S(1)} %get-tuple-element.9.peak, f32[96,1024]{1,0:T(8,128)S(1)} %get-tuple-element.10.total), custom_call_target="tpu_custom_call" | custom-call | flops 335544320 | bytes 327680 | tf_op jit(solution)/shard_map/far/pallas_call | solution.py:205
  49.4 9.3 %all_to_all.15.attended = bf16[8,80,128]{2,1,0:T(8,128)(2,1)S(1)} all-to-all(bf16[8,80,128]{2,1,0:T(8,128)(2,1)S(1)} %far.1), channel_id=1, replica_groups=mesh['frame'=64,'row'=8] {'row'}, dimensions={0} | all-to-all | bytes 327680 | tf_op jit(solution)/shard_map/all_to_all | solution.py:274
  58.7 1.0 %mix.1 = bf16[128,640]{1,0:T(8,128)(2,1)} custom-call(bf16[8,80,128]{2,1,0:T(8,128)(2,1)S(1)} %all_to_all.15.attended, bf16[128,640]{1,0:T(8,128)(2,1)S(1)} %stage.1.own.held.latents, bf16[640,640]{1,0:T(8,128)(2,1)S(1)} %copy-done.3), custom_call_target="tpu_custom_call" | custom-call | flops 104857600 | bytes 819200 | tf_op jit(solution)/shard_map/mix/pallas_call | solution.py:205
  (24 shorter events, 1.0 us)
Async XLA Ops:
  0.0 5.7 %collective-permute-start.1 = (bf16[128,640]{1,0:T(8,128)(2,1)}, bf16[128,640]{1,0:T(8,128)(2,1)S(1)}, u32[]{:S(2)}, u32[]{:S(2)}) collective-permute-start(bf16[128,640]{1,0:T(8,128)(2,1)} %bitcast.3), channel_id=1, source_target_pairs={{0,128},{1,129},{2,130},{3,131},{4,132},{5,133},{6,134},{7,135}} | collective-permute-start | bytes 491528 | tf_op jit(solution)/shard_map/ppermute | solution.py:229
  0.7 5.0 %collective-permute-start.2 = (bf16[128,640]{1,0:T(8,128)(2,1)}, bf16[128,640]{1,0:T(8,128)(2,1)S(1)}, u32[]{:S(2)}, u32[]{:S(2)}) collective-permute-start(bf16[128,640]{1,0:T(8,128)(2,1)} %bitcast.4), channel_id=1, source_target_pairs={{0,256},{1,257},{2,258},{3,259},{4,260},{5,261},{6,262},{7,263}} | collective-permute-start | bytes 491528 | tf_op jit(solution)/shard_map/ppermute | solution.py:229
  1.3 11.7 %collective-permute-start.3 = (bf16[128,640]{1,0:T(8,128)(2,1)}, bf16[128,640]{1,0:T(8,128)(2,1)S(1)}, u32[]{:S(2)}, u32[]{:S(2)}) collective-permute-start(bf16[128,640]{1,0:T(8,128)(2,1)} %bitcast.5), channel_id=1, source_target_pairs={{0,384},{1,385},{2,386},{3,387},{4,388},{5,389},{6,390},{7,391}} | collective-permute-start | bytes 491528 | tf_op jit(solution)/shard_map/ppermute | solution.py:229
  2.6 17.2 %collective-permute-start = (bf16[128,640]{1,0:T(8,128)(2,1)}, bf16[128,640]{1,0:T(8,128)(2,1)S(1)}, u32[]{:S(2)}, u32[]{:S(2)}) collective-permute-start(bf16[128,640]{1,0:T(8,128)(2,1)} %bitcast.6), channel_id=1, source_target_pairs={{0,8},{8,16},{16,24},{24,32},{32,40},{40,48},{48,56},{56,64},{64,7... | collective-permute-start | bytes 491528 | tf_op jit(solution)/shard_map/ppermute | solution.py:232
  4.6 0.9 %copy-start.5 = (bf16[1,128,640]{2,1,0:T(8,128)(2,1)S(1)}, bf16[1,128,640]{2,1,0:T(8,128)(2,1)}, u32[]{:S(2)}) copy-start(bf16[1,128,640]{2,1,0:T(8,128)(2,1)} %param.6) | copy-start | bytes 491524
  13.1 5.8 %copy-start = (bf16[640,640]{1,0:T(8,128)(2,1)S(1)}, bf16[640,640]{1,0:T(8,128)(2,1)}, u32[]{:S(2)}) copy-start(bf16[640,640]{1,0:T(8,128)(2,1)} %rest_4_.1) | copy-start | bytes 2457604
  13.1 5.9 %copy-start.1 = (bf16[640,640]{1,0:T(8,128)(2,1)S(1)}, bf16[640,640]{1,0:T(8,128)(2,1)}, u32[]{:S(2)}) copy-start(bf16[640,640]{1,0:T(8,128)(2,1)} %rest_5_.1) | copy-start | bytes 2457604
  13.1 5.9 %copy-start.2 = (bf16[640,640]{1,0:T(8,128)(2,1)S(1)}, bf16[640,640]{1,0:T(8,128)(2,1)}, u32[]{:S(2)}) copy-start(bf16[640,640]{1,0:T(8,128)(2,1)} %w_query.1) | copy-start | bytes 2457604
  13.1 5.9 %copy-start.4 = (f32[640]{0:T(1024)S(1)}, f32[640]{0:T(1024)}, u32[]{:S(2)}) copy-start(f32[640]{0:T(1024)} %rest_3_.1) | copy-start | bytes 7684
  13.1 13.8 %collective-permute-start.4 = (bf16[128,640]{1,0:T(8,128)(2,1)S(1)}, bf16[128,640]{1,0:T(8,128)(2,1)S(1)}, u32[]{:S(2)}, u32[]{:S(2)}) collective-permute-start(bf16[128,640]{1,0:T(8,128)(2,1)S(1)} %pick_a.1.after.held), channel_id=1, source_target_pairs={{0,64},{128,192},{256,320},{384,448},{1,65},{129,193},{257,321},{3... | collective-permute-start | bytes 491528 | tf_op jit(solution)/shard_map/ppermute | solution.py:229
  14.6 12.3 %collective-permute-start.5 = (bf16[128,640]{1,0:T(8,128)(2,1)S(1)}, bf16[128,640]{1,0:T(8,128)(2,1)S(1)}, u32[]{:S(2)}, u32[]{:S(2)}) collective-permute-start(bf16[128,640]{1,0:T(8,128)(2,1)S(1)} %pick_a.1.after.held), channel_id=1, source_target_pairs={{0,16},{128,144},{256,272},{384,400},{1,17},{129,145},{257,273},{3... | collective-permute-start | bytes 491528 | tf_op jit(solution)/shard_map/ppermute | solution.py:229
  15.9 11.0 %collective-permute-start.6 = (bf16[128,640]{1,0:T(8,128)(2,1)S(1)}, bf16[128,640]{1,0:T(8,128)(2,1)S(1)}, u32[]{:S(2)}, u32[]{:S(2)}) collective-permute-start(bf16[128,640]{1,0:T(8,128)(2,1)S(1)} %pick_a.1.after.held), channel_id=1, source_target_pairs={{0,32},{128,160},{256,288},{384,416},{1,33},{129,161},{257,289},{3... | collective-permute-start | bytes 491528 | tf_op jit(solution)/shard_map/ppermute | solution.py:229
  17.6 9.3 %collective-permute-start.7 = (bf16[128,640]{1,0:T(8,128)(2,1)S(1)}, bf16[128,640]{1,0:T(8,128)(2,1)S(1)}, u32[]{:S(2)}, u32[]{:S(2)}) collective-permute-start(bf16[128,640]{1,0:T(8,128)(2,1)S(1)} %pick_a.1.after.held), channel_id=1, source_target_pairs={{0,48},{128,176},{256,304},{384,432},{1,49},{129,177},{257,305},{3... | collective-permute-start | bytes 491528 | tf_op jit(solution)/shard_map/ppermute | solution.py:229
  21.2 16.0 %all-to-all-start = ((bf16[8,400,128]{2,1,0:T(8,128)(2,1)}), bf16[8,400,128]{2,1,0:T(8,128)(2,1)S(1)}, u32[]{:S(2)}, u32[]{:S(2)}) async-start(bf16[8,400,128]{2,1,0:T(8,128)(2,1)} %prior_rows.1), calls=%async_computation | async-start | bytes 1638400 | tf_op jit(solution)/shard_map/all_to_all | solution.py:256
  27.0 3.3 %collective-permute-start.8 = (bf16[128,640]{1,0:T(8,128)(2,1)S(1)}, bf16[128,640]{1,0:T(8,128)(2,1)S(1)}, u32[]{:S(2)}, u32[]{:S(2)}) collective-permute-start(bf16[128,640]{1,0:T(8,128)(2,1)S(1)} %pick_b.1.held), channel_id=1, source_target_pairs={{16,80},{32,96},{48,112},{144,208},{160,224},{176,240},{272,336},{... | collective-permute-start | bytes 491528 | tf_op jit(solution)/shard_map/ppermute | solution.py:229
  27.7 4.1 %collective-permute-start.9 = (bf16[128,640]{1,0:T(8,128)(2,1)S(1)}, bf16[128,640]{1,0:T(8,128)(2,1)S(1)}, u32[]{:S(2)}, u32[]{:S(2)}) collective-permute-start(bf16[128,640]{1,0:T(8,128)(2,1)S(1)} %pick_b.1.held), channel_id=1, source_target_pairs={{0,72},{16,88},{32,104},{48,120},{128,200},{144,216},{160,232},{17... | collective-permute-start | bytes 491528 | tf_op jit(solution)/shard_map/ppermute | solution.py:229
  29.0 2.8 %collective-permute-start.10 = (bf16[128,640]{1,0:T(8,128)(2,1)S(1)}, bf16[128,640]{1,0:T(8,128)(2,1)S(1)}, u32[]{:S(2)}, u32[]{:S(2)}) collective-permute-start(bf16[128,640]{1,0:T(8,128)(2,1)S(1)} %pick_b.1.held), channel_id=1, source_target_pairs={{0,8},{16,24},{32,40},{48,56},{128,136},{144,152},{160,168},{176,1... | collective-permute-start | bytes 491528 | tf_op jit(solution)/shard_map/ppermute | solution.py:229
  37.2 11.0 %all-to-all-start.1 = ((bf16[8,160,128]{2,1,0:T(8,128)(2,1)}), bf16[8,160,128]{2,1,0:T(8,128)(2,1)S(1)}, u32[]{:S(2)}, u32[]{:S(2)}) async-start(bf16[8,160,128]{2,1,0:T(8,128)(2,1)} %first_rows.1), calls=%async_computation.1 | async-start | bytes 655360 | tf_op jit(solution)/shard_map/all_to_all | solution.py:268
  43.7 15.0 %copy-start.3 = (bf16[640,640]{1,0:T(8,128)(2,1)S(1)}, bf16[640,640]{1,0:T(8,128)(2,1)}, u32[]{:S(2)}) copy-start(bf16[640,640]{1,0:T(8,128)(2,1)} %w_out.1) | copy-start | bytes 2457604
